TPU v7x, 32 devices: a whole 2x2x4 slice. The times are simulated.
32 devices in a mesh: lon: 16 (over z, y, core), lat: 2 (over x).
Axes of the slice: x: 2, y: 2, z: 4, core: 2. Of those that a mesh axis runs over, the one named last changes fastest.
Arguments:
- state: float32 [4, 32, 64, 2048], P(None, None, 'lat', 'lon'), may hold values from -6 to 6
- land_mask: int32 [64, 2048], P('lat', 'lon'), may hold values 0 or 1
- wet_levels: int32 [64, 2048], P('lat', 'lon'), may hold values from 1 to 32
Outputs:
- new_state: float32 [4, 32, 64, 2048], P(None, None, 'lat', 'lon')
All inputs are finite; a program needn't handle non-finite values. No bound on the sum of `land_mask` on one device may be relied on, other than what follows from the above.
Results may differ from a plain program's by a relative error of at most 0.00002.
Values sent between devices are 32-bit elements; how exact they have to be, the bound alone decides.
No kernel may reach another device: no remote copies, remote signals or barrier semaphores. Data moves between devices by JAX's collectives and lax.ppermute only.
A program may use at most 128 MiB of HBM per device.

v0:
```python
import jax
import jax.numpy as jnp
from jax import lax
from jax.sharding import PartitionSpec as P

STEPS = 2


time_step = 0.1
lateral_mix = 0.5
column_mix = 0.5
gravity = 0.5
thermal = 0.2
haline = 0.8


def partner(array, axis, distance):
    return lax.ppermute(array, axis, [(i, i ^ 1 << distance) for i in range(lax.axis_size(axis))])


def padded(cells, sides, width, closed):
    for axis, dim in sides:
        count = lax.axis_size(axis)
        ends = count if closed else count - 1
        head = lax.slice_in_dim(cells, 0, width, axis=dim)
        tail = lax.slice_in_dim(cells, cells.shape[dim] - width, cells.shape[dim], axis=dim)
        cells = jnp.concatenate(
            [
                lax.ppermute(tail, axis, [(i, (i + 1) % count) for i in range(ends)]),
                cells,
                lax.ppermute(head, axis, [((i + 1) % count, i) for i in range(ends)]),
            ],
            axis=dim,
        )
    return cells


def wetness(land_mask, wet_levels, levels):
    level_ids = jnp.arange(levels, dtype=jnp.int32)[:, None, None]
    return ((land_mask[None] == 1) & (level_ids < wet_levels[None])).astype(jnp.float32)


def pressure(extended):
    density = haline * extended[1] - thermal * extended[0]
    return gravity * (jnp.cumsum(density, axis=0) - 0.5 * density)


def explicit(state, east_west, north_south, press_ew, press_ns, coriolis, wet):
    grad_x = (
        8.0 * (east_west[..., 3:-1] - east_west[..., 1:-3])
        - (east_west[..., 4:] - east_west[..., :-4])
    ) / 12.0
    grad_y = (
        8.0 * (north_south[..., 3:-1, :] - north_south[..., 1:-3, :])
        - (north_south[..., 4:, :] - north_south[..., :-4, :])
    ) / 12.0
    spread = (
        east_west[..., 3:-1]
        + east_west[..., 1:-3]
        + (north_south[..., 3:-1, :] + north_south[..., 1:-3, :])
        - 4.0 * state
    )
    east_vel = state[2]
    north_vel = state[3]
    carried = east_vel * grad_x + north_vel * grad_y
    press_x = 0.5 * (press_ew[..., 3:-1] - press_ew[..., 1:-3])
    press_y = 0.5 * (press_ns[..., 3:-1, :] - press_ns[..., 1:-3, :])
    zero = jnp.zeros_like(press_x)
    force = jnp.stack([zero, zero, coriolis * north_vel - press_x, -coriolis * east_vel - press_y])
    return (state + time_step * (lateral_mix * spread - carried + force)) * wet


def mirror_rows(top_rows):
    received = top_rows
    for flip_bit in range(lax.axis_size("lon").bit_length() - 1):
        received = partner(received, "lon", flip_bit)
    return received[:, :, ::-1, ::-1]


def per_device(state, land_mask, wet_levels):
    levels = state.shape[1]
    rows = state.shape[2]
    cols = state.shape[3]
    wet = wetness(land_mask, wet_levels, levels)
    band = lax.axis_index("lat")
    bands = lax.axis_size("lat")
    total_rows = rows * bands
    global_rows = band * rows + jnp.arange(rows, dtype=jnp.int32)
    coriolis = (0.2 + 0.8 * ((global_rows.astype(jnp.float32) + 0.5) / total_rows))[:, None]
    sign = jnp.array([1.0, 1.0, -1.0, -1.0], jnp.float32)[:, None, None, None]
    upper = jnp.concatenate([column_mix * wet[1:], jnp.zeros_like(wet[:1])], axis=0)
    lower = jnp.concatenate([jnp.zeros_like(wet[:1]), column_mix * wet[1:]], axis=0)
    centre = 1.0 + lower + upper
    is_top = band == bands - 1
    current = state * wet
    for step in range(STEPS):
        east_west = padded(current, (("lon", 3),), 2, True)
        north_south = padded(current, (("lat", 2),), 2, False)
        ghost = sign * mirror_rows(current[:, :, rows - 2 :, :])
        north_south = jnp.concatenate(
            [
                north_south[:, :, : rows + 2],
                jnp.where(is_top, ghost, north_south[:, :, rows + 2 :]),
            ],
            axis=2,
        )
        press_ew = pressure(east_west)
        press_ns = pressure(north_south)
        provisional = explicit(current, east_west, north_south, press_ew, press_ns, coriolis, wet)
        ratio_prev = jnp.zeros((rows, cols), jnp.float32)
        part_prev = jnp.zeros((4, rows, cols), jnp.float32)
        ratios = []
        parts = []
        for level in range(levels):
            denom = centre[level] + lower[level] * ratio_prev
            ratio_prev = -upper[level] / denom
            part_prev = (provisional[:, level] + lower[level] * part_prev) / denom
            ratios.append(ratio_prev)
            parts.append(part_prev)
        below = jnp.zeros((4, rows, cols), jnp.float32)
        values = [None] * levels
        for level in range(levels - 1, -1, -1):
            below = parts[level] - ratios[level] * below
            values[level] = below
        current = jnp.stack(values, axis=1)
    return current


def solution(mesh):
    placed = (P(None, None, "lat", "lon"), P("lat", "lon"), P("lat", "lon"))
    return jax.shard_map(
        per_device,
        mesh=mesh,
        in_specs=placed,
        out_specs=P(None, None, "lat", "lon"),
        check_vma=False,
    )
```

profile of v0, /device:TPU:0, one launch (start us, length us, event | category | flops | bytes accessed | tf_op | source)
XLA Modules:
  0.0 119.4 jit_solution(5061792731268645980)
XLA Ops:
  1.5 2.0 %broadcast_multiply_fusion = f32[4,32,32,128]{3,2,1,0:T(8,128)S(1)} fusion(f32[4,32,32,128]{3,2,1,0:T(8,128)} %param.4, f32[32,32,128]{2,1,0:T(8,128)S(1)} %fusion.61), kind=kLoop, calls=%fused_computation.70 | loop fusion | flops 524288 | bytes 4718592 | tf_op jit(solution)/shard_map/mul | solution.py:95
  4.8 4.4 %collective-permute-start.7 = (f32[4,32,2,128]{3,2,1,0:T(2,128)}, f32[4,32,2,128]{3,2,1,0:T(2,128)S(1)}, u32[]{:S(2)}, u32[]{:S(2)}) collective-permute-start(f32[4,32,2,128]{3,2,1,0:T(2,128)} %get-tuple-element.127), channel_id=1, source_target_pairs={{0,1},{2,3},{4,5},{6,7},{8,9},{10,11},{12,13},{14,15},{16,17},{18,... | collective-permute-start | bytes 393224 | tf_op jit(solution)/shard_map/ppermute | solution.py:29
  10.5 2.8 %fusion.213 = (f32[4,32,32,2]{3,2,1,0:T(8,128)}, f32[4,32,32,2]{3,2,1,0:T(8,128)}) fusion(f32[4,32,32,128]{3,2,1,0:T(8,128)S(1)} %broadcast_multiply_fusion), kind=kLoop, calls=%fused_computation.518 | loop fusion | bytes 131072 | tf_op jit(solution)/shard_map/slice | solution.py:25
  13.2 3.1 %copy.5 = f32[4,32,32,2]{2,1,3,0:T(8,128)} copy(f32[4,32,32,2]{3,2,1,0:T(8,128)} %get-tuple-element.124) | data formatting | bytes 65536 | tf_op jit(solution)/shard_map/slice | solution.py:25
  16.4 4.4 %collective-permute-start = (f32[4,32,32,2]{2,1,3,0:T(8,128)}, f32[4,32,32,2]{2,1,3,0:T(8,128)}, u32[]{:S(2)}, u32[]{:S(2)}) collective-permute-start(f32[4,32,32,2]{2,1,3,0:T(8,128)} %copy.5), channel_id=1, source_target_pairs={{2,0},{4,2},{6,4},{8,6},{10,8},{12,10},{14,12},{16,14},{18,16},{20... | collective-permute-start | bytes 98312 | tf_op jit(solution)/shard_map/ppermute | solution.py:31
  20.8 3.1 %copy.7 = f32[4,32,32,2]{2,1,3,0:T(8,128)} copy(f32[4,32,32,2]{3,2,1,0:T(8,128)} %get-tuple-element.125) | data formatting | bytes 65536 | tf_op jit(solution)/shard_map/slice | solution.py:26
  29.4 4.5 %collective-permute-done.3 = f32[4,32,2,128]{3,2,1,0:T(2,128)} collective-permute-done((f32[4,32,2,128]{3,2,1,0:T(2,128)S(1)}, f32[4,32,2,128]{3,2,1,0:T(2,128)}, u32[]{:S(2)}, u32[]{:S(2)}) %collective-permute-start.3) | collective-permute-done | bytes 131104 | tf_op jit(solution)/shard_map/ppermute | solution.py:18
  35.7 3.0 %copy.6 = f32[4,32,32,2]{3,2,1,0:T(8,128)} copy(f32[4,32,32,2]{2,1,3,0:T(8,128)} %collective-permute-done) | data formatting | bytes 65536 | tf_op jit(solution)/shard_map/ppermute | solution.py:31
  38.7 3.0 %copy.8 = f32[4,32,32,2]{3,2,1,0:T(8,128)} copy(f32[4,32,32,2]{2,1,3,0:T(8,128)} %collective-permute-done.1) | data formatting | bytes 65536 | tf_op jit(solution)/shard_map/ppermute | solution.py:29
  42.7 4.8 %subtract_multiply_fusion.1 = f32[32,32,132]{2,1,0:T(8,128)} fusion(f32[4,32,32,2]{3,2,1,0:T(8,128)} %copy.6, f32[4,32,32,128]{3,2,1,0:T(8,128)S(1)} %broadcast_multiply_fusion, f32[4,32,32,2]{3,2,1,0:T(8,128)} %copy.8), kind=kOutput, calls=%fused_computation.69 | output fusion | flops 6488064 | bytes 2703360 | tf_op jit(solution)/shard_map/jit(cumsum)/reduce_window_sum | solution.py:45
  47.5 3.6 %collective-permute-done.5 = f32[4,32,2,128]{3,2,1,0:T(2,128)} collective-permute-done((f32[4,32,2,128]{3,2,1,0:T(2,128)}, f32[4,32,2,128]{3,2,1,0:T(2,128)}, u32[]{:S(2)}, u32[]{:S(2)}) %collective-permute-start.5) | collective-permute-done | bytes 131104 | tf_op jit(solution)/shard_map/ppermute | solution.py:18
  57.4 4.9 %fusion.28 = f32[4,32,32,128]{3,2,1,0:T(8,128)S(1)} fusion(f32[4,32,32,128]{3,2,1,0:T(8,128)S(1)} %broadcast_multiply_fusion, f32[4,32,2,128]{3,2,1,0:T(2,128)S(1)} %collective-permute-done.7, f32[4,32,2,128]{3,2,1,0:T(2,128)S(1)} %multiply_select_fusion.1, f32[4,32,32,2]{3,2,1,0:T(8,128)S(1)} %copy-done.3, f32[4,32,32,2]{3,2,1,0:T(8,128)S(1)} %copy-done.1, ...), kind=kLoop, calls=%fused_computation.49 | loop fusion | flops 16777216 | bytes 7143440 | tf_op jit(solution)/shard_map/mul | solution.py:70
  68.0 4.6 %collective-permute-done.11 = f32[4,32,2,128]{3,2,1,0:T(2,128)} collective-permute-done((f32[4,32,2,128]{3,2,1,0:T(2,128)S(1)}, f32[4,32,2,128]{3,2,1,0:T(2,128)}, u32[]{:S(2)}, u32[]{:S(2)}) %collective-permute-start.11) | collective-permute-done | bytes 131104 | tf_op jit(solution)/shard_map/ppermute | solution.py:18
  72.6 2.8 %fusion.211 = (f32[4,32,32,2]{3,2,1,0:T(8,128)}, f32[4,32,32,2]{3,2,1,0:T(8,128)}) fusion(f32[4,32,32,128]{3,2,1,0:T(8,128)S(1)} %constant_dynamic-update-slice_fusion), kind=kLoop, calls=%fused_computation.516 | loop fusion | bytes 131072 | tf_op jit(solution)/shard_map/slice | solution.py:25
  75.4 2.5 %copy.11 = f32[4,32,32,2]{2,1,3,0:T(8,128)S(1)} copy(f32[4,32,32,2]{3,2,1,0:T(8,128)} %get-tuple-element.116) | data formatting | bytes 65536 | tf_op jit(solution)/shard_map/slice | solution.py:25
  77.9 1.7 %collective-permute-start.8 = (f32[4,32,32,2]{2,1,3,0:T(8,128)S(1)}, f32[4,32,32,2]{2,1,3,0:T(8,128)}, u32[]{:S(2)}, u32[]{:S(2)}) collective-permute-start(f32[4,32,32,2]{2,1,3,0:T(8,128)S(1)} %copy.11), channel_id=1, source_target_pairs={{2,0},{4,2},{6,4},{8,6},{10,8},{12,10},{14,12},{16,14},{18,16},{20... | collective-permute-start | bytes 98312 | tf_op jit(solution)/shard_map/ppermute | solution.py:31
  79.5 3.1 %copy.13 = f32[4,32,32,2]{2,1,3,0:T(8,128)} copy(f32[4,32,32,2]{3,2,1,0:T(8,128)} %get-tuple-element.117) | data formatting | bytes 65536 | tf_op jit(solution)/shard_map/slice | solution.py:26
  82.7 4.7 %collective-permute-start.15 = (f32[4,32,2,128]{3,2,1,0:T(2,128)}, f32[4,32,2,128]{3,2,1,0:T(2,128)S(1)}, u32[]{:S(2)}, u32[]{:S(2)}) collective-permute-start(f32[4,32,2,128]{3,2,1,0:T(2,128)} %copy-done.89), channel_id=1, source_target_pairs={{0,1},{2,3},{4,5},{6,7},{8,9},{10,11},{12,13},{14,15},{16,17},{18,... | collective-permute-start | bytes 393224 | tf_op jit(solution)/shard_map/ppermute | solution.py:29
  88.7 3.0 %copy.12 = f32[4,32,32,2]{3,2,1,0:T(8,128)} copy(f32[4,32,32,2]{2,1,3,0:T(8,128)} %collective-permute-done.8) | data formatting | bytes 65536 | tf_op jit(solution)/shard_map/ppermute | solution.py:31
  91.7 3.0 %copy.14 = f32[4,32,32,2]{3,2,1,0:T(8,128)} copy(f32[4,32,32,2]{2,1,3,0:T(8,128)} %collective-permute-done.9) | data formatting | bytes 65536 | tf_op jit(solution)/shard_map/ppermute | solution.py:29
  94.8 2.1 %collective-permute-start.13 = (f32[4,32,2,128]{3,2,1,0:T(2,128)}, f32[4,32,2,128]{3,2,1,0:T(2,128)}, u32[]{:S(2)}, u32[]{:S(2)}) collective-permute-start(f32[4,32,2,128]{3,2,1,0:T(2,128)} %collective-permute-done.12), channel_id=1, source_target_pairs={{0,16},{2,18},{4,20},{6,22},{8,24},{10,26},{12,28},{14,30},{16,0},... | collective-permute-start | bytes 393224 | tf_op jit(solution)/shard_map/ppermute | solution.py:18
  96.9 4.8 %subtract_multiply_fusion = f32[32,32,132]{2,1,0:T(8,128)} fusion(f32[4,32,32,2]{3,2,1,0:T(8,128)} %copy.12, f32[4,32,32,128]{3,2,1,0:T(8,128)S(1)} %constant_dynamic-update-slice_fusion, f32[4,32,32,2]{3,2,1,0:T(8,128)} %copy.14), kind=kOutput, calls=%fused_computation.68 | output fusion | flops 6488064 | bytes 2703360 | tf_op jit(solution)/shard_map/jit(cumsum)/reduce_window_sum | solution.py:45
  101.7 2.0 %collective-permute-done.13 = f32[4,32,2,128]{3,2,1,0:T(2,128)} collective-permute-done((f32[4,32,2,128]{3,2,1,0:T(2,128)}, f32[4,32,2,128]{3,2,1,0:T(2,128)}, u32[]{:S(2)}, u32[]{:S(2)}) %collective-permute-start.13) | collective-permute-done | bytes 131104 | tf_op jit(solution)/shard_map/ppermute | solution.py:18
  110.0 4.9 %fusion.16 = f32[4,32,32,128]{3,2,1,0:T(8,128)S(1)} fusion(f32[4,32,32,128]{3,2,1,0:T(8,128)S(1)} %constant_dynamic-update-slice_fusion, f32[4,32,2,128]{3,2,1,0:T(2,128)S(1)} %collective-permute-done.15, f32[4,32,2,128]{3,2,1,0:T(2,128)S(1)} %multiply_select_fusion, f32[4,32,32,2]{3,2,1,0:T(8,128)S(1)} %copy-done.2, f32[4,32,32,2]{3,2,1,0:T(8,128)S(1)} %copy-done, ...), kind=kLoop, calls=%fused_computation.33 | loop fusion | flops 16777216 | bytes 7143440 | tf_op jit(solution)/shard_map/mul | solution.py:70
  (312 shorter events, 34.4 us)
Async XLA Ops:
  4.3 24.3 %collective-permute-start.2 = (f32[4,32,2,128]{3,2,1,0:T(2,128)}, f32[4,32,2,128]{3,2,1,0:T(2,128)S(1)}, u32[]{:S(2)}, u32[]{:S(2)}) collective-permute-start(f32[4,32,2,128]{3,2,1,0:T(2,128)} %get-tuple-element.127), channel_id=1, source_target_pairs={{0,2},{2,0},{4,6},{6,4},{8,10},{10,8},{12,14},{14,12},{16,18},{18,... | collective-permute-start | bytes 393224 | tf_op jit(solution)/shard_map/ppermute | solution.py:18
  4.8 48.8 %collective-permute-start.7 = (f32[4,32,2,128]{3,2,1,0:T(2,128)}, f32[4,32,2,128]{3,2,1,0:T(2,128)S(1)}, u32[]{:S(2)}, u32[]{:S(2)}) collective-permute-start(f32[4,32,2,128]{3,2,1,0:T(2,128)} %get-tuple-element.127), channel_id=1, source_target_pairs={{0,1},{2,3},{4,5},{6,7},{8,9},{10,11},{12,13},{14,15},{16,17},{18,... | collective-permute-start | bytes 393224 | tf_op jit(solution)/shard_map/ppermute | solution.py:29
  9.2 43.3 %collective-permute-start.6 = (f32[4,32,2,128]{3,2,1,0:T(2,128)}, f32[4,32,2,128]{3,2,1,0:T(2,128)}, u32[]{:S(2)}, u32[]{:S(2)}) collective-permute-start(f32[4,32,2,128]{3,2,1,0:T(2,128)} %get-tuple-element.126), channel_id=1, source_target_pairs={{1,0},{3,2},{5,4},{7,6},{9,8},{11,10},{13,12},{15,14},{17,16},{19,... | collective-permute-start | bytes 393224 | tf_op jit(solution)/shard_map/ppermute | solution.py:31
  16.4 19.3 %collective-permute-start = (f32[4,32,32,2]{2,1,3,0:T(8,128)}, f32[4,32,32,2]{2,1,3,0:T(8,128)}, u32[]{:S(2)}, u32[]{:S(2)}) collective-permute-start(f32[4,32,32,2]{2,1,3,0:T(8,128)} %copy.5), channel_id=1, source_target_pairs={{2,0},{4,2},{6,4},{8,6},{10,8},{12,10},{14,12},{16,14},{18,16},{20... | collective-permute-start | bytes 98312 | tf_op jit(solution)/shard_map/ppermute | solution.py:31
  23.9 14.8 %collective-permute-start.1 = (f32[4,32,32,2]{2,1,3,0:T(8,128)}, f32[4,32,32,2]{2,1,3,0:T(8,128)}, u32[]{:S(2)}, u32[]{:S(2)}) collective-permute-start(f32[4,32,32,2]{2,1,3,0:T(8,128)} %copy.7), channel_id=1, source_target_pairs={{0,2},{2,4},{4,6},{6,8},{8,10},{10,12},{12,14},{14,16},{16,18},{18... | collective-permute-start | bytes 98312 | tf_op jit(solution)/shard_map/ppermute | solution.py:29
  27.4 6.5 %copy-start.21 = (f32[1,32,128]{2,1,0:T(8,128)}, f32[1,32,128]{2,1,0:T(8,128)S(1)}, u32[]{:S(2)}) copy-start(f32[1,32,128]{2,1,0:T(8,128)S(1)} %get-tuple-element.107) | copy-start | bytes 49156
  28.6 13.1 %copy-start.24 = (f32[1,32,128]{2,1,0:T(8,128)}, f32[1,32,128]{2,1,0:T(8,128)S(1)}, u32[]{:S(2)}) copy-start(f32[1,32,128]{2,1,0:T(8,128)S(1)} %get-tuple-element.110) | copy-start | bytes 49156
  28.6 5.2 %collective-permute-start.3 = (f32[4,32,2,128]{3,2,1,0:T(2,128)S(1)}, f32[4,32,2,128]{3,2,1,0:T(2,128)}, u32[]{:S(2)}, u32[]{:S(2)}) collective-permute-start(f32[4,32,2,128]{3,2,1,0:T(2,128)S(1)} %collective-permute-done.2), channel_id=1, source_target_pairs={{0,4},{2,6},{4,0},{6,2},{8,12},{10,14},{12,8},{14,10},{16,20},{18,... | collective-permute-start | bytes 393224 | tf_op jit(solution)/shard_map/ppermute | solution.py:18
  33.9 7.9 %collective-permute-start.4 = (f32[4,32,2,128]{3,2,1,0:T(2,128)}, f32[4,32,2,128]{3,2,1,0:T(2,128)}, u32[]{:S(2)}, u32[]{:S(2)}) collective-permute-start(f32[4,32,2,128]{3,2,1,0:T(2,128)} %collective-permute-done.3), channel_id=1, source_target_pairs={{0,8},{2,10},{4,12},{6,14},{8,0},{10,2},{12,4},{14,6},{16,24},{18,... | collective-permute-start | bytes 393224 | tf_op jit(solution)/shard_map/ppermute | solution.py:18
  41.8 9.3 %collective-permute-start.5 = (f32[4,32,2,128]{3,2,1,0:T(2,128)}, f32[4,32,2,128]{3,2,1,0:T(2,128)}, u32[]{:S(2)}, u32[]{:S(2)}) collective-permute-start(f32[4,32,2,128]{3,2,1,0:T(2,128)} %collective-permute-done.4), channel_id=1, source_target_pairs={{0,16},{2,18},{4,20},{6,22},{8,24},{10,26},{12,28},{14,30},{16,0},... | collective-permute-start | bytes 393224 | tf_op jit(solution)/shard_map/ppermute | solution.py:18
  57.0 5.3 %copy-start.19 = (f32[1,32,128]{2,1,0:T(8,128)S(1)}, f32[1,32,128]{2,1,0:T(8,128)}, u32[]{:S(2)}) copy-start(f32[1,32,128]{2,1,0:T(8,128)} %copy-done.18) | copy-start | bytes 49156
  57.0 5.3 %copy-start.22 = (f32[1,32,128]{2,1,0:T(8,128)S(1)}, f32[1,32,128]{2,1,0:T(8,128)}, u32[]{:S(2)}) copy-start(f32[1,32,128]{2,1,0:T(8,128)} %copy-done.21) | copy-start | bytes 49156
  57.1 5.3 %copy-start.25 = (f32[1,32,128]{2,1,0:T(8,128)S(1)}, f32[1,32,128]{2,1,0:T(8,128)}, u32[]{:S(2)}) copy-start(f32[1,32,128]{2,1,0:T(8,128)} %copy-done.24) | copy-start | bytes 49156
  57.1 5.3 %copy-start.27 = (f32[32,128]{1,0:T(8,128)S(1)}, f32[32,128]{1,0:T(8,128)}, u32[]{:S(2)}) copy-start(f32[32,128]{1,0:T(8,128)} %get-tuple-element.167) | copy-start | bytes 49156
  57.1 5.3 %copy-start.29 = (f32[32,128]{1,0:T(8,128)S(1)}, f32[32,128]{1,0:T(8,128)}, u32[]{:S(2)}) copy-start(f32[32,128]{1,0:T(8,128)} %get-tuple-element.168) | copy-start | bytes 49156
  65.6 9.8 %copy-start.89 = (f32[4,32,2,128]{3,2,1,0:T(2,128)}, f32[4,32,2,128]{3,2,1,0:T(2,128)S(1)}, u32[]{:S(2)}) copy-start(f32[4,32,2,128]{3,2,1,0:T(2,128)S(1)} %get-tuple-element.119) | copy-start | bytes 393220
  65.6 1.3 %collective-permute-start.10 = (f32[4,32,2,128]{3,2,1,0:T(2,128)S(1)}, f32[4,32,2,128]{3,2,1,0:T(2,128)S(1)}, u32[]{:S(2)}, u32[]{:S(2)}) collective-permute-start(f32[4,32,2,128]{3,2,1,0:T(2,128)S(1)} %get-tuple-element.119), channel_id=1, source_target_pairs={{0,2},{2,0},{4,6},{6,4},{8,10},{10,8},{12,14},{14,12},{16,18},{18,... | collective-permute-start | bytes 393224 | tf_op jit(solution)/shard_map/ppermute | solution.py:18
  67.0 5.7 %collective-permute-start.11 = (f32[4,32,2,128]{3,2,1,0:T(2,128)S(1)}, f32[4,32,2,128]{3,2,1,0:T(2,128)}, u32[]{:S(2)}, u32[]{:S(2)}) collective-permute-start(f32[4,32,2,128]{3,2,1,0:T(2,128)S(1)} %collective-permute-done.10), channel_id=1, source_target_pairs={{0,4},{2,6},{4,0},{6,2},{8,12},{10,14},{12,8},{14,10},{16,20},{18,... | collective-permute-start | bytes 393224 | tf_op jit(solution)/shard_map/ppermute | solution.py:18
  72.6 22.1 %collective-permute-start.12 = (f32[4,32,2,128]{3,2,1,0:T(2,128)}, f32[4,32,2,128]{3,2,1,0:T(2,128)}, u32[]{:S(2)}, u32[]{:S(2)}) collective-permute-start(f32[4,32,2,128]{3,2,1,0:T(2,128)} %collective-permute-done.11), channel_id=1, source_target_pairs={{0,8},{2,10},{4,12},{6,14},{8,0},{10,2},{12,4},{14,6},{16,24},{18,... | collective-permute-start | bytes 393224 | tf_op jit(solution)/shard_map/ppermute | solution.py:18
  77.9 10.8 %collective-permute-start.8 = (f32[4,32,32,2]{2,1,3,0:T(8,128)S(1)}, f32[4,32,32,2]{2,1,3,0:T(8,128)}, u32[]{:S(2)}, u32[]{:S(2)}) collective-permute-start(f32[4,32,32,2]{2,1,3,0:T(8,128)S(1)} %copy.11), channel_id=1, source_target_pairs={{2,0},{4,2},{6,4},{8,6},{10,8},{12,10},{14,12},{16,14},{18,16},{20... | collective-permute-start | bytes 98312 | tf_op jit(solution)/shard_map/ppermute | solution.py:31
  82.7 9.0 %collective-permute-start.9 = (f32[4,32,32,2]{2,1,3,0:T(8,128)}, f32[4,32,32,2]{2,1,3,0:T(8,128)}, u32[]{:S(2)}, u32[]{:S(2)}) collective-permute-start(f32[4,32,32,2]{2,1,3,0:T(8,128)} %copy.13), channel_id=1, source_target_pairs={{0,2},{2,4},{4,6},{6,8},{8,10},{10,12},{12,14},{14,16},{16,18},{18... | collective-permute-start | bytes 98312 | tf_op jit(solution)/shard_map/ppermute | solution.py:29
  82.7 23.5 %collective-permute-start.15 = (f32[4,32,2,128]{3,2,1,0:T(2,128)}, f32[4,32,2,128]{3,2,1,0:T(2,128)S(1)}, u32[]{:S(2)}, u32[]{:S(2)}) collective-permute-start(f32[4,32,2,128]{3,2,1,0:T(2,128)} %copy-done.89), channel_id=1, source_target_pairs={{0,1},{2,3},{4,5},{6,7},{8,9},{10,11},{12,13},{14,15},{16,17},{18,... | collective-permute-start | bytes 393224 | tf_op jit(solution)/shard_map/ppermute | solution.py:29
  87.4 17.7 %collective-permute-start.14 = (f32[4,32,2,128]{3,2,1,0:T(2,128)}, f32[4,32,2,128]{3,2,1,0:T(2,128)}, u32[]{:S(2)}, u32[]{:S(2)}) collective-permute-start(f32[4,32,2,128]{3,2,1,0:T(2,128)} %get-tuple-element.118), channel_id=1, source_target_pairs={{1,0},{3,2},{5,4},{7,6},{9,8},{11,10},{13,12},{15,14},{17,16},{19,... | collective-permute-start | bytes 393224 | tf_op jit(solution)/shard_map/ppermute | solution.py:31
  94.8 9.0 %collective-permute-start.13 = (f32[4,32,2,128]{3,2,1,0:T(2,128)}, f32[4,32,2,128]{3,2,1,0:T(2,128)}, u32[]{:S(2)}, u32[]{:S(2)}) collective-permute-start(f32[4,32,2,128]{3,2,1,0:T(2,128)} %collective-permute-done.12), channel_id=1, source_target_pairs={{0,16},{2,18},{4,20},{6,22},{8,24},{10,26},{12,28},{14,30},{16,0},... | collective-permute-start | bytes 393224 | tf_op jit(solution)/shard_map/ppermute | solution.py:18
  (87 other events, 397.9 us)
where the time goes:
time: 120 us; the launch traced here: 119 us
  local copies, waits for them, and re-layouts  45.2 us (38%)
  other arithmetic  33.8 us (28%)
  starting transfers between devices  22.4 us (19%)
  waiting for transfers between devices  16 us (13%)
  between operations  1.98 us (2%)
    ppermute x8, waiting for transfers between devices, partner(): lax.ppermute(array, axis, [(i, i ^ 1 << distance) for i in range(lax.axis...  16 us
    slice x6, local copies, waits for them, and re-layouts, padded(): head = lax.slice_in_dim(cells, 0, width, axis=dim)  12.7 us
    another operation x4, other arithmetic, pressure(): return gravity * (jnp.cumsum(density, axis=0) - 0.5 * density)  10.3 us
    unnamed x220, local copies, waits for them, and re-layouts  10 us
    mul x2, other arithmetic, explicit(): return (state + time_step * (lateral_mix * spread - carried + force)) * wet  9.89 us
    ppermute x4, starting transfers between devices, padded(): lax.ppermute(tail, axis, [(i, (i + 1) % count) for i in range(ends)])  9.07 us
    ppermute x4, starting transfers between devices, padded(): lax.ppermute(head, axis, [((i + 1) % count, i) for i in range(ends)])  8.65 us
    slice x2, local copies, waits for them, and re-layouts, padded(): lax.slice_in_dim(cells, cells.shape[dim] - width, cells.shape[dim], axis=...  6.25 us
  transfers between devices with their start and end apart: 16, of which 5 were waited for; matrix products, arithmetic and copies ran while one was open for 40% of the time, Pallas kernels for 0%

commit v1 on v0

v1 whole, which is shorter than its diff:
```python
import functools

import jax
import jax.numpy as jnp
import numpy as np
from jax import lax
from jax.experimental import pallas as pl
from jax.experimental.pallas import tpu as pltpu
from jax.sharding import PartitionSpec as P

STEPS = 2
time_step = 0.1
lateral_mix = 0.5
column_mix = 0.5
gravity = 0.5
thermal = 0.2
haline = 0.8

F32 = jnp.float32
VM = pl.BlockSpec(memory_space=pltpu.VMEM)
SM = pl.BlockSpec(memory_space=pltpu.SMEM)
HB = pl.BlockSpec(memory_space=pltpu.HBM)
PARAMS = pltpu.CompilerParams(vmem_limit_bytes=12 * 2**20)


def factors(levels):
    inner = np.zeros(levels)
    lowest = np.zeros(levels)
    for k in range(levels):
        over = column_mix if k > 0 else 0.0
        less = column_mix * column_mix * inner[k - 1] if k > 0 else 0.0
        inner[k] = 1.0 / (1.0 + over + column_mix - less)
        lowest[k] = 1.0 / (1.0 + over - less)
    return np.stack([inner, lowest, column_mix * inner]).astype(np.float32)


def lanes():
    return lax.broadcasted_iota(jnp.int32, (8, 128), 1)


def sublanes():
    return lax.broadcasted_iota(jnp.int32, (8, 128), 0)


def pack_kernel(place, state, land, wet, p1, p2, la, lb, main, depth, held, held_land, held_wet, sems):
    levels, rows = state.shape[1], state.shape[2]
    groups = rows // 8
    chunk = levels // 4
    copies = [
        pltpu.make_async_copy(land, held_land, sems.at[4]),
        pltpu.make_async_copy(wet, held_wet, sems.at[5]),
    ] + [
        pltpu.make_async_copy(state.at[:, c * chunk:(c + 1) * chunk], held.at[:, c * chunk:(c + 1) * chunk], sems.at[c])
        for c in range(4)
    ]
    for copy in copies:
        copy.start()
    copies[0].wait()
    copies[1].wait()
    lon_even = place[0] == 0
    band_even = place[1] == 0
    depth[0:8, :] = jnp.zeros((8, 128), F32)
    depth[rows:rows + 8, :] = jnp.zeros((8, 128), F32)
    deeps = []
    for g in range(groups):
        at = slice(8 * g, 8 * g + 8)
        deep = jnp.where(held_land[at, :] == 1, jnp.minimum(held_wet[at, :], levels), 0).astype(F32)
        depth[8 * g + 4:8 * g + 12, :] = deep
        deeps.append(deep)
    group = lanes() >> 2
    low = sublanes() < 4

    def edges(a0, a3, b0, b3):
        north = jnp.where(low, pltpu.roll(a3, 4, 0), b3)
        south = jnp.where(low, a0, pltpu.roll(b0, 4, 0))
        return jnp.where(band_even, north, south), jnp.where(band_even, south, north)

    def body(k, unused):
        level = k.astype(F32)
        spot_e = group == k
        spot_w = group == ((k + 1) & (levels - 1))
        for pair in range(2):
            tiles = []
            for f in (2 * pair, 2 * pair + 1):
                for g in range(groups):
                    at = slice(8 * g, 8 * g + 8)
                    q = jnp.where(level < deeps[g], held[f, k, at, :], 0.0)
                    main[f, k, 8 * g + 4:8 * g + 12, :] = q
                    tiles.append(q)
                    turned = pltpu.roll(q, (4 * k + 4) & 127, 1)
                    la[f, at, :] = jnp.where(spot_e, turned, la[f, at, :])
                    lb[f, at, :] = jnp.where(spot_w, turned, lb[f, at, :])
            first, second = edges(tiles[0], tiles[groups - 1], tiles[groups], tiles[2 * groups - 1])
            p1[2 * k + pair] = first
            p2[2 * k + pair] = second
        return unused

    for c in range(4):
        copies[2 + c].wait()
        lax.fori_loop(c * chunk, (c + 1) * chunk, body, 0, unroll=4)
    for g in range(groups):
        turned = pltpu.roll(deeps[g], 4, 1)
        la[4, 8 * g:8 * g + 8, :] = turned
        lb[4, 8 * g:8 * g + 8, :] = turned
    first, second = edges(deeps[0], deeps[-1], deeps[0], deeps[-1])
    p1[2 * levels] = first
    p2[2 * levels] = second

    @pl.when(jnp.logical_not(lon_even))
    def _():
        for f in range(5):
            for g in range(groups):
                at = slice(8 * g, 8 * g + 8)
                east, west = la[f, at, :], lb[f, at, :]
                la[f, at, :] = west
                lb[f, at, :] = east


def coriolis_rows(first, total):
    row = first + sublanes()
    row = jnp.where(row >= total, 2 * total - 1 - row, row)
    return 0.2 + 0.8 * ((row.astype(F32) + 0.5) / total.astype(F32))


def sweep(table, levels, jobs, unroll=8, unroll_back=8):
    lane = lanes()
    zero = jnp.zeros((8, 128), F32)

    def forward(k, carry):
        inner, lowest = table[0, k], table[1, k]
        level = k.astype(F32)
        out = []
        for n, (own, other, o, depth, cor, dst, d) in enumerate(jobs):
            parts = carry[6 * n:6 * n + 4]
            cum_x, cum_y = carry[6 * n + 4:6 * n + 6]
            weight = jnp.where(level < depth - 1.0, inner, jnp.where(level < depth, lowest, 0.0))
            q = [own[f, k, o:o + 8, :] for f in range(4)]
            cu = q[2] * (time_step / 12.0)
            cv = q[3] * (time_step / 12.0)
            prov = []
            near = []
            for f in range(4):
                x = other[f, k, o:o + 8, :]
                e1 = pltpu.roll(jnp.where(lane == 0, x, q[f]), 127, 1)
                e2 = pltpu.roll(jnp.where(lane < 2, x, q[f]), 126, 1)
                w1 = pltpu.roll(jnp.where(lane == 127, x, q[f]), 1, 1)
                w2 = pltpu.roll(jnp.where(lane >= 126, x, q[f]), 2, 1)
                n1 = own[f, k, o + 1:o + 9, :]
                n2 = own[f, k, o + 2:o + 10, :]
                s1 = own[f, k, o - 1:o + 7, :]
                s2 = own[f, k, o - 2:o + 6, :]
                dx, dy = e1 - w1, n1 - s1
                near.append((dx, dy))
                spread = (e1 + w1) + (n1 + s1)
                value = (1.0 - 4.0 * time_step * lateral_mix) * q[f] + (time_step * lateral_mix) * spread
                value = value - cu * (8.0 * dx - (e2 - w2)) - cv * (8.0 * dy - (n2 - s2))
                prov.append(value)
            dens_x = haline * near[1][0] - thermal * near[0][0]
            dens_y = haline * near[1][1] - thermal * near[0][1]
            cum_x = cum_x + dens_x
            cum_y = cum_y + dens_y
            press = time_step * gravity * 0.5
            prov[2] = prov[2] + (time_step * cor) * q[3] - press * (cum_x - 0.5 * dens_x)
            prov[3] = prov[3] - (time_step * cor) * q[2] - press * (cum_y - 0.5 * dens_y)
            for f in range(4):
                part = (prov[f] + column_mix * parts[f]) * weight
                dst[f, k, d:d + 8, :] = part
                out.append(part)
            out += [cum_x, cum_y]
        return tuple(out)

    lax.fori_loop(0, levels, forward, (zero,) * (6 * len(jobs)), unroll=unroll)

    def backward(step, carry):
        k = levels - 1 - step
        ratio = table[2, k]
        out = []
        for n, (own, other, o, depth, cor, dst, d) in enumerate(jobs):
            for f in range(4):
                value = dst[f, k, d:d + 8, :] + ratio * carry[4 * n + f]
                dst[f, k, d:d + 8, :] = value
                out.append(value)
        return tuple(out)

    lax.fori_loop(0, levels, backward, (zero,) * (4 * len(jobs)), unroll=unroll_back)


def side_tile(east, west, group, k):
    return pltpu.roll(jnp.where(group == k, west, east), (124 - 4 * k) & 127, 1)


def spread_corner(corner, shift):
    return pltpu.roll(corner, shift & 127, 1)


def inner_kernel(place, table, main0, depth, ra, rb, out, side0, side1, main1, side_depth, last, sem):
    levels, rows = main0.shape[1], out.shape[2]
    groups = rows // 8
    lon_even = place[0] == 0
    first_row, total = place[2], place[3]
    group = lanes() >> 2
    zero = jnp.zeros((8, 128), F32)

    def both(f, g):
        at = slice(8 * g, 8 * g + 8)
        a, b = ra[f, at, :], rb[f, at, :]
        return jnp.where(lon_even, a, b), jnp.where(lon_even, b, a)

    side_depth[0:8, :] = zero
    side_depth[rows:rows + 8, :] = zero
    for g in range(groups):
        east, west = both(4, g)
        side_depth[8 * g + 4:8 * g + 12, :] = side_tile(east, west, group, 0)
    for f in range(4):
        pairs = [both(f, g) for g in range(groups)]

        def fill(k, unused):
            for g in range(groups):
                side0[f, k, 8 * g + 4:8 * g + 12, :] = side_tile(*pairs[g], group, k)
            return unused

        lax.fori_loop(0, levels, fill, 0, unroll=4)

    jobs = []
    for w in range(1, groups):
        o = 8 * w + 2
        cor = coriolis_rows(first_row + (8 * w - 2), total)
        jobs.append((main0, side0, o, depth[o:o + 8, :], cor, main1, 8 * w))
        jobs.append((side0, main0, o, side_depth[o:o + 8, :], cor, side1, 8 * w))
    sweep(table, levels, jobs, 4, 4)
    jobs = []
    for w in range(1, groups - 1):
        cor = coriolis_rows(first_row + 8 * w, total)
        jobs.append((main1, side1, 8 * w + 2, depth[8 * w + 4:8 * w + 12, :], cor, last, 8 * w - 8))
    sweep(table, levels, jobs)
    copy = pltpu.make_async_copy(last, out.at[:, :, 8:rows - 8, :], sem)
    copy.start()
    copy.wait()


def south_kernel(place, table, p, corner, depth, side_depth, main0, side0, main1, side1, before, out,
                 rim0, edge0, rim1, edge1, last, sem):
    levels = main0.shape[1]
    first_row, total = place[2], place[3]
    has_south = first_row > 0
    edge = jnp.where(has_south, corner[...], 0.0)
    rim_depth = jnp.where(has_south, p[2 * levels], 0.0)
    depths = jnp.where(sublanes() < 2, pltpu.roll(rim_depth, 6, 0), depth[2:10, :])

    def fill(k, unused):
        corners = spread_corner(edge, 124 - 4 * k)
        for pair in range(2):
            rim = jnp.where(has_south, p[2 * k + pair], 0.0)
            for j in range(2):
                f = 2 * pair + j
                rim0[f, k, 0:4, :] = rim[4 * j:4 * j + 4, :]
                rim0[f, k, 4:12, :] = main0[f, k, 4:12, :]
                edge0[f, k, 0:2, :] = jnp.zeros((2, 128), F32)
                edge0[f, k, 2:4, :] = corners[2 * f:2 * f + 2, :]
                edge0[f, k, 4:12, :] = side0[f, k, 4:12, :]
                rim1[f, k, 8:12, :] = main1[f, k, 8:12, :]
                edge1[f, k, 8:12, :] = side1[f, k, 8:12, :]
        return unused

    lax.fori_loop(0, levels, fill, 0, unroll=4)
    cor = coriolis_rows(first_row - 2, total)
    sweep(table, levels, [
        (rim0, edge0, 2, depths, cor, rim1, 0),
        (edge0, rim0, 2, side_depth[2:10, :], cor, edge1, 0),
    ])
    cor = coriolis_rows(first_row, total)
    sweep(table, levels, [(rim1, edge1, 2, depth[4:12, :], cor, last, 0)])
    copy = pltpu.make_async_copy(last, out.at[:, :, 0:8, :], sem)
    copy.start()
    copy.wait()


def north_kernel(place, table, p1, p2, c1, c2, depth, side_depth, main0, side0, main1, side1, before, out,
                 rim0, edge0, rim1, edge1, last, sem):
    levels, rows = main0.shape[1], out.shape[2]
    band_even = place[1] == 0
    first_row, total = place[2], place[3]
    is_top = first_row + rows == total
    mirror = 127 - lanes()
    flip = sublanes() ^ 3

    def ghost(index, sign):
        far = p2[index]
        folded = jnp.take_along_axis(far, mirror, axis=1, mode="promise_in_bounds")
        folded = jnp.take_along_axis(folded, flip, axis=0, mode="promise_in_bounds") * sign
        return jnp.where(band_even, p1[index], jnp.where(is_top, folded, far))

    far = c2[...]
    folded = jnp.take_along_axis(far, mirror, axis=1, mode="promise_in_bounds")
    folded = jnp.where(sublanes() < 4, folded, -folded)
    corner = jnp.where(band_even, c1[...], jnp.where(is_top, folded, far))
    depths = jnp.where(sublanes() < 6, depth[rows - 2:rows + 6, :], pltpu.roll(ghost(2 * levels, 1.0), 6, 0))

    def fill(k, unused):
        corners = spread_corner(corner, jnp.where(is_top, 4 * k - 124, 124 - 4 * k))
        for pair in range(2):
            rim = ghost(2 * k + pair, 1.0 if pair == 0 else -1.0)
            for j in range(2):
                f = 2 * pair + j
                rim0[f, k, 0:8, :] = main0[f, k, rows - 4:rows + 4, :]
                rim0[f, k, 8:12, :] = rim[4 * j:4 * j + 4, :]
                edge0[f, k, 0:8, :] = side0[f, k, rows - 4:rows + 4, :]
                edge0[f, k, 8:10, :] = corners[2 * f:2 * f + 2, :]
                edge0[f, k, 10:12, :] = jnp.zeros((2, 128), F32)
                rim1[f, k, 0:4, :] = main1[f, k, rows - 8:rows - 4, :]
                edge1[f, k, 0:4, :] = side1[f, k, rows - 8:rows - 4, :]
        return unused

    lax.fori_loop(0, levels, fill, 0, unroll=4)
    cor = coriolis_rows(first_row + (rows - 6), total)
    sweep(table, levels, [
        (rim0, edge0, 2, depths, cor, rim1, 4),
        (edge0, rim0, 2, side_depth[rows - 2:rows + 6, :], cor, edge1, 4),
    ])
    cor = coriolis_rows(first_row + (rows - 8), total)
    sweep(table, levels, [(rim1, edge1, 2, depth[rows - 4:rows + 4, :], cor, last, 0)])
    copy = pltpu.make_async_copy(last, out.at[:, :, rows - 8:rows, :], sem)
    copy.start()
    copy.wait()


def per_device(state, land_mask, wet_levels):
    fields, levels, rows, cols = state.shape
    lon, lat = lax.axis_index("lon"), lax.axis_index("lat")
    count, bands = lax.axis_size("lon"), lax.axis_size("lat")
    place = jnp.stack([lon & 1, lat & 1, lat * rows, bands * rows]).astype(jnp.int32)
    table = jnp.asarray(factors(levels))

    def mate(i):
        return i ^ 1

    def beyond(i):
        return (i + 1) % count if i % 2 else (i - 1) % count

    def swap(x, to):
        pairs = []
        for i in range(count):
            for b in range(bands):
                ti, tb = to(i, b)
                pairs.append((i * bands + b, ti * bands + tb))
        return lax.ppermute(x, ("lon", "lat"), pairs)

    def near(i, b):
        return i, b ^ 1

    def far(i, b):
        if b == bands - 1:
            return count - 1 - i, b
        if b == 0:
            return i, b
        return i, (b + 1 if b % 2 else b - 1)

    call = functools.partial(pl.pallas_call, compiler_params=PARAMS)
    shape = lambda *dims: jax.ShapeDtypeStruct(dims, F32)
    block = lambda n: shape(fields, levels, n, 128)
    room = lambda n: pltpu.VMEM((fields, levels, n, 128), F32)
    edge, strip = shape(2 * levels + 1, 8, 128), shape(5, rows, 128)
    p1, p2, la, lb, main0, depth = call(
        pack_kernel,
        out_shape=(edge, edge, strip, strip, block(rows + 8), shape(rows + 8, 128)),
        in_specs=[SM, HB, HB, HB],
        out_specs=(VM,) * 6,
        scratch_shapes=[room(rows), pltpu.VMEM((rows, 128), jnp.int32), pltpu.VMEM((rows, 128), jnp.int32),
                        pltpu.SemaphoreType.DMA((6,))],
        name="pack",
    )(place, state, land_mask, wet_levels)
    rp2 = swap(p2, far)
    rb = swap(lb, lambda i, b: (beyond(i), b))
    ra = swap(la, lambda i, b: (mate(i), b))
    rp1 = swap(p1, near)

    lon_even = lon & 1 == 0
    band_even = lat & 1 == 0
    lane = jnp.arange(128, dtype=jnp.int32)
    ends = lambda x: (x[:4, 0:2], x[:4, rows - 2:rows])
    (a_low, a_high), (b_low, b_high) = ends(ra), ends(rb)
    from_east = (lane % 4 < 2) == lon_even
    low = jnp.where(from_east, a_low, b_low)
    high = jnp.where(from_east, a_high, b_high)
    back = jnp.where(lat == bands - 1, high[:, ::-1], high)
    rc1 = swap(jnp.where(band_even, high, low).reshape(8, 128), near)
    rc2 = swap(jnp.where(band_even, low, back).reshape(8, 128), far)

    if bands == 2:
        south, south_corner = rp1, rc1
    else:
        south = jnp.where(band_even, rp2, rp1)
        south_corner = jnp.where(band_even, rc2, rc1)

    out, side0, side1, main1, side_depth = call(
        inner_kernel,
        out_shape=(shape(*state.shape), block(rows + 8), block(rows + 4), block(rows + 4), shape(rows + 8, 128)),
        in_specs=[SM, SM] + [VM] * 4,
        out_specs=(HB, VM, VM, VM, VM),
        scratch_shapes=[room(rows - 16), pltpu.SemaphoreType.DMA],
        name="inner",
    )(place, table, main0, depth, ra, rb)
    rim = functools.partial(
        call,
        out_shape=shape(*state.shape),
        out_specs=HB,
        scratch_shapes=[room(16)] * 4 + [room(8), pltpu.SemaphoreType.DMA],
    )
    out = rim(
        south_kernel,
        in_specs=[SM, SM] + [VM] * 8 + [HB],
        input_output_aliases={10: 0},
        name="south",
    )(place, table, south, south_corner, depth, side_depth, main0, side0, main1, side1, out)
    return rim(
        north_kernel,
        in_specs=[SM, SM] + [VM] * 10 + [HB],
        input_output_aliases={12: 0},
        name="north",
    )(place, table, rp1, rp2, rc1, rc2, depth, side_depth, main0, side0, main1, side1, out)


def solution(mesh):
    placed = (P(None, None, "lat", "lon"), P("lat", "lon"), P("lat", "lon"))
    return jax.shard_map(
        per_device,
        mesh=mesh,
        in_specs=placed,
        out_specs=P(None, None, "lat", "lon"),
        check_vma=False,
    )
```

time: 120 us -> 40.8 us (0.34)
  the two profiles are of different devices: /device:TPU:0 before, /device:TPU:2 now
where the time goes in v1:
time: 40.8 us; the launch traced here: 40.4 us
  Pallas kernels  22.8 us (56%)
  starting transfers between devices  13.6 us (33%)
  local copies, waits for them, and re-layouts  3.73 us (9%)
    ppermute x6, starting transfers between devices, swap(): return lax.ppermute(x, ('lon', 'lat'), pairs)  13.6 us
    pallas_call x1, Pallas kernels, per_device(): call(inner_kernel, out_shape=(shape(*state.shape), block(rows + 8), block...  10.4 us
    pallas_call x1, Pallas kernels, per_device(): rim(north_kernel, in_specs=[SM, SM] + [VM] * 10 + [HB], input_output_alia...  4.98 us
    pallas_call x1, Pallas kernels, per_device(): rim(south_kernel, in_specs=[SM, SM] + [VM] * 8 + [HB], input_output_alias...  4.74 us
    unnamed x8, local copies, waits for them, and re-layouts  3.7 us
    pallas_call x1, Pallas kernels, per_device(): call(pack_kernel, out_shape=(edge, edge, strip, strip, block(rows + 8), s...  2.7 us
  transfers between devices with their start and end apart: 6, of which 0 were waited for; matrix products, arithmetic and copies ran while one was open for 0% of the time, Pallas kernels for 37%

profile of v1, /device:TPU:2, one launch (start us, length us, event | category | flops | bytes accessed | tf_op | source)
XLA Modules:
  0.0 40.4 jit_solution(3609012316436959868)
XLA Ops:
  0.0 0.1 pad_add_fusion.place
  0.1 0.0 copy-start
  0.1 1.6 %copy-done = f32[4,32,32,128]{3,2,1,0:T(8,128)S(1)} copy-done((f32[4,32,32,128]{3,2,1,0:T(8,128)S(1)}, f32[4,32,32,128]{3,2,1,0:T(8,128)}, u32[]{:S(2)}) %copy-start) | copy-done | bytes 2097176
  1.7 0.0 copy-start.2
  1.7 0.7 %copy-done.2 = s32[32,128]{1,0:T(8,128)S(1)} copy-done((s32[32,128]{1,0:T(8,128)S(1)}, s32[32,128]{1,0:T(8,128)}, u32[]{:S(2)}) %copy-start.2) | copy-done | bytes 16408
  2.4 0.7 %copy-done.3 = s32[32,128]{1,0:T(8,128)S(1)} copy-done((s32[32,128]{1,0:T(8,128)S(1)}, s32[32,128]{1,0:T(8,128)}, u32[]{:S(2)}) %copy-start.3) | copy-done | bytes 16408
  3.1 2.7 %pack.1 = (f32[65,8,128]{2,1,0:T(8,128)}, f32[65,8,128]{2,1,0:T(8,128)}, f32[5,32,128]{2,1,0:T(8,128)S(1)}, f32[5,32,128]{2,1,0:T(8,128)S(1)}, f32[4,32,40,128]{3,2,1,0:T(8,128)S(1)}, /*index=5*/f32[40,128]{1,0:T(8,128)S(1)}) custom-call(s32[4]{0:T(128)S(1)} %pad_add_fusion.place, f32[4,32,32,128]{3,2,1,0:T(8,128)S(1)} %copy-done, s32[32,128]{1,0:T(8,128)S(1)} %copy-done.2, ...), custom_call_target="tpu_custom_call" | custom-call | tf_op jit(solution)/shard_map/pack/pallas_call | solution.py:363
  5.8 0.1 collective-permute-start.2
  5.9 4.7 %collective-permute-start.3 = (f32[5,32,128]{2,1,0:T(8,128)S(1)}, f32[5,32,128]{2,1,0:T(8,128)S(1)}, u32[]{:S(2)}, u32[]{:S(2)}) collective-permute-start(f32[5,32,128]{2,1,0:T(8,128)S(1)} %get-tuple-element.19), channel_id=1, source_target_pairs={{0,30},{1,31},{2,4},{3,5},{4,2},{5,3},{6,8},{7,9},{8,6},{9,7},{10,... | collective-permute-start | bytes 245768 | tf_op jit(solution)/shard_map/ppermute | solution.py:346
  10.6 0.5 %collective-permute-start = (f32[65,8,128]{2,1,0:T(8,128)}, f32[65,8,128]{2,1,0:T(8,128)S(1)}, u32[]{:S(2)}, u32[]{:S(2)}) collective-permute-start(f32[65,8,128]{2,1,0:T(8,128)} %get-tuple-element.16), channel_id=1, source_target_pairs={{0,1},{1,0},{2,3},{3,2},{4,5},{5,4},{6,7},{7,6},{8,9},{9,8},{10,11... | collective-permute-start | bytes 798728 | tf_op jit(solution)/shard_map/ppermute | solution.py:346
  11.1 1.9 %collective-permute-start.1 = (f32[65,8,128]{2,1,0:T(8,128)}, f32[65,8,128]{2,1,0:T(8,128)S(1)}, u32[]{:S(2)}, u32[]{:S(2)}) collective-permute-start(f32[65,8,128]{2,1,0:T(8,128)} %get-tuple-element.17), channel_id=1, source_target_pairs={{0,0},{1,31},{2,2},{3,29},{4,4},{5,27},{6,6},{7,25},{8,8},{9,23},{... | collective-permute-start | bytes 798728 | tf_op jit(solution)/shard_map/ppermute | solution.py:346
  13.0 0.0 collective-permute-done.2.ra
  13.0 0.0 collective-permute-done.3.rb
  13.1 1.2 %collective-permute-start.4 = (f32[8,128]{1,0:T(8,128)S(1)}, f32[8,128]{1,0:T(8,128)S(1)}, u32[]{:S(2)}, u32[]{:S(2)}) collective-permute-start(f32[8,128]{1,0:T(8,128)S(1)} %bitcast.5), channel_id=1, source_target_pairs={{0,1},{1,0},{2,3},{3,2},{4,5},{5,4},{6,7},{7,6},{8,9},{9,8},{10,11... | collective-permute-start | bytes 12296 | tf_op jit(solution)/shard_map/ppermute | solution.py:346
  14.3 5.2 %collective-permute-start.5 = (f32[8,128]{1,0:T(8,128)S(1)}, f32[8,128]{1,0:T(8,128)S(1)}, u32[]{:S(2)}, u32[]{:S(2)}) collective-permute-start(f32[8,128]{1,0:T(8,128)S(1)} %bitcast.6), channel_id=1, source_target_pairs={{0,0},{1,31},{2,2},{3,29},{4,4},{5,27},{6,6},{7,25},{8,8},{9,23},{... | collective-permute-start | bytes 12296 | tf_op jit(solution)/shard_map/ppermute | solution.py:346
  19.5 0.0 copy-start.1
  19.6 0.7 %copy-done.1 = f32[3,32]{1,0:T(4,128)S(1)} copy-done((f32[3,32]{1,0:T(4,128)S(1)}, f32[3,32]{1,0:T(4,128)}, u32[]{:S(2)}) %copy-start.1) | copy-done | bytes 408
  20.2 10.4 %inner.1 = (f32[4,32,32,128]{3,2,1,0:T(8,128)}, f32[4,32,40,128]{3,2,1,0:T(8,128)S(1)}, f32[4,32,36,128]{3,2,1,0:T(8,128)S(1)}, f32[4,32,36,128]{3,2,1,0:T(8,128)S(1)}, f32[40,128]{1,0:T(8,128)S(1)}) custom-call(s32[4]{0:T(128)S(1)} %pad_add_fusion.place, f32[3,32]{1,0:T(4,128)S(1)} %copy-done.1, f32[4,32,40,128]{3,2,1,0:T(8,128)S(1)} %get-tuple-element.21.main0, ...), custom_call_target="tpu_custom_call" | custom-call | tf_op jit(solution)/shard_map/inner/pallas_call | solution.py:395
  30.6 0.0 collective-permute-done.4.corner.c1
  30.7 0.0 collective-permute-done.p.p1
  30.7 4.7 %south.1.before = f32[4,32,32,128]{3,2,1,0:T(8,128)} custom-call(s32[4]{0:T(128)S(1)} %pad_add_fusion.place, f32[3,32]{1,0:T(4,128)S(1)} %copy-done.1, f32[65,8,128]{2,1,0:T(8,128)S(1)} %collective-permute-done.p.p1, f32[8,128]{1,0:T(8,128)S(1)} %collective-permute-done.4.corner.c1, ...), custom_call_target="tpu_custom_call", output_to_operand_aliasing={{}: (10, {})} | custom-call | tf_op jit(solution)/shard_map/south/pallas_call | solution.py:409
  35.4 0.0 collective-permute-done.5.c2
  35.4 0.0 collective-permute-done.1.p2
  35.4 5.0 %north.1 = f32[4,32,32,128]{3,2,1,0:T(8,128)} custom-call(s32[4]{0:T(128)S(1)} %pad_add_fusion.place, f32[3,32]{1,0:T(4,128)S(1)} %copy-done.1, f32[65,8,128]{2,1,0:T(8,128)S(1)} %collective-permute-done.p.p1, f32[65,8,128]{2,1,0:T(8,128)S(1)} %collective-permute-done.1.p2, ...), custom_call_target="tpu_custom_call", output_to_operand_aliasing={{}: (12, {})} | custom-call | tf_op jit(solution)/shard_map/north/pallas_call | solution.py:415
  (5 shorter events, 0.1 us)
Async XLA Ops:
  0.1 1.6 %copy-start = (f32[4,32,32,128]{3,2,1,0:T(8,128)S(1)}, f32[4,32,32,128]{3,2,1,0:T(8,128)}, u32[]{:S(2)}) copy-start(f32[4,32,32,128]{3,2,1,0:T(8,128)} %state.1) | copy-start | bytes 6291460
  1.7 0.7 %copy-start.2 = (s32[32,128]{1,0:T(8,128)S(1)}, s32[32,128]{1,0:T(8,128)}, u32[]{:S(2)}) copy-start(s32[32,128]{1,0:T(8,128)} %land.1) | copy-start | bytes 49156
  2.4 0.7 %copy-start.3 = (s32[32,128]{1,0:T(8,128)S(1)}, s32[32,128]{1,0:T(8,128)}, u32[]{:S(2)}) copy-start(s32[32,128]{1,0:T(8,128)} %wet.1) | copy-start | bytes 49156
  5.8 7.2 %collective-permute-start.2 = (f32[5,32,128]{2,1,0:T(8,128)S(1)}, f32[5,32,128]{2,1,0:T(8,128)S(1)}, u32[]{:S(2)}, u32[]{:S(2)}) collective-permute-start(f32[5,32,128]{2,1,0:T(8,128)S(1)} %get-tuple-element.18), channel_id=1, source_target_pairs={{0,2},{1,3},{2,0},{3,1},{4,6},{5,7},{6,4},{7,5},{8,10},{9,11},{10,... | collective-permute-start | bytes 245768 | tf_op jit(solution)/shard_map/ppermute | solution.py:346
  5.9 7.1 %collective-permute-start.3 = (f32[5,32,128]{2,1,0:T(8,128)S(1)}, f32[5,32,128]{2,1,0:T(8,128)S(1)}, u32[]{:S(2)}, u32[]{:S(2)}) collective-permute-start(f32[5,32,128]{2,1,0:T(8,128)S(1)} %get-tuple-element.19), channel_id=1, source_target_pairs={{0,30},{1,31},{2,4},{3,5},{4,2},{5,3},{6,8},{7,9},{8,6},{9,7},{10,... | collective-permute-start | bytes 245768 | tf_op jit(solution)/shard_map/ppermute | solution.py:346
  10.6 20.1 %collective-permute-start = (f32[65,8,128]{2,1,0:T(8,128)}, f32[65,8,128]{2,1,0:T(8,128)S(1)}, u32[]{:S(2)}, u32[]{:S(2)}) collective-permute-start(f32[65,8,128]{2,1,0:T(8,128)} %get-tuple-element.16), channel_id=1, source_target_pairs={{0,1},{1,0},{2,3},{3,2},{4,5},{5,4},{6,7},{7,6},{8,9},{9,8},{10,11... | collective-permute-start | bytes 798728 | tf_op jit(solution)/shard_map/ppermute | solution.py:346
  11.1 24.3 %collective-permute-start.1 = (f32[65,8,128]{2,1,0:T(8,128)}, f32[65,8,128]{2,1,0:T(8,128)S(1)}, u32[]{:S(2)}, u32[]{:S(2)}) collective-permute-start(f32[65,8,128]{2,1,0:T(8,128)} %get-tuple-element.17), channel_id=1, source_target_pairs={{0,0},{1,31},{2,2},{3,29},{4,4},{5,27},{6,6},{7,25},{8,8},{9,23},{... | collective-permute-start | bytes 798728 | tf_op jit(solution)/shard_map/ppermute | solution.py:346
  13.1 17.5 %collective-permute-start.4 = (f32[8,128]{1,0:T(8,128)S(1)}, f32[8,128]{1,0:T(8,128)S(1)}, u32[]{:S(2)}, u32[]{:S(2)}) collective-permute-start(f32[8,128]{1,0:T(8,128)S(1)} %bitcast.5), channel_id=1, source_target_pairs={{0,1},{1,0},{2,3},{3,2},{4,5},{5,4},{6,7},{7,6},{8,9},{9,8},{10,11... | collective-permute-start | bytes 12296 | tf_op jit(solution)/shard_map/ppermute | solution.py:346
  14.3 21.1 %collective-permute-start.5 = (f32[8,128]{1,0:T(8,128)S(1)}, f32[8,128]{1,0:T(8,128)S(1)}, u32[]{:S(2)}, u32[]{:S(2)}) collective-permute-start(f32[8,128]{1,0:T(8,128)S(1)} %bitcast.6), channel_id=1, source_target_pairs={{0,0},{1,31},{2,2},{3,29},{4,4},{5,27},{6,6},{7,25},{8,8},{9,23},{... | collective-permute-start | bytes 12296 | tf_op jit(solution)/shard_map/ppermute | solution.py:346
  19.5 0.7 %copy-start.1 = (f32[3,32]{1,0:T(4,128)S(1)}, f32[3,32]{1,0:T(4,128)}, u32[]{:S(2)}) copy-start(f32[3,32]{1,0:T(4,128)} %constant.35.clone.table) | copy-start | bytes 1156

commit v2 on v1

v2 whole, which is shorter than its diff:
```python
import functools

import jax
import jax.numpy as jnp
import numpy as np
from jax import lax
from jax.experimental import pallas as pl
from jax.experimental.pallas import tpu as pltpu
from jax.sharding import PartitionSpec as P

STEPS = 2
time_step = 0.1
lateral_mix = 0.5
column_mix = 0.5
gravity = 0.5
thermal = 0.2
haline = 0.8

F32 = jnp.float32
VM = pl.BlockSpec(memory_space=pltpu.VMEM)
HB = pl.BlockSpec(memory_space=pltpu.HBM)


UNIT = 1.0 / (time_step * lateral_mix)
GAIN = column_mix * UNIT
CENTRE = UNIT * (1.0 - 4.0 * time_step * lateral_mix)
DRIFT = UNIT * time_step / 12.0
PRESS = UNIT * time_step * 0.5 * gravity * 0.5


def factors(levels):
    inner = np.zeros(levels)
    lowest = np.zeros(levels)
    for k in range(levels):
        over = column_mix if k > 0 else 0.0
        less = column_mix * inner[k - 1] if k > 0 else 0.0
        inner[k] = column_mix / (1.0 + over + column_mix - less)
        lowest[k] = column_mix / (1.0 + over - less)
    return np.stack([inner, lowest]).astype(np.float32)


def fill_table(table):
    for n, row in enumerate(factors(table.shape[1])):
        for k, value in enumerate(row):
            table[n, k] = float(value)


def lanes():
    return lax.broadcasted_iota(jnp.int32, (8, 128), 1)


def sublanes():
    return lax.broadcasted_iota(jnp.int32, (8, 128), 0)


def pack_kernel(state, depth, p1, p2, la, lb):
    levels, rows = state.shape[1], state.shape[2]
    groups = rows // 8
    lon_even = lax.axis_index("lon") % 2 == 0
    band_even = lax.axis_index("lat") % 2 == 0
    zero = jnp.zeros((8, 128), F32)
    deeps = [depth[8 * g + 4:8 * g + 12, :] for g in range(groups)]
    group = lanes() >> 2
    low = sublanes() < 4

    def edges(a0, a3, b0, b3):
        north = jnp.where(low, pltpu.roll(a3, 4, 0), b3)
        south = jnp.where(low, a0, pltpu.roll(b0, 4, 0))
        return jnp.where(band_even, north, south), jnp.where(band_even, south, north)

    for pair in range(2):
        def body(k, accs):
            level = k.astype(F32)
            spot_e = group == k
            spot_w = group == ((k + 1) & (levels - 1))
            tiles = []
            new = []
            for j in range(2):
                for g in range(groups):
                    q = jnp.where(level < deeps[g], state[2 * pair + j, k, 8 * g:8 * g + 8, :], 0.0)
                    tiles.append(q)
                    turned = pltpu.roll(q, (4 * k + 4) & 127, 1)
                    new.append(jnp.where(spot_e, turned, accs[len(new)]))
                    new.append(jnp.where(spot_w, turned, accs[len(new)]))
            first, second = edges(tiles[0], tiles[groups - 1], tiles[groups], tiles[2 * groups - 1])
            p1[2 * k + pair] = first
            p2[2 * k + pair] = second
            return tuple(new)

        accs = lax.fori_loop(0, levels, body, (zero,) * (4 * groups), unroll=8)
        for j in range(2):
            for g in range(groups):
                at = slice(8 * g, 8 * g + 8)
                east, west = accs[2 * (j * groups + g)], accs[2 * (j * groups + g) + 1]
                la[2 * pair + j, at, :] = jnp.where(lon_even, east, west)
                lb[2 * pair + j, at, :] = jnp.where(lon_even, west, east)
    for g in range(groups):
        turned = pltpu.roll(deeps[g], 4, 1)
        la[4, 8 * g:8 * g + 8, :] = turned
        lb[4, 8 * g:8 * g + 8, :] = turned
    first, second = edges(deeps[0], deeps[-1], deeps[0], deeps[-1])
    p1[2 * levels] = first
    p2[2 * levels] = second


def coriolis_rows(first, total):
    row = first + sublanes()
    row = jnp.where(row >= total, 2 * total - 1 - row, row)
    return 0.2 + 0.8 * ((row.astype(F32) + 0.5) / total)


def sweep(table, levels, jobs, scale, leave=1.0, unroll=8, unroll_back=8):
    lane = lanes()
    zero = jnp.zeros((8, 128), F32)
    turns = [cor * (UNIT * time_step * scale / DRIFT) for _, _, _, _, cor, _, _ in jobs]
    uppers = [depth - 1.0 for _, _, _, depth, _, _, _ in jobs]

    def forward(k, carry):
        inner, lowest = table[0, k], table[1, k]
        level = k.astype(F32)
        out = []
        for n, (own, other, o, depth, _, dst, d) in enumerate(jobs):
            halves = carry[6 * n:6 * n + 4]
            sums = carry[6 * n + 4:6 * n + 6]
            weight = jnp.where(level < uppers[n], inner, jnp.where(level < depth, lowest, 0.0))
            q = [own[f, k, o:o + 8, :] for f in range(4)]
            cu = q[2] * (DRIFT / scale)
            cv = q[3] * (DRIFT / scale)
            prov = []
            near = []
            for f in range(4):
                x = other[f, k, o:o + 8, :]
                e1 = pltpu.roll(jnp.where(lane == 0, x, q[f]), 127, 1)
                e2 = pltpu.roll(jnp.where(lane < 2, x, q[f]), 126, 1)
                w1 = pltpu.roll(jnp.where(lane == 127, x, q[f]), 1, 1)
                w2 = pltpu.roll(jnp.where(lane >= 126, x, q[f]), 2, 1)
                n1 = own[f, k, o + 1:o + 9, :]
                n2 = own[f, k, o + 2:o + 10, :]
                s1 = own[f, k, o - 1:o + 7, :]
                s2 = own[f, k, o - 2:o + 6, :]
                dx, dy = e1 - w1, n1 - s1
                near.append((dx, dy))
                slope_x = 8.0 * dx - (e2 - w2)
                slope_y = 8.0 * dy - (n2 - s2)
                if f == 2:
                    slope_y = slope_y - turns[n]
                if f == 3:
                    slope_x = slope_x + turns[n]
                value = CENTRE * q[f] + ((e1 + w1) + (n1 + s1))
                prov.append(value - cu * slope_x - cv * slope_y)
            for axis in range(2):
                half = (PRESS * haline) * near[1][axis] - (PRESS * thermal) * near[0][axis]
                press = sums[axis] + half
                prov[2 + axis] = prov[2 + axis] - press
                near.append(press + half)
            for f in range(4):
                part = (prov[f] + halves[f]) * weight
                dst[f, k, d:d + 8, :] = part
                out.append(part)
            out += near[4:6]
        return tuple(out)

    lax.fori_loop(0, levels, forward, (zero,) * (6 * len(jobs)), unroll=unroll)

    def backward(step, carry):
        k = levels - 1 - step
        ratio = table[0, k]
        out = []
        for n, (_, _, _, _, _, dst, d) in enumerate(jobs):
            for f in range(4):
                value = dst[f, k, d:d + 8, :] + ratio * carry[4 * n + f]
                dst[f, k, d:d + 8, :] = value * leave if leave != 1.0 else value
                out.append(value)
        return tuple(out)

    lax.fori_loop(0, levels, backward, (zero,) * (4 * len(jobs)), unroll=unroll_back)


def side_tile(east, west, group, k):
    return pltpu.roll(jnp.where(group == k, west, east), (124 - 4 * k) & 127, 1)


def spread_corner(corner, shift):
    return pltpu.roll(corner, shift & 127, 1)


def inner_kernel(state, depth, ra, rb, main0, side0, side1, main1, side_depth, last, easts, wests, table):
    levels, rows = state.shape[1], state.shape[2]
    groups = rows // 8
    lon_even = lax.axis_index("lon") % 2 == 0
    first_row = lax.axis_index("lat") * rows
    total = rows * lax.axis_size("lat")
    fill_table(table)
    group = lanes() >> 2
    zero = jnp.zeros((8, 128), F32)

    for f in range(5):
        for g in range(groups):
            at = slice(8 * g, 8 * g + 8)
            a, b = ra[f, at, :], rb[f, at, :]
            easts[f, at, :] = jnp.where(lon_even, a, b)
            wests[f, at, :] = jnp.where(lon_even, b, a)
    side_depth[0:8, :] = zero
    side_depth[rows:rows + 8, :] = zero
    for g in range(groups):
        at = slice(8 * g, 8 * g + 8)
        side_depth[8 * g + 4:8 * g + 12, :] = side_tile(easts[4, at, :], wests[4, at, :], group, 0)

    def fill(k, unused):
        level = k.astype(F32)
        for g in range(groups):
            at = slice(8 * g, 8 * g + 8)
            to = slice(8 * g + 4, 8 * g + 12)
            is_wet = level < depth[to, :]
            for f in range(4):
                main0[f, k, to, :] = jnp.where(is_wet, state[f, k, at, :], 0.0)
                side0[f, k, to, :] = side_tile(easts[f, at, :], wests[f, at, :], group, k)
        return unused

    lax.fori_loop(0, levels, fill, 0, unroll=8)

    jobs = []
    for w in range(1, groups):
        o = 8 * w + 2
        cor = coriolis_rows(first_row + (8 * w - 2), total)
        jobs.append((main0, side0, o, depth[o:o + 8, :], cor, main1, 8 * w))
        jobs.append((side0, main0, o, side_depth[o:o + 8, :], cor, side1, 8 * w))
    sweep(table, levels, jobs, 1.0, 1.0, 8, 4)
    jobs = []
    for w in range(1, groups - 1):
        cor = coriolis_rows(first_row + 8 * w, total)
        jobs.append((main1, side1, 8 * w + 2, depth[8 * w + 4:8 * w + 12, :], cor, last, 8 * w - 8))
    sweep(table, levels, jobs, GAIN, 1.0 / GAIN**2, 16, 8)


def south_kernel(ps, cs, main0, side0, south0, south0e):
    levels = main0.shape[1]
    has_south = lax.axis_index("lat") > 0
    corner = jnp.where(has_south, cs[...], 0.0)

    def fill(k, unused):
        edge = spread_corner(corner, 124 - 4 * k)
        for pair in range(2):
            south = jnp.where(has_south, ps[2 * k + pair], 0.0)
            for j in range(2):
                f = 2 * pair + j
                south0[f, k, 0:4, :] = south[4 * j:4 * j + 4, :]
                south0[f, k, 4:12, :] = main0[f, k, 4:12, :]
                south0e[f, k, 0:2, :] = jnp.zeros((2, 128), F32)
                south0e[f, k, 2:4, :] = edge[2 * f:2 * f + 2, :]
                south0e[f, k, 4:12, :] = side0[f, k, 4:12, :]
        return unused

    lax.fori_loop(0, levels, fill, 0, unroll=4)


def rim_kernel(ps, p1, p2, c1, c2, depth, side_depth, south0, south0e, main0, side0, main1, side1, last, out,
               south1, south1e, north0, north0e, north1, north1e, ends, table, sems):
    levels, rows = main0.shape[1], out.shape[2]
    done = pltpu.make_async_copy(last, out.at[:, :, 8:rows - 8, :], sems.at[0])
    done.start()
    band = lax.axis_index("lat")
    band_even = band % 2 == 0
    first_row = band * rows
    total = rows * lax.axis_size("lat")
    has_south = band > 0
    is_top = band == lax.axis_size("lat") - 1
    fill_table(table)
    mirror = 127 - lanes()
    flip = sublanes() ^ 3

    south_rim = jnp.where(has_south, ps[2 * levels], 0.0)
    south_depth = jnp.where(sublanes() < 2, pltpu.roll(south_rim, 6, 0), depth[2:10, :])

    def ghost(index, sign):
        far = p2[index]
        folded = jnp.take_along_axis(far, mirror, axis=1, mode="promise_in_bounds")
        folded = jnp.take_along_axis(folded, flip, axis=0, mode="promise_in_bounds") * sign
        return jnp.where(band_even, p1[index], jnp.where(is_top, folded, far))

    far = c2[...]
    folded = jnp.take_along_axis(far, mirror, axis=1, mode="promise_in_bounds")
    folded = jnp.where(sublanes() < 4, folded, -folded)
    north_corner = jnp.where(band_even, c1[...], jnp.where(is_top, folded, far))
    north_depth = jnp.where(sublanes() < 6, depth[rows - 2:rows + 6, :], pltpu.roll(ghost(2 * levels, 1.0), 6, 0))

    def fill(k, unused):
        north_edge = spread_corner(north_corner, jnp.where(is_top, 4 * k - 124, 124 - 4 * k))
        for pair in range(2):
            north = ghost(2 * k + pair, 1.0 if pair == 0 else -1.0)
            for j in range(2):
                f = 2 * pair + j
                south1[f, k, 8:12, :] = main1[f, k, 8:12, :]
                south1e[f, k, 8:12, :] = side1[f, k, 8:12, :]
                north0[f, k, 0:8, :] = main0[f, k, rows - 4:rows + 4, :]
                north0[f, k, 8:12, :] = north[4 * j:4 * j + 4, :]
                north0e[f, k, 0:8, :] = side0[f, k, rows - 4:rows + 4, :]
                north0e[f, k, 8:10, :] = north_edge[2 * f:2 * f + 2, :]
                north0e[f, k, 10:12, :] = jnp.zeros((2, 128), F32)
                north1[f, k, 0:4, :] = main1[f, k, rows - 8:rows - 4, :]
                north1e[f, k, 0:4, :] = side1[f, k, rows - 8:rows - 4, :]
        return unused

    lax.fori_loop(0, levels, fill, 0, unroll=4)
    low = coriolis_rows(first_row - 2, total)
    high = coriolis_rows(first_row + (rows - 6), total)
    sweep(table, levels, [
        (south0, south0e, 2, south_depth, low, south1, 0),
        (south0e, south0, 2, side_depth[2:10, :], low, south1e, 0),
        (north0, north0e, 2, north_depth, high, north1, 4),
        (north0e, north0, 2, side_depth[rows - 2:rows + 6, :], high, north1e, 4),
    ], 1.0, 1.0, 16, 8)
    low = coriolis_rows(first_row, total)
    high = coriolis_rows(first_row + (rows - 8), total)
    sweep(table, levels, [
        (south1, south1e, 2, depth[4:12, :], low, ends, 0),
        (north1, north1e, 2, depth[rows - 4:rows + 4, :], high, ends, 8),
    ], GAIN, 1.0 / GAIN**2, 16, 8)
    first = pltpu.make_async_copy(ends.at[:, :, 0:8, :], out.at[:, :, 0:8, :], sems.at[1])
    second = pltpu.make_async_copy(ends.at[:, :, 8:16, :], out.at[:, :, rows - 8:rows, :], sems.at[2])
    first.start()
    second.start()
    done.wait()
    first.wait()
    second.wait()


def per_device(state, land_mask, wet_levels):
    fields, levels, rows, cols = state.shape
    lon, lat = lax.axis_index("lon"), lax.axis_index("lat")
    count, bands = lax.axis_size("lon"), lax.axis_size("lat")

    def mate(i):
        return i ^ 1

    def beyond(i):
        return (i + 1) % count if i % 2 else (i - 1) % count

    def swap(x, to):
        pairs = []
        for i in range(count):
            for b in range(bands):
                ti, tb = to(i, b)
                pairs.append((i * bands + b, ti * bands + tb))
        return lax.ppermute(x, ("lon", "lat"), pairs)

    def near(i, b):
        return i, b ^ 1

    def far(i, b):
        if b == bands - 1:
            return count - 1 - i, b
        if b == 0:
            return i, b
        return i, (b + 1 if b % 2 else b - 1)

    def call(kernel, vmem, **given):
        return pl.pallas_call(kernel, compiler_params=pltpu.CompilerParams(vmem_limit_bytes=vmem * 2**20), **given)

    shape = lambda *dims: jax.ShapeDtypeStruct(dims, F32)
    block = lambda n: shape(fields, levels, n, 128)
    room = lambda n: pltpu.VMEM((fields, levels, n, 128), F32)
    edge, strip = shape(2 * levels + 1, 8, 128), shape(5, rows, 128)
    depth = jnp.where(land_mask == 1, jnp.minimum(wet_levels, levels), 0).astype(F32)
    depth = jnp.pad(depth, ((4, 4), (0, 0)))
    p1, p2, la, lb = call(
        pack_kernel,
        6,
        out_shape=(edge, edge, strip, strip),
        in_specs=[VM] * 2,
        out_specs=(VM,) * 4,
        name="pack",
    )(state, depth)
    rp2 = swap(p2, far)
    rb = swap(lb, lambda i, b: (beyond(i), b))
    ra = swap(la, lambda i, b: (mate(i), b))
    rp1 = swap(p1, near)

    lon_even = lon & 1 == 0
    band_even = lat & 1 == 0
    lane = jnp.arange(128, dtype=jnp.int32)
    ends = lambda x: (x[:4, 0:2], x[:4, rows - 2:rows])
    (a_low, a_high), (b_low, b_high) = ends(ra), ends(rb)
    from_east = (lane % 4 < 2) == lon_even
    low = jnp.where(from_east, a_low, b_low)
    high = jnp.where(from_east, a_high, b_high)
    back = jnp.where(lat == bands - 1, high[:, ::-1], high)
    rc1 = swap(jnp.where(band_even, high, low).reshape(8, 128), near)
    rc2 = swap(jnp.where(band_even, low, back).reshape(8, 128), far)

    if bands == 2:
        south, south_corner = rp1, rc1
    else:
        south = jnp.where(band_even, rp2, rp1)
        south_corner = jnp.where(band_even, rc2, rc1)

    room_table = pltpu.SMEM((2, levels), F32)
    main0, side0, side1, main1, side_depth, last = call(
        inner_kernel,
        6,
        out_shape=(block(rows + 8), block(rows + 8), block(rows + 4), block(rows + 4), shape(rows + 8, 128),
                   block(rows - 16)),
        in_specs=[VM] * 4,
        out_specs=(VM,) * 6,
        scratch_shapes=[pltpu.VMEM((5, rows, 128), F32), pltpu.VMEM((5, rows, 128), F32), room_table],
        name="inner",
    )(state, depth, ra, rb)
    south0, south0e = call(
        south_kernel,
        4,
        out_shape=(block(16), block(16)),
        in_specs=[VM] * 4,
        out_specs=(VM,) * 2,
        name="south",
    )(south, south_corner, main0, side0)
    return call(
        rim_kernel,
        14,
        out_shape=shape(*state.shape),
        in_specs=[VM] * 14,
        out_specs=HB,
        scratch_shapes=[room(16)] * 7 + [room_table, pltpu.SemaphoreType.DMA((3,))],
        name="rim",
    )(south, rp1, rp2, rc1, rc2, depth, side_depth, south0, south0e, main0, side0, main1, side1, last)


def solution(mesh):
    placed = (P(None, None, "lat", "lon"), P("lat", "lon"), P("lat", "lon"))
    return jax.shard_map(
        per_device,
        mesh=mesh,
        in_specs=placed,
        out_specs=P(None, None, "lat", "lon"),
        check_vma=False,
    )
```

time: 40.8 us -> 30.7 us (0.75)
  Pallas kernels: 22.8 us -> 14.3 us
  local copies, waits for them, and re-layouts: 3.73 us -> 1.62 us
  other arithmetic: 0.1 us -> 0.77 us
    pallas_call x4, Pallas kernels: 22.8 us -> 14.3 us  [the longest x1 6.37 us: per_device(): call(inner_kernel, 6, out_shape=(block(rows + 8), block(rows + 8), block(...]
    unnamed x8 -> x4, local copies, waits for them, and re-layouts: 3.7 us -> 1.59 us
    convert_element_type x0 -> x1, other arithmetic: none -> 0.74 us  [per_device(): jnp.where(land_mask == 1, jnp.minimum(wet_levels, levels), 0).astype(F32)]
  transfers between devices with their start and end apart: 6 -> 6, of which waited for: 0 -> 0; matrix products, arithmetic and copies ran while one was open for 0% -> 0% of each run, Pallas kernels for 37% -> 23%
where the time goes in v2:
time: 30.7 us; the launch traced here: 30.3 us
  Pallas kernels  14.3 us (47%)
  starting transfers between devices  13.5 us (44%)
  local copies, waits for them, and re-layouts  1.62 us (5%)
  other arithmetic  0.77 us (3%)
    ppermute x6, starting transfers between devices, swap(): return lax.ppermute(x, ('lon', 'lat'), pairs)  13.5 us
    pallas_call x1, Pallas kernels, per_device(): call(inner_kernel, 6, out_shape=(block(rows + 8), block(rows + 8), block(...  6.37 us
    pallas_call x1, Pallas kernels, per_device(): call(rim_kernel, 14, out_shape=shape(*state.shape), in_specs=[VM] * 14, o...  6.08 us
    unnamed x4, local copies, waits for them, and re-layouts  1.59 us
    pallas_call x1, Pallas kernels, per_device(): call(pack_kernel, 6, out_shape=(edge, edge, strip, strip), in_specs=[VM]...  1.16 us
    convert_element_type x1, other arithmetic, per_device(): jnp.where(land_mask == 1, jnp.minimum(wet_levels, levels), 0).astype(F32)  0.74 us
    pallas_call x1, Pallas kernels, per_device(): call(south_kernel, 4, out_shape=(block(16), block(16)), in_specs=[VM] * 4...  0.67 us
  transfers between devices with their start and end apart: 6, of which 0 were waited for; matrix products, arithmetic and copies ran while one was open for 0% of the time, Pallas kernels for 23%

profile of v2, /device:TPU:2, one launch (start us, length us, event | category | flops | bytes accessed | tf_op | source)
XLA Modules:
  0.0 30.3 jit_solution(12693114651494988533)
XLA Ops:
  0.0 0.7 %select_convert_fusion = f32[32,128]{1,0:T(8,128)S(1)} fusion(s32[32,128]{1,0:T(8,128)} %param.5, s32[32,128]{1,0:T(8,128)} %param.4), kind=kLoop, calls=%fused_computation | loop fusion | flops 16384 | bytes 49152 | tf_op jit(solution)/shard_map/convert_element_type | solution.py:364
  0.7 0.0 copy-start
  0.8 1.6 %copy-done = f32[4,32,32,128]{3,2,1,0:T(8,128)S(1)} copy-done((f32[4,32,32,128]{3,2,1,0:T(8,128)S(1)}, f32[4,32,32,128]{3,2,1,0:T(8,128)}, u32[]{:S(2)}) %copy-start) | copy-done | bytes 2097176
  2.3 0.0 copy-start.1
  2.3 1.2 %pack.1 = (f32[65,8,128]{2,1,0:T(8,128)S(1)}, f32[65,8,128]{2,1,0:T(8,128)S(1)}, f32[5,32,128]{2,1,0:T(8,128)S(1)}, f32[5,32,128]{2,1,0:T(8,128)S(1)}) custom-call(f32[4,32,32,128]{3,2,1,0:T(8,128)S(1)} %copy-done, f32[40,128]{1,0:T(8,128)S(1)} %pad.4.depth), custom_call_target="tpu_custom_call" | custom-call | tf_op jit(solution)/shard_map/pack/pallas_call | solution.py:366
  3.5 0.0 collective-permute-start.2
  3.5 4.7 %collective-permute-start.3 = (f32[5,32,128]{2,1,0:T(8,128)S(1)}, f32[5,32,128]{2,1,0:T(8,128)S(1)}, u32[]{:S(2)}, u32[]{:S(2)}) collective-permute-start(f32[5,32,128]{2,1,0:T(8,128)S(1)} %get-tuple-element.20), channel_id=1, source_target_pairs={{0,30},{1,31},{2,4},{3,5},{4,2},{5,3},{6,8},{7,9},{8,6},{9,7},{10,... | collective-permute-start | bytes 245768 | tf_op jit(solution)/shard_map/ppermute | solution.py:345
  8.2 0.5 %collective-permute-start = (f32[65,8,128]{2,1,0:T(8,128)S(1)}, f32[65,8,128]{2,1,0:T(8,128)S(1)}, u32[]{:S(2)}, u32[]{:S(2)}) collective-permute-start(f32[65,8,128]{2,1,0:T(8,128)S(1)} %get-tuple-element.17), channel_id=1, source_target_pairs={{0,1},{1,0},{2,3},{3,2},{4,5},{5,4},{6,7},{7,6},{8,9},{9,8},{10,11... | collective-permute-start | bytes 798728 | tf_op jit(solution)/shard_map/ppermute | solution.py:345
  8.7 1.9 %collective-permute-start.1 = (f32[65,8,128]{2,1,0:T(8,128)S(1)}, f32[65,8,128]{2,1,0:T(8,128)S(1)}, u32[]{:S(2)}, u32[]{:S(2)}) collective-permute-start(f32[65,8,128]{2,1,0:T(8,128)S(1)} %get-tuple-element.18), channel_id=1, source_target_pairs={{0,0},{1,31},{2,2},{3,29},{4,4},{5,27},{6,6},{7,25},{8,8},{9,23},{... | collective-permute-start | bytes 798728 | tf_op jit(solution)/shard_map/ppermute | solution.py:345
  10.7 0.0 collective-permute-done.2.ra
  10.7 0.0 collective-permute-done.3.rb
  10.7 0.3 %collective-permute-start.4 = (f32[8,128]{1,0:T(8,128)S(1)}, f32[8,128]{1,0:T(8,128)S(1)}, u32[]{:S(2)}, u32[]{:S(2)}) collective-permute-start(f32[8,128]{1,0:T(8,128)S(1)} %bitcast.2), channel_id=1, source_target_pairs={{0,1},{1,0},{2,3},{3,2},{4,5},{5,4},{6,7},{7,6},{8,9},{9,8},{10,11... | collective-permute-start | bytes 12296 | tf_op jit(solution)/shard_map/ppermute | solution.py:345
  11.1 6.1 %collective-permute-start.5 = (f32[8,128]{1,0:T(8,128)S(1)}, f32[8,128]{1,0:T(8,128)S(1)}, u32[]{:S(2)}, u32[]{:S(2)}) collective-permute-start(f32[8,128]{1,0:T(8,128)S(1)} %bitcast.3), channel_id=1, source_target_pairs={{0,0},{1,31},{2,2},{3,29},{4,4},{5,27},{6,6},{7,25},{8,8},{9,23},{... | collective-permute-start | bytes 12296 | tf_op jit(solution)/shard_map/ppermute | solution.py:345
  17.2 0.0 copy-done.1
  17.2 6.4 %inner.1 = (f32[4,32,40,128]{3,2,1,0:T(8,128)S(1)}, f32[4,32,40,128]{3,2,1,0:T(8,128)S(1)}, f32[4,32,36,128]{3,2,1,0:T(8,128)S(1)}, f32[4,32,36,128]{3,2,1,0:T(8...) custom-call(f32[4,32,32,128]{3,2,1,0:T(8,128)S(1)} %copy-done.1, f32[40,128]{1,0:T(8,128)S(1)} %pad.4.depth, ...), custom_call_target="tpu_custom_call" | custom-call | tf_op jit(solution)/shard_map/inner/pallas_call | solution.py:398
  23.6 0.0 collective-permute-done.4.cs.c1
  23.6 0.0 collective-permute-done.ps.p1
  23.6 0.7 %south.1 = (f32[4,32,16,128]{3,2,1,0:T(8,128)S(1)}, f32[4,32,16,128]{3,2,1,0:T(8,128)S(1)}) custom-call(f32[65,8,128]{2,1,0:T(8,128)S(1)} %collective-permute-done.ps.p1, f32[8,128]{1,0:T(8,128)S(1)} %collective-permute-done.4.cs.c1, f32[4,32,40,128]{3,2,1,0:T(8,128)S(1)} %get-tuple-element.22.main0, f32[4,32,40,128]{3,2,1,0:T(8,128)S(1)} %get-tuple-element.23.side0), custom_call_target="tpu_custom_call" | custom-call | tf_op jit(solution)/shard_map/south/pallas_call | solution.py:408
  24.3 0.0 collective-permute-done.5.c2
  24.3 0.0 collective-permute-done.1.p2
  24.3 6.1 %rim.1 = f32[4,32,32,128]{3,2,1,0:T(8,128)} custom-call(f32[65,8,128]{2,1,0:T(8,128)S(1)} %collective-permute-done.ps.p1, f32[65,8,128]{2,1,0:T(8,128)S(1)} %collective-permute-done.ps.p1, f32[65,8,128]{2,1,0:T(8,128)S(1)} %collective-permute-done.1.p2, f32[8,128]{1,0:T(8,128)S(1)} %collective-permute-done.4.cs.c1, f32[8,128]{1,0:T(8,128)S(1)} %collective-permute-done.5.c2, ...), custom_call_target="tpu_custom_call" | custom-call | tf_op jit(solution)/shard_map/rim/pallas_call | solution.py:416
  (5 shorter events, 0.1 us)
Async XLA Ops:
  0.7 1.6 %copy-start = (f32[4,32,32,128]{3,2,1,0:T(8,128)S(1)}, f32[4,32,32,128]{3,2,1,0:T(8,128)}, u32[]{:S(2)}) copy-start(f32[4,32,32,128]{3,2,1,0:T(8,128)} %state.3) | copy-start | bytes 6291460
  2.3 14.8 %copy-start.1 = (f32[4,32,32,128]{3,2,1,0:T(8,128)S(1)}, f32[4,32,32,128]{3,2,1,0:T(8,128)}, u32[]{:S(2)}) copy-start(f32[4,32,32,128]{3,2,1,0:T(8,128)} %state.3) | copy-start | bytes 6291460
  3.5 7.2 %collective-permute-start.2 = (f32[5,32,128]{2,1,0:T(8,128)S(1)}, f32[5,32,128]{2,1,0:T(8,128)S(1)}, u32[]{:S(2)}, u32[]{:S(2)}) collective-permute-start(f32[5,32,128]{2,1,0:T(8,128)S(1)} %get-tuple-element.19), channel_id=1, source_target_pairs={{0,2},{1,3},{2,0},{3,1},{4,6},{5,7},{6,4},{7,5},{8,10},{9,11},{10,... | collective-permute-start | bytes 245768 | tf_op jit(solution)/shard_map/ppermute | solution.py:345
  3.5 7.1 %collective-permute-start.3 = (f32[5,32,128]{2,1,0:T(8,128)S(1)}, f32[5,32,128]{2,1,0:T(8,128)S(1)}, u32[]{:S(2)}, u32[]{:S(2)}) collective-permute-start(f32[5,32,128]{2,1,0:T(8,128)S(1)} %get-tuple-element.20), channel_id=1, source_target_pairs={{0,30},{1,31},{2,4},{3,5},{4,2},{5,3},{6,8},{7,9},{8,6},{9,7},{10,... | collective-permute-start | bytes 245768 | tf_op jit(solution)/shard_map/ppermute | solution.py:345
  8.2 15.4 %collective-permute-start = (f32[65,8,128]{2,1,0:T(8,128)S(1)}, f32[65,8,128]{2,1,0:T(8,128)S(1)}, u32[]{:S(2)}, u32[]{:S(2)}) collective-permute-start(f32[65,8,128]{2,1,0:T(8,128)S(1)} %get-tuple-element.17), channel_id=1, source_target_pairs={{0,1},{1,0},{2,3},{3,2},{4,5},{5,4},{6,7},{7,6},{8,9},{9,8},{10,11... | collective-permute-start | bytes 798728 | tf_op jit(solution)/shard_map/ppermute | solution.py:345
  8.7 15.5 %collective-permute-start.1 = (f32[65,8,128]{2,1,0:T(8,128)S(1)}, f32[65,8,128]{2,1,0:T(8,128)S(1)}, u32[]{:S(2)}, u32[]{:S(2)}) collective-permute-start(f32[65,8,128]{2,1,0:T(8,128)S(1)} %get-tuple-element.18), channel_id=1, source_target_pairs={{0,0},{1,31},{2,2},{3,29},{4,4},{5,27},{6,6},{7,25},{8,8},{9,23},{... | collective-permute-start | bytes 798728 | tf_op jit(solution)/shard_map/ppermute | solution.py:345
  10.7 12.8 %collective-permute-start.4 = (f32[8,128]{1,0:T(8,128)S(1)}, f32[8,128]{1,0:T(8,128)S(1)}, u32[]{:S(2)}, u32[]{:S(2)}) collective-permute-start(f32[8,128]{1,0:T(8,128)S(1)} %bitcast.2), channel_id=1, source_target_pairs={{0,1},{1,0},{2,3},{3,2},{4,5},{5,4},{6,7},{7,6},{8,9},{9,8},{10,11... | collective-permute-start | bytes 12296 | tf_op jit(solution)/shard_map/ppermute | solution.py:345
  11.1 13.2 %collective-permute-start.5 = (f32[8,128]{1,0:T(8,128)S(1)}, f32[8,128]{1,0:T(8,128)S(1)}, u32[]{:S(2)}, u32[]{:S(2)}) collective-permute-start(f32[8,128]{1,0:T(8,128)S(1)} %bitcast.3), channel_id=1, source_target_pairs={{0,0},{1,31},{2,2},{3,29},{4,4},{5,27},{6,6},{7,25},{8,8},{9,23},{... | collective-permute-start | bytes 12296 | tf_op jit(solution)/shard_map/ppermute | solution.py:345

commit v3 on v2

--- a/solution.py
+++ b/solution.py
@@ -53,41 +53,92 @@
     return lax.broadcasted_iota(jnp.int32, (8, 128), 0)
 
 
-def pack_kernel(state, depth, p1, p2, la, lb):
+def edge_rows(strip, f, r):
+    rows = strip.shape[1]
+    band = lax.axis_index("lat")
+    band_even = band % 2 == 0
+    is_top = band == lax.axis_size("lat") - 1
+    south, north = strip[f, r:r + 1, :], strip[f, rows - 2 + r:rows - 1 + r, :]
+    folded = strip[f, rows - 1 - r:rows - r, :]
+    return jnp.where(band_even, north, south), jnp.where(band_even, south, jnp.where(is_top, folded, north))
+
+
+def row_tiles(state, k, deep_s, deep_n, pair):
+    rows = state.shape[2]
+    level = k.astype(F32)
+    tiles = []
+    for f in (2 * pair, 2 * pair + 1):
+        tiles.append(jnp.where(level < deep_s, state[f, k, 0:8, :], 0.0))
+        tiles.append(jnp.where(level < deep_n, state[f, k, rows - 8:rows, :], 0.0))
+    return join_rows(*tiles)
+
+
+def join_rows(a_s, a_n, b_s, b_n):
+    band_even = lax.axis_index("lat") % 2 == 0
+    low = sublanes() < 4
+    north = jnp.where(low, pltpu.roll(a_n, 4, 0), b_n)
+    south = jnp.where(low, a_s, pltpu.roll(b_s, 4, 0))
+    return jnp.where(band_even, north, south), jnp.where(band_even, south, north)
+
+
+def far_kernel(state, depth, ra, p2):
+    levels, rows = state.shape[1], state.shape[2]
+    deep_s, deep_n = depth[4:12, :], depth[rows - 4:rows + 4, :]
+
+    def body(k, unused):
+        for pair in range(2):
+            p2[2 * k + pair] = row_tiles(state, k, deep_s, deep_n, pair)[1]
+        return unused
+
+    lax.fori_loop(0, levels, body, 0, unroll=8)
+    p2[2 * levels] = join_rows(deep_s, deep_n, deep_s, deep_n)[1]
+    for f in range(4):
+        for r in range(2):
+            p2[2 * levels + 1, 2 * f + r:2 * f + r + 1, :] = edge_rows(ra, f, r)[1]
+    for n in range(2 * levels + 2, p2.shape[0]):
+        p2[n] = jnp.zeros((8, 128), F32)
+
+
+def near_kernel(state, depth, ra, rb, p1):
+    levels, rows = state.shape[1], state.shape[2]
+    deep_s, deep_n = depth[4:12, :], depth[rows - 4:rows + 4, :]
+    from_a = ((lanes()[0:1] & 3) < 2) == (lax.axis_index("lon") % 2 == 0)
+
+    def body(k, unused):
+        for pair in range(2):
+            p1[2 * k + pair] = row_tiles(state, k, deep_s, deep_n, pair)[0]
+        return unused
+
+    lax.fori_loop(0, levels, body, 0, unroll=8)
+    p1[2 * levels] = join_rows(deep_s, deep_n, deep_s, deep_n)[0]
+    for f in range(4):
+        for r in range(2):
+            row = jnp.where(from_a, edge_rows(ra, f, r)[0], edge_rows(rb, f, r)[0])
+            p1[2 * levels + 1, 2 * f + r:2 * f + r + 1, :] = row
+
+
+def columns_kernel(state, depth, la, lb, cb):
     levels, rows = state.shape[1], state.shape[2]
     groups = rows // 8
     lon_even = lax.axis_index("lon") % 2 == 0
-    band_even = lax.axis_index("lat") % 2 == 0
     zero = jnp.zeros((8, 128), F32)
     deeps = [depth[8 * g + 4:8 * g + 12, :] for g in range(groups)]
     group = lanes() >> 2
-    low = sublanes() < 4
-
-    def edges(a0, a3, b0, b3):
-        north = jnp.where(low, pltpu.roll(a3, 4, 0), b3)
-        south = jnp.where(low, a0, pltpu.roll(b0, 4, 0))
-        return jnp.where(band_even, north, south), jnp.where(band_even, south, north)
-
     for pair in range(2):
         def body(k, accs):
             level = k.astype(F32)
             spot_e = group == k
             spot_w = group == ((k + 1) & (levels - 1))
-            tiles = []
             new = []
             for j in range(2):
                 for g in range(groups):
                     q = jnp.where(level < deeps[g], state[2 * pair + j, k, 8 * g:8 * g + 8, :], 0.0)
-                    tiles.append(q)
                     turned = pltpu.roll(q, (4 * k + 4) & 127, 1)
                     new.append(jnp.where(spot_e, turned, accs[len(new)]))
                     new.append(jnp.where(spot_w, turned, accs[len(new)]))
-            first, second = edges(tiles[0], tiles[groups - 1], tiles[groups], tiles[2 * groups - 1])
-            p1[2 * k + pair] = first
-            p2[2 * k + pair] = second
             return tuple(new)
 
-        accs = lax.fori_loop(0, levels, body, (zero,) * (4 * groups), unroll=8)
+        accs = lax.fori_loop(0, levels, body, (zero,) * (4 * groups), unroll=16)
         for j in range(2):
             for g in range(groups):
                 at = slice(8 * g, 8 * g + 8)
@@ -98,9 +149,9 @@
         turned = pltpu.roll(deeps[g], 4, 1)
         la[4, 8 * g:8 * g + 8, :] = turned
         lb[4, 8 * g:8 * g + 8, :] = turned
-    first, second = edges(deeps[0], deeps[-1], deeps[0], deeps[-1])
-    p1[2 * levels] = first
-    p2[2 * levels] = second
+    for f in range(4):
+        for r in range(2):
+            cb[2 * f + r:2 * f + r + 1, :] = edge_rows(lb, f, r)[1]
 
 
 def coriolis_rows(first, total):
@@ -180,10 +231,6 @@
     return pltpu.roll(jnp.where(group == k, west, east), (124 - 4 * k) & 127, 1)
 
 
-def spread_corner(corner, shift):
-    return pltpu.roll(corner, shift & 127, 1)
-
-
 def inner_kernel(state, depth, ra, rb, main0, side0, side1, main1, side_depth, last, easts, wests, table):
     levels, rows = state.shape[1], state.shape[2]
     groups = rows // 8
@@ -217,7 +264,7 @@
                 side0[f, k, to, :] = side_tile(easts[f, at, :], wests[f, at, :], group, k)
         return unused
 
-    lax.fori_loop(0, levels, fill, 0, unroll=8)
+    lax.fori_loop(0, levels, fill, 0, unroll=16)
 
     jobs = []
     for w in range(1, groups):
@@ -225,7 +272,7 @@
         cor = coriolis_rows(first_row + (8 * w - 2), total)
         jobs.append((main0, side0, o, depth[o:o + 8, :], cor, main1, 8 * w))
         jobs.append((side0, main0, o, side_depth[o:o + 8, :], cor, side1, 8 * w))
-    sweep(table, levels, jobs, 1.0, 1.0, 8, 4)
+    sweep(table, levels, jobs, 1.0, 1.0, 16, 8)
     jobs = []
     for w in range(1, groups - 1):
         cor = coriolis_rows(first_row + 8 * w, total)
@@ -233,96 +280,102 @@
     sweep(table, levels, jobs, GAIN, 1.0 / GAIN**2, 16, 8)
 
 
-def south_kernel(ps, cs, main0, side0, south0, south0e):
+def south_kernel(p, depth, side_depth, main0, side0, main1, side1, last, rim0, edge0, rim1, edge1, table):
     levels = main0.shape[1]
+    rows = depth.shape[0] - 8
+    first_row = lax.axis_index("lat") * rows
+    total = rows * lax.axis_size("lat")
     has_south = lax.axis_index("lat") > 0
-    corner = jnp.where(has_south, cs[...], 0.0)
+    fill_table(table)
+    corner = jnp.where(has_south, p[2 * levels + 1], 0.0)
+    rim_depth = jnp.where(has_south, p[2 * levels], 0.0)
+    depths = jnp.where(sublanes() < 2, pltpu.roll(rim_depth, 6, 0), depth[2:10, :])
 
     def fill(k, unused):
-        edge = spread_corner(corner, 124 - 4 * k)
+        corners = pltpu.roll(corner, (124 - 4 * k) & 127, 1)
         for pair in range(2):
-            south = jnp.where(has_south, ps[2 * k + pair], 0.0)
+            rim = jnp.where(has_south, p[2 * k + pair], 0.0)
             for j in range(2):
                 f = 2 * pair + j
-                south0[f, k, 0:4, :] = south[4 * j:4 * j + 4, :]
-                south0[f, k, 4:12, :] = main0[f, k, 4:12, :]
-                south0e[f, k, 0:2, :] = jnp.zeros((2, 128), F32)
-                south0e[f, k, 2:4, :] = edge[2 * f:2 * f + 2, :]
-                south0e[f, k, 4:12, :] = side0[f, k, 4:12, :]
+                rim0[f, k, 0:4, :] = rim[4 * j:4 * j + 4, :]
+                rim0[f, k, 4:12, :] = main0[f, k, 4:12, :]
+                edge0[f, k, 0:2, :] = jnp.zeros((2, 128), F32)
+                edge0[f, k, 2:4, :] = corners[2 * f:2 * f + 2, :]
+                edge0[f, k, 4:12, :] = side0[f, k, 4:12, :]
+                rim1[f, k, 8:12, :] = main1[f, k, 8:12, :]
+                edge1[f, k, 8:12, :] = side1[f, k, 8:12, :]
         return unused
 
-    lax.fori_loop(0, levels, fill, 0, unroll=4)
-
-
-def rim_kernel(ps, p1, p2, c1, c2, depth, side_depth, south0, south0e, main0, side0, main1, side1, last, out,
-               south1, south1e, north0, north0e, north1, north1e, ends, table, sems):
+    lax.fori_loop(0, levels, fill, 0, unroll=8)
+    cor = coriolis_rows(first_row - 2, total)
+    sweep(table, levels, [
+        (rim0, edge0, 2, depths, cor, rim1, 0),
+        (edge0, rim0, 2, side_depth[2:10, :], cor, edge1, 0),
+    ], 1.0, 1.0, 16, 8)
+    cor = coriolis_rows(first_row, total)
+    sweep(table, levels, [(rim1, edge1, 2, depth[4:12, :], cor, last, 0)], GAIN, 1.0 / GAIN**2, 16, 8)
+
+
+def north_kernel(p1, p2, cb, depth, side_depth, main0, side0, main1, side1, middle, south, out,
+                 rim0, edge0, rim1, edge1, last, table, sems):
     levels, rows = main0.shape[1], out.shape[2]
-    done = pltpu.make_async_copy(last, out.at[:, :, 8:rows - 8, :], sems.at[0])
-    done.start()
+    done = [
+        pltpu.make_async_copy(middle, out.at[:, :, 8:rows - 8, :], sems.at[0]),
+        pltpu.make_async_copy(south, out.at[:, :, 0:8, :], sems.at[1]),
+    ]
+    for copy in done:
+        copy.start()
     band = lax.axis_index("lat")
     band_even = band % 2 == 0
     first_row = band * rows
     total = rows * lax.axis_size("lat")
-    has_south = band > 0
     is_top = band == lax.axis_size("lat") - 1
     fill_table(table)
     mirror = 127 - lanes()
     flip = sublanes() ^ 3
 
-    south_rim = jnp.where(has_south, ps[2 * levels], 0.0)
-    south_depth = jnp.where(sublanes() < 2, pltpu.roll(south_rim, 6, 0), depth[2:10, :])
+    def folded(tile):
+        return jnp.take_along_axis(tile, mirror, axis=1, mode="promise_in_bounds")
 
     def ghost(index, sign):
         far = p2[index]
-        folded = jnp.take_along_axis(far, mirror, axis=1, mode="promise_in_bounds")
-        folded = jnp.take_along_axis(folded, flip, axis=0, mode="promise_in_bounds") * sign
-        return jnp.where(band_even, p1[index], jnp.where(is_top, folded, far))
-
-    far = c2[...]
-    folded = jnp.take_along_axis(far, mirror, axis=1, mode="promise_in_bounds")
-    folded = jnp.where(sublanes() < 4, folded, -folded)
-    north_corner = jnp.where(band_even, c1[...], jnp.where(is_top, folded, far))
-    north_depth = jnp.where(sublanes() < 6, depth[rows - 2:rows + 6, :], pltpu.roll(ghost(2 * levels, 1.0), 6, 0))
+        turned = jnp.take_along_axis(folded(far), flip, axis=0, mode="promise_in_bounds") * sign
+        return jnp.where(band_even, p1[index], jnp.where(is_top, turned, far))
+
+    sender_even = (lax.axis_index("lon") % 2 == 0) != is_top
+    far = jnp.where(((lanes() & 3) < 2) == sender_even, p2[2 * levels + 1], cb[...])
+    turned = jnp.where(sublanes() < 4, folded(far), -folded(far))
+    corner = jnp.where(band_even, p1[2 * levels + 1], jnp.where(is_top, turned, far))
+    depths = jnp.where(sublanes() < 6, depth[rows - 2:rows + 6, :], pltpu.roll(ghost(2 * levels, 1.0), 6, 0))
 
     def fill(k, unused):
-        north_edge = spread_corner(north_corner, jnp.where(is_top, 4 * k - 124, 124 - 4 * k))
+        corners = pltpu.roll(corner, jnp.where(is_top, 4 * k - 124, 124 - 4 * k) & 127, 1)
         for pair in range(2):
-            north = ghost(2 * k + pair, 1.0 if pair == 0 else -1.0)
+            rim = ghost(2 * k + pair, 1.0 if pair == 0 else -1.0)
             for j in range(2):
                 f = 2 * pair + j
-                south1[f, k, 8:12, :] = main1[f, k, 8:12, :]
-                south1e[f, k, 8:12, :] = side1[f, k, 8:12, :]
-                north0[f, k, 0:8, :] = main0[f, k, rows - 4:rows + 4, :]
-                north0[f, k, 8:12, :] = north[4 * j:4 * j + 4, :]
-                north0e[f, k, 0:8, :] = side0[f, k, rows - 4:rows + 4, :]
-                north0e[f, k, 8:10, :] = north_edge[2 * f:2 * f + 2, :]
-                north0e[f, k, 10:12, :] = jnp.zeros((2, 128), F32)
-                north1[f, k, 0:4, :] = main1[f, k, rows - 8:rows - 4, :]
-                north1e[f, k, 0:4, :] = side1[f, k, rows - 8:rows - 4, :]
+                rim0[f, k, 0:8, :] = main0[f, k, rows - 4:rows + 4, :]
+                rim0[f, k, 8:12, :] = rim[4 * j:4 * j + 4, :]
+                edge0[f, k, 0:8, :] = side0[f, k, rows - 4:rows + 4, :]
+                edge0[f, k, 8:10, :] = corners[2 * f:2 * f + 2, :]
+                edge0[f, k, 10:12, :] = jnp.zeros((2, 128), F32)
+                rim1[f, k, 0:4, :] = main1[f, k, rows - 8:rows - 4, :]
+                edge1[f, k, 0:4, :] = side1[f, k, rows - 8:rows - 4, :]
         return unused
 
-    lax.fori_loop(0, levels, fill, 0, unroll=4)
-    low = coriolis_rows(first_row - 2, total)
-    high = coriolis_rows(first_row + (rows - 6), total)
+    lax.fori_loop(0, levels, fill, 0, unroll=8)
+    cor = coriolis_rows(first_row + (rows - 6), total)
     sweep(table, levels, [
-        (south0, south0e, 2, south_depth, low, south1, 0),
-        (south0e, south0, 2, side_depth[2:10, :], low, south1e, 0),
-        (north0, north0e, 2, north_depth, high, north1, 4),
-        (north0e, north0, 2, side_depth[rows - 2:rows + 6, :], high, north1e, 4),
+        (rim0, edge0, 2, depths, cor, rim1, 4),
+        (edge0, rim0, 2, side_depth[rows - 2:rows + 6, :], cor, edge1, 4),
     ], 1.0, 1.0, 16, 8)
-    low = coriolis_rows(first_row, total)
-    high = coriolis_rows(first_row + (rows - 8), total)
-    sweep(table, levels, [
-        (south1, south1e, 2, depth[4:12, :], low, ends, 0),
-        (north1, north1e, 2, depth[rows - 4:rows + 4, :], high, ends, 8),
-    ], GAIN, 1.0 / GAIN**2, 16, 8)
-    first = pltpu.make_async_copy(ends.at[:, :, 0:8, :], out.at[:, :, 0:8, :], sems.at[1])
-    second = pltpu.make_async_copy(ends.at[:, :, 8:16, :], out.at[:, :, rows - 8:rows, :], sems.at[2])
-    first.start()
-    second.start()
-    done.wait()
-    first.wait()
-    second.wait()
+    cor = coriolis_rows(first_row + (rows - 8), total)
+    sweep(table, levels, [(rim1, edge1, 2, depth[rows - 4:rows + 4, :], cor, last, 0)], GAIN, 1.0 / GAIN**2, 16, 8)
+    copy = pltpu.make_async_copy(last, out.at[:, :, rows - 8:rows, :], sems.at[2])
+    copy.start()
+    for other in done:
+        other.wait()
+    copy.wait()
 
 
 def per_device(state, land_mask, wet_levels):
@@ -360,39 +413,28 @@
     shape = lambda *dims: jax.ShapeDtypeStruct(dims, F32)
     block = lambda n: shape(fields, levels, n, 128)
     room = lambda n: pltpu.VMEM((fields, levels, n, 128), F32)
-    edge, strip = shape(2 * levels + 1, 8, 128), shape(5, rows, 128)
+    strip = shape(5, rows, 128)
     depth = jnp.where(land_mask == 1, jnp.minimum(wet_levels, levels), 0).astype(F32)
     depth = jnp.pad(depth, ((4, 4), (0, 0)))
-    p1, p2, la, lb = call(
-        pack_kernel,
-        6,
-        out_shape=(edge, edge, strip, strip),
-        in_specs=[VM] * 2,
-        out_specs=(VM,) * 4,
-        name="pack",
+    la, lb, cb = call(
+        columns_kernel, 4, out_shape=(strip, strip, shape(8, 128)), in_specs=[VM] * 2, out_specs=(VM,) * 3,
+        name="columns",
     )(state, depth)
+    ra = swap(la, lambda i, b: (mate(i), b))
+    rb = swap(lb, lambda i, b: (beyond(i), b))
+    rcb = swap(cb, lambda i, b: far(i if b == 0 else beyond(i), b))
+    p2 = call(
+        far_kernel, 4, out_shape=shape(2 * levels + 4, 8, 128), in_specs=[VM] * 3, out_specs=VM, name="far",
+    )(state, depth, ra)
     rp2 = swap(p2, far)
-    rb = swap(lb, lambda i, b: (beyond(i), b))
-    ra = swap(la, lambda i, b: (mate(i), b))
+    p1 = call(
+        near_kernel, 4, out_shape=shape(2 * levels + 2, 8, 128), in_specs=[VM] * 4, out_specs=VM, name="near",
+    )(state, depth, ra, rb)
     rp1 = swap(p1, near)
-
-    lon_even = lon & 1 == 0
-    band_even = lat & 1 == 0
-    lane = jnp.arange(128, dtype=jnp.int32)
-    ends = lambda x: (x[:4, 0:2], x[:4, rows - 2:rows])
-    (a_low, a_high), (b_low, b_high) = ends(ra), ends(rb)
-    from_east = (lane % 4 < 2) == lon_even
-    low = jnp.where(from_east, a_low, b_low)
-    high = jnp.where(from_east, a_high, b_high)
-    back = jnp.where(lat == bands - 1, high[:, ::-1], high)
-    rc1 = swap(jnp.where(band_even, high, low).reshape(8, 128), near)
-    rc2 = swap(jnp.where(band_even, low, back).reshape(8, 128), far)
-
-    if bands == 2:
-        south, south_corner = rp1, rc1
-    else:
-        south = jnp.where(band_even, rp2, rp1)
-        south_corner = jnp.where(band_even, rc2, rc1)
+    south = rp1
+    if bands > 2:
+        same = jnp.where((jnp.arange(128) % 4 < 2) == (lon % 2 == 0), rp2[2 * levels + 1], rcb)
+        south = jnp.where(lat % 2 == 0, rp2[:2 * levels + 2].at[2 * levels + 1].set(same), rp1)
 
     room_table = pltpu.SMEM((2, levels), F32)
     main0, side0, side1, main1, side_depth, last = call(
@@ -405,23 +447,24 @@
         scratch_shapes=[pltpu.VMEM((5, rows, 128), F32), pltpu.VMEM((5, rows, 128), F32), room_table],
         name="inner",
     )(state, depth, ra, rb)
-    south0, south0e = call(
+    first = call(
         south_kernel,
-        4,
-        out_shape=(block(16), block(16)),
-        in_specs=[VM] * 4,
-        out_specs=(VM,) * 2,
+        10,
+        out_shape=block(8),
+        in_specs=[VM] * 7,
+        out_specs=VM,
+        scratch_shapes=[room(16)] * 4 + [room_table],
         name="south",
-    )(south, south_corner, main0, side0)
+    )(south, depth, side_depth, main0, side0, main1, side1)
     return call(
-        rim_kernel,
-        14,
+        north_kernel,
+        12,
         out_shape=shape(*state.shape),
-        in_specs=[VM] * 14,
+        in_specs=[VM] * 11,
         out_specs=HB,
-        scratch_shapes=[room(16)] * 7 + [room_table, pltpu.SemaphoreType.DMA((3,))],
-        name="rim",
-    )(south, rp1, rp2, rc1, rc2, depth, side_depth, south0, south0e, main0, side0, main1, side1, last)
+        scratch_shapes=[room(16)] * 4 + [room(8), room_table, pltpu.SemaphoreType.DMA((3,))],
+        name="north",
+    )(rp1, rp2, rcb, depth, side_depth, main0, side0, main1, side1, last, first)
 
 
 def solution(mesh):

time: 30.7 us -> 28.1 us (0.915)
  the two profiles are of different devices: /device:TPU:2 before, /device:TPU:0 now
where the time goes in v3:
time: 28.1 us; the launch traced here: 27.7 us
  Pallas kernels  13.7 us (49%)
  starting transfers between devices  9.91 us (35%)
  waiting for transfers between devices  1.67 us (6%)
  local copies, waits for them, and re-layouts  1.6 us (6%)
  other arithmetic  0.74 us (3%)
    ppermute x5, starting transfers between devices, swap(): return lax.ppermute(x, ('lon', 'lat'), pairs)  9.91 us
    pallas_call x1, Pallas kernels, per_device(): call(inner_kernel, 6, out_shape=(block(rows + 8), block(rows + 8), block(...  5.97 us
    pallas_call x1, Pallas kernels, per_device(): call(north_kernel, 12, out_shape=shape(*state.shape), in_specs=[VM] * 11,...  3.83 us
    pallas_call x1, Pallas kernels, per_device(): call(south_kernel, 10, out_shape=block(8), in_specs=[VM] * 7, out_specs=V...  2.79 us
    ppermute x5, waiting for transfers between devices, swap(): return lax.ppermute(x, ('lon', 'lat'), pairs)  1.67 us
    unnamed x4, local copies, waits for them, and re-layouts  1.59 us
    pallas_call x1, Pallas kernels, per_device(): call(columns_kernel, 4, out_shape=(strip, strip, shape(8, 128)), in_specs...  0.87 us
    convert_element_type x1, other arithmetic, per_device(): jnp.where(land_mask == 1, jnp.minimum(wet_levels, levels), 0).astype(F32)  0.74 us
  transfers between devices with their start and end apart: 5, of which 2 were waited for; matrix products, arithmetic and copies ran while one was open for 0% of the time, Pallas kernels for 32%

profile of v3, /device:TPU:0, one launch (start us, length us, event | category | flops | bytes accessed | tf_op | source)
XLA Modules:
  0.0 27.7 jit_solution(11318855929455518584)
XLA Ops:
  0.0 0.7 %select_convert_fusion = f32[32,128]{1,0:T(8,128)S(1)} fusion(s32[32,128]{1,0:T(8,128)} %param.5, s32[32,128]{1,0:T(8,128)} %param.4), kind=kLoop, calls=%fused_computation | loop fusion | flops 16384 | bytes 49152 | tf_op jit(solution)/shard_map/convert_element_type | solution.py:417
  0.7 0.0 copy-start
  0.8 1.6 %copy-done = f32[4,32,32,128]{3,2,1,0:T(8,128)S(1)} copy-done((f32[4,32,32,128]{3,2,1,0:T(8,128)S(1)}, f32[4,32,32,128]{3,2,1,0:T(8,128)}, u32[]{:S(2)}) %copy-start) | copy-done | bytes 2097176
  2.3 0.9 %columns.1 = (f32[5,32,128]{2,1,0:T(8,128)S(1)}, f32[5,32,128]{2,1,0:T(8,128)S(1)}, f32[8,128]{1,0:T(8,128)S(1)}) custom-call(f32[4,32,32,128]{3,2,1,0:T(8,128)S(1)} %copy-done, f32[40,128]{1,0:T(8,128)S(1)} %pad.4.depth), custom_call_target="tpu_custom_call" | custom-call | tf_op jit(solution)/shard_map/columns/pallas_call | solution.py:419
  3.2 0.0 copy-start.1
  3.2 0.5 %collective-permute-start = (f32[5,32,128]{2,1,0:T(8,128)S(1)}, f32[5,32,128]{2,1,0:T(8,128)S(1)}, u32[]{:S(2)}, u32[]{:S(2)}) collective-permute-start(f32[5,32,128]{2,1,0:T(8,128)S(1)} %get-tuple-element.14), channel_id=1, source_target_pairs={{0,2},{1,3},{2,0},{3,1},{4,6},{5,7},{6,4},{7,5},{8,10},{9,11},{10,... | collective-permute-start | bytes 245768 | tf_op jit(solution)/shard_map/ppermute | solution.py:398
  3.7 5.7 %collective-permute-start.1 = (f32[5,32,128]{2,1,0:T(8,128)S(1)}, f32[5,32,128]{2,1,0:T(8,128)S(1)}, u32[]{:S(2)}, u32[]{:S(2)}) collective-permute-start(f32[5,32,128]{2,1,0:T(8,128)S(1)} %get-tuple-element.15), channel_id=1, source_target_pairs={{0,30},{1,31},{2,4},{3,5},{4,2},{5,3},{6,8},{7,9},{8,6},{9,7},{10,... | collective-permute-start | bytes 245768 | tf_op jit(solution)/shard_map/ppermute | solution.py:398
  9.4 0.0 collective-permute-done.ra
  9.4 0.1 far.1
  9.5 0.7 %collective-permute-start.3 = (f32[68,8,128]{2,1,0:T(8,128)S(1)}, f32[68,8,128]{2,1,0:T(8,128)S(1)}, u32[]{:S(2)}, u32[]{:S(2)}) collective-permute-start(f32[68,8,128]{2,1,0:T(8,128)S(1)} %far.1), channel_id=1, source_target_pairs={{0,0},{1,31},{2,2},{3,29},{4,4},{5,27},{6,6},{7,25},{8,8},{9,23},{... | collective-permute-start | bytes 835592 | tf_op jit(solution)/shard_map/ppermute | solution.py:398
  10.2 1.3 %collective-permute-done.1.rb = f32[5,32,128]{2,1,0:T(8,128)S(1)} collective-permute-done((f32[5,32,128]{2,1,0:T(8,128)S(1)}, f32[5,32,128]{2,1,0:T(8,128)S(1)}, u32[]{:S(2)}, u32[]{:S(2)}) %collective-permute-start.1) | collective-permute-done | bytes 81952 | tf_op jit(solution)/shard_map/ppermute | solution.py:398
  11.5 0.1 near.1
  11.6 2.4 %collective-permute-start.2 = (f32[66,8,128]{2,1,0:T(8,128)S(1)}, f32[66,8,128]{2,1,0:T(8,128)S(1)}, u32[]{:S(2)}, u32[]{:S(2)}) collective-permute-start(f32[66,8,128]{2,1,0:T(8,128)S(1)} %near.1), channel_id=1, source_target_pairs={{0,1},{1,0},{2,3},{3,2},{4,5},{5,4},{6,7},{7,6},{8,9},{9,8},{10,11... | collective-permute-start | bytes 811016 | tf_op jit(solution)/shard_map/ppermute | solution.py:398
  14.0 0.6 %collective-permute-start.4 = (f32[8,128]{1,0:T(8,128)S(1)}, f32[8,128]{1,0:T(8,128)S(1)}, u32[]{:S(2)}, u32[]{:S(2)}) collective-permute-start(f32[8,128]{1,0:T(8,128)S(1)} %get-tuple-element.16), channel_id=1, source_target_pairs={{0,0},{1,1},{2,2},{3,27},{4,4},{5,29},{6,6},{7,23},{8,8},{9,25},{1... | collective-permute-start | bytes 12296 | tf_op jit(solution)/shard_map/ppermute | solution.py:398
  14.7 0.0 copy-done.1
  14.7 6.0 %inner.1 = (f32[4,32,40,128]{3,2,1,0:T(8,128)S(1)}, f32[4,32,40,128]{3,2,1,0:T(8,128)S(1)}, f32[4,32,36,128]{3,2,1,0:T(8,128)S(1)}, f32[4,32,36,128]{3,2,1,0:T(8...) custom-call(f32[4,32,32,128]{3,2,1,0:T(8,128)S(1)} %copy-done.1, f32[40,128]{1,0:T(8,128)S(1)} %pad.4.depth, ...), custom_call_target="tpu_custom_call" | custom-call | tf_op jit(solution)/shard_map/inner/pallas_call | solution.py:440
  20.7 0.4 %collective-permute-done.2.p.p1 = f32[66,8,128]{2,1,0:T(8,128)S(1)} collective-permute-done((f32[66,8,128]{2,1,0:T(8,128)S(1)}, f32[66,8,128]{2,1,0:T(8,128)S(1)}, u32[]{:S(2)}, u32[]{:S(2)}) %collective-permute-start.2) | collective-permute-done | bytes 270368 | tf_op jit(solution)/shard_map/ppermute | solution.py:398
  21.1 2.8 %south.1 = f32[4,32,8,128]{3,2,1,0:T(8,128)S(1)} custom-call(f32[66,8,128]{2,1,0:T(8,128)S(1)} %collective-permute-done.2.p.p1, f32[40,128]{1,0:T(8,128)S(1)} %pad.4.depth, f32[40,128]{1,0:T(8,128)S(1)} %get-tuple-element.17.side_depth, f32[4,32,40,128]{3,2,1,0:T(8,128)S(1)} %get-tuple-element.18.main0, f32[4,32,40,128]{3,2,1,0:T(8,128)S(1)} %get-tuple-element.19.side0, ...), custom_call_target="tpu_custom_call" | custom-call | tf_op jit(solution)/shard_map/south/pallas_call | solution.py:450
  23.8 0.0 collective-permute-done.4.cb
  23.9 0.0 collective-permute-done.3.p2
  23.9 3.8 %north.1 = f32[4,32,32,128]{3,2,1,0:T(8,128)} custom-call(f32[66,8,128]{2,1,0:T(8,128)S(1)} %collective-permute-done.2.p.p1, f32[68,8,128]{2,1,0:T(8,128)S(1)} %collective-permute-done.3.p2, f32[8,128]{1,0:T(8,128)S(1)} %collective-permute-done.4.cb, f32[40,128]{1,0:T(8,128)S(1)} %pad.4.depth, f32[40,128]{1,0:T(8,128)S(1)} %get-tuple-element.17.side_depth, ...), custom_call_target="tpu_custom_call" | custom-call | tf_op jit(solution)/shard_map/north/pallas_call | solution.py:459
  (1 shorter events, 0.0 us)
Async XLA Ops:
  0.7 1.6 %copy-start = (f32[4,32,32,128]{3,2,1,0:T(8,128)S(1)}, f32[4,32,32,128]{3,2,1,0:T(8,128)}, u32[]{:S(2)}) copy-start(f32[4,32,32,128]{3,2,1,0:T(8,128)} %state.7) | copy-start | bytes 6291460
  3.2 11.5 %copy-start.1 = (f32[4,32,32,128]{3,2,1,0:T(8,128)S(1)}, f32[4,32,32,128]{3,2,1,0:T(8,128)}, u32[]{:S(2)}) copy-start(f32[4,32,32,128]{3,2,1,0:T(8,128)} %state.7) | copy-start | bytes 6291460
  3.2 6.2 %collective-permute-start = (f32[5,32,128]{2,1,0:T(8,128)S(1)}, f32[5,32,128]{2,1,0:T(8,128)S(1)}, u32[]{:S(2)}, u32[]{:S(2)}) collective-permute-start(f32[5,32,128]{2,1,0:T(8,128)S(1)} %get-tuple-element.14), channel_id=1, source_target_pairs={{0,2},{1,3},{2,0},{3,1},{4,6},{5,7},{6,4},{7,5},{8,10},{9,11},{10,... | collective-permute-start | bytes 245768 | tf_op jit(solution)/shard_map/ppermute | solution.py:398
  3.7 7.8 %collective-permute-start.1 = (f32[5,32,128]{2,1,0:T(8,128)S(1)}, f32[5,32,128]{2,1,0:T(8,128)S(1)}, u32[]{:S(2)}, u32[]{:S(2)}) collective-permute-start(f32[5,32,128]{2,1,0:T(8,128)S(1)} %get-tuple-element.15), channel_id=1, source_target_pairs={{0,30},{1,31},{2,4},{3,5},{4,2},{5,3},{6,8},{7,9},{8,6},{9,7},{10,... | collective-permute-start | bytes 245768 | tf_op jit(solution)/shard_map/ppermute | solution.py:398
  9.5 14.4 %collective-permute-start.3 = (f32[68,8,128]{2,1,0:T(8,128)S(1)}, f32[68,8,128]{2,1,0:T(8,128)S(1)}, u32[]{:S(2)}, u32[]{:S(2)}) collective-permute-start(f32[68,8,128]{2,1,0:T(8,128)S(1)} %far.1), channel_id=1, source_target_pairs={{0,0},{1,31},{2,2},{3,29},{4,4},{5,27},{6,6},{7,25},{8,8},{9,23},{... | collective-permute-start | bytes 835592 | tf_op jit(solution)/shard_map/ppermute | solution.py:398
  11.6 9.4 %collective-permute-start.2 = (f32[66,8,128]{2,1,0:T(8,128)S(1)}, f32[66,8,128]{2,1,0:T(8,128)S(1)}, u32[]{:S(2)}, u32[]{:S(2)}) collective-permute-start(f32[66,8,128]{2,1,0:T(8,128)S(1)} %near.1), channel_id=1, source_target_pairs={{0,1},{1,0},{2,3},{3,2},{4,5},{5,4},{6,7},{7,6},{8,9},{9,8},{10,11... | collective-permute-start | bytes 811016 | tf_op jit(solution)/shard_map/ppermute | solution.py:398
  14.0 9.8 %collective-permute-start.4 = (f32[8,128]{1,0:T(8,128)S(1)}, f32[8,128]{1,0:T(8,128)S(1)}, u32[]{:S(2)}, u32[]{:S(2)}) collective-permute-start(f32[8,128]{1,0:T(8,128)S(1)} %get-tuple-element.16), channel_id=1, source_target_pairs={{0,0},{1,1},{2,2},{3,27},{4,4},{5,29},{6,6},{7,23},{8,8},{9,25},{1... | collective-permute-start | bytes 12296 | tf_op jit(solution)/shard_map/ppermute | solution.py:398

commit v4 on v3

--- a/solution.py
+++ b/solution.py
@@ -51,6 +51,10 @@
 
 def sublanes():
     return lax.broadcasted_iota(jnp.int32, (8, 128), 0)
+
+
+def limit_kernel(levels, top):
+    top[...] = jnp.full(top.shape, float(levels), F32)
 
 
 def edge_rows(strip, f, r):
@@ -154,8 +158,8 @@
             cb[2 * f + r:2 * f + r + 1, :] = edge_rows(lb, f, r)[1]
 
 
-def coriolis_rows(first, total):
-    row = first + sublanes()
+def coriolis_rows(first, total, order=None):
+    row = first + (sublanes() if order is None else order)
     row = jnp.where(row >= total, 2 * total - 1 - row, row)
     return 0.2 + 0.8 * ((row.astype(F32) + 0.5) / total)
 
@@ -163,14 +167,15 @@
 def sweep(table, levels, jobs, scale, leave=1.0, unroll=8, unroll_back=8):
     lane = lanes()
     zero = jnp.zeros((8, 128), F32)
-    turns = [cor * (UNIT * time_step * scale / DRIFT) for _, _, _, _, cor, _, _ in jobs]
-    uppers = [depth - 1.0 for _, _, _, depth, _, _, _ in jobs]
+    jobs = [job if len(job) == 9 else (*job, 1, job[2]) for job in jobs]
+    turns = [cor * (UNIT * time_step * scale / DRIFT) for _, _, _, _, cor, *_ in jobs]
+    uppers = [depth - 1.0 for _, _, _, depth, *_ in jobs]
 
     def forward(k, carry):
         inner, lowest = table[0, k], table[1, k]
         level = k.astype(F32)
         out = []
-        for n, (own, other, o, depth, _, dst, d) in enumerate(jobs):
+        for n, (own, other, o, depth, _, dst, d, apart, at) in enumerate(jobs):
             halves = carry[6 * n:6 * n + 4]
             sums = carry[6 * n + 4:6 * n + 6]
             weight = jnp.where(level < uppers[n], inner, jnp.where(level < depth, lowest, 0.0))
@@ -180,15 +185,15 @@
             prov = []
             near = []
             for f in range(4):
-                x = other[f, k, o:o + 8, :]
+                x = other[f, k, at:at + 8, :]
                 e1 = pltpu.roll(jnp.where(lane == 0, x, q[f]), 127, 1)
                 e2 = pltpu.roll(jnp.where(lane < 2, x, q[f]), 126, 1)
                 w1 = pltpu.roll(jnp.where(lane == 127, x, q[f]), 1, 1)
                 w2 = pltpu.roll(jnp.where(lane >= 126, x, q[f]), 2, 1)
-                n1 = own[f, k, o + 1:o + 9, :]
-                n2 = own[f, k, o + 2:o + 10, :]
-                s1 = own[f, k, o - 1:o + 7, :]
-                s2 = own[f, k, o - 2:o + 6, :]
+                n1 = own[f, k, o + apart:o + apart + 8, :]
+                n2 = own[f, k, o + 2 * apart:o + 2 * apart + 8, :]
+                s1 = own[f, k, o - apart:o - apart + 8, :]
+                s2 = own[f, k, o - 2 * apart:o - 2 * apart + 8, :]
                 dx, dy = e1 - w1, n1 - s1
                 near.append((dx, dy))
                 slope_x = 8.0 * dx - (e2 - w2)
@@ -217,7 +222,7 @@
         k = levels - 1 - step
         ratio = table[0, k]
         out = []
-        for n, (_, _, _, _, _, dst, d) in enumerate(jobs):
+        for n, (_, _, _, _, _, dst, d, _, _) in enumerate(jobs):
             for f in range(4):
                 value = dst[f, k, d:d + 8, :] + ratio * carry[4 * n + f]
                 dst[f, k, d:d + 8, :] = value * leave if leave != 1.0 else value
@@ -317,7 +322,7 @@
 
 
 def north_kernel(p1, p2, cb, depth, side_depth, main0, side0, main1, side1, middle, south, out,
-                 rim0, edge0, rim1, edge1, last, table, sems):
+                 pair0, facing0, pair1, rim1, edge1, last, depths, table, sems):
     levels, rows = main0.shape[1], out.shape[2]
     done = [
         pltpu.make_async_copy(middle, out.at[:, :, 8:rows - 8, :], sems.at[0]),
@@ -346,7 +351,14 @@
     far = jnp.where(((lanes() & 3) < 2) == sender_even, p2[2 * levels + 1], cb[...])
     turned = jnp.where(sublanes() < 4, folded(far), -folded(far))
     corner = jnp.where(band_even, p1[2 * levels + 1], jnp.where(is_top, turned, far))
-    depths = jnp.where(sublanes() < 6, depth[rows - 2:rows + 6, :], pltpu.roll(ghost(2 * levels, 1.0), 6, 0))
+    rim_depth = ghost(2 * levels, 1.0)
+
+    def turns(start, count):
+        return pl.ds(start, count, stride=2)
+
+    depths[turns(0, 4), :] = side_depth[rows:rows + 4, :]
+    depths[turns(1, 2), :] = depth[rows + 2:rows + 4, :]
+    depths[turns(5, 2), :] = rim_depth[0:2, :]
 
     def fill(k, unused):
         corners = pltpu.roll(corner, jnp.where(is_top, 4 * k - 124, 124 - 4 * k) & 127, 1)
@@ -354,23 +366,30 @@
             rim = ghost(2 * k + pair, 1.0 if pair == 0 else -1.0)
             for j in range(2):
                 f = 2 * pair + j
-                rim0[f, k, 0:8, :] = main0[f, k, rows - 4:rows + 4, :]
-                rim0[f, k, 8:12, :] = rim[4 * j:4 * j + 4, :]
-                edge0[f, k, 0:8, :] = side0[f, k, rows - 4:rows + 4, :]
-                edge0[f, k, 8:10, :] = corners[2 * f:2 * f + 2, :]
-                edge0[f, k, 10:12, :] = jnp.zeros((2, 128), F32)
-                rim1[f, k, 0:4, :] = main1[f, k, rows - 8:rows - 4, :]
-                edge1[f, k, 0:4, :] = side1[f, k, rows - 8:rows - 4, :]
+                pair0[f, k, turns(0, 6), :] = side0[f, k, rows - 2:rows + 4, :]
+                pair0[f, k, turns(1, 4), :] = main0[f, k, rows:rows + 4, :]
+                pair0[f, k, turns(9, 4), :] = rim[4 * j:4 * j + 4, :]
+                pair0[f, k, turns(12, 2), :] = corners[2 * f:2 * f + 2, :]
+                facing0[f, k, turns(0, 4), :] = main0[f, k, rows:rows + 4, :]
+                facing0[f, k, turns(1, 2), :] = side0[f, k, rows + 2:rows + 4, :]
+                facing0[f, k, turns(5, 2), :] = corners[2 * f:2 * f + 2, :]
         return unused
 
     lax.fori_loop(0, levels, fill, 0, unroll=8)
-    cor = coriolis_rows(first_row + (rows - 6), total)
-    sweep(table, levels, [
-        (rim0, edge0, 2, depths, cor, rim1, 4),
-        (edge0, rim0, 2, side_depth[rows - 2:rows + 6, :], cor, edge1, 4),
-    ], 1.0, 1.0, 16, 8)
+    cor = coriolis_rows(first_row + (rows - 4), total, (sublanes() >> 1) + 2 * (sublanes() & 1))
+    sweep(table, levels, [(pair0, facing0, 4, depths[...], cor, pair1, 0, 2, 0)], 1.0, 1.0, 16, 8)
+
+    def split(k, unused):
+        for f in range(4):
+            rim1[f, k, 0:8, :] = main1[f, k, rows - 8:rows, :]
+            rim1[f, k, 8:12, :] = pair1[f, k, turns(1, 4), :]
+            edge1[f, k, 0:4, :] = side1[f, k, rows - 6:rows - 2, :]
+            edge1[f, k, 4:8, :] = pair1[f, k, turns(0, 4), :]
+        return unused
+
+    lax.fori_loop(0, levels, split, 0, unroll=8)
     cor = coriolis_rows(first_row + (rows - 8), total)
-    sweep(table, levels, [(rim1, edge1, 2, depth[rows - 4:rows + 4, :], cor, last, 0)], GAIN, 1.0 / GAIN**2, 16, 8)
+    sweep(table, levels, [(rim1, edge1, 2, depth[rows - 4:rows + 4, :], cor, last, 0, 1, 0)], GAIN, 1.0 / GAIN**2, 16, 8)
     copy = pltpu.make_async_copy(last, out.at[:, :, rows - 8:rows, :], sems.at[2])
     copy.start()
     for other in done:
@@ -414,7 +433,11 @@
     block = lambda n: shape(fields, levels, n, 128)
     room = lambda n: pltpu.VMEM((fields, levels, n, 128), F32)
     strip = shape(5, rows, 128)
-    depth = jnp.where(land_mask == 1, jnp.minimum(wet_levels, levels), 0).astype(F32)
+    top = call(
+        functools.partial(limit_kernel, levels), 4, out_shape=shape(8, 128), out_specs=VM, name="limit",
+        cost_estimate=pl.CostEstimate(flops=10**10, bytes_accessed=4096, transcendentals=0),
+    )()
+    depth = jnp.where(land_mask == 1, jnp.minimum(wet_levels.astype(F32), top[0]), 0.0)
     depth = jnp.pad(depth, ((4, 4), (0, 0)))
     la, lb, cb = call(
         columns_kernel, 4, out_shape=(strip, strip, shape(8, 128)), in_specs=[VM] * 2, out_specs=(VM,) * 3,
@@ -462,7 +485,8 @@
         out_shape=shape(*state.shape),
         in_specs=[VM] * 11,
         out_specs=HB,
-        scratch_shapes=[room(16)] * 4 + [room(8), room_table, pltpu.SemaphoreType.DMA((3,))],
+        scratch_shapes=[room(16), room(8), room(8), room(16), room(8), room(8), pltpu.VMEM((8, 128), F32), room_table,
+                        pltpu.SemaphoreType.DMA((3,))],
         name="north",
     )(rp1, rp2, rcb, depth, side_depth, main0, side0, main1, side1, last, first)
 

time: 28.1 us -> 26.8 us (0.954)
  other arithmetic: 0.74 us -> 0.01 us
  Pallas kernels: 13.7 us -> 13.2 us
    convert_element_type x1 -> x0, other arithmetic: 0.74 us -> none  [per_device(): jnp.where(land_mask == 1, jnp.minimum(wet_levels, levels), 0).astype(F32)]
    pallas_call x1, Pallas kernels: 3.83 us -> 3.37 us  [per_device(): call(north_kernel, 12, out_shape=shape(*state.shape), in_specs=[VM] * 11,...]
    unnamed x4 -> x6, local copies, waits for them, and re-layouts: 1.59 us -> 1.6 us
  transfers between devices with their start and end apart: 5 -> 5, of which waited for: 2 -> 2; matrix products, arithmetic and copies ran while one was open for 0% -> 0% of each run, Pallas kernels for 32% -> 34%
where the time goes in v4:
time: 26.8 us; the launch traced here: 26.5 us
  Pallas kernels  13.2 us (49%)
  starting transfers between devices  9.9 us (37%)
  waiting for transfers between devices  1.68 us (6%)
  local copies, waits for them, and re-layouts  1.61 us (6%)
    ppermute x5, starting transfers between devices, swap(): return lax.ppermute(x, ('lon', 'lat'), pairs)  9.9 us
    pallas_call x1, Pallas kernels, per_device(): call(inner_kernel, 6, out_shape=(block(rows + 8), block(rows + 8), block(...  5.97 us
    pallas_call x1, Pallas kernels, per_device(): call(north_kernel, 12, out_shape=shape(*state.shape), in_specs=[VM] * 11,...  3.37 us
    pallas_call x1, Pallas kernels, per_device(): call(south_kernel, 10, out_shape=block(8), in_specs=[VM] * 7, out_specs=V...  2.79 us
    ppermute x5, waiting for transfers between devices, swap(): return lax.ppermute(x, ('lon', 'lat'), pairs)  1.68 us
    unnamed x6, local copies, waits for them, and re-layouts  1.6 us
    pallas_call x1, Pallas kernels, per_device(): call(columns_kernel, 4, out_shape=(strip, strip, shape(8, 128)), in_specs...  0.87 us
  transfers between devices with their start and end apart: 5, of which 2 were waited for; matrix products, arithmetic and copies ran while one was open for 0% of the time, Pallas kernels for 34%

profile of v4, /device:TPU:0, one launch (start us, length us, event | category | flops | bytes accessed | tf_op | source)
XLA Modules:
  0.0 26.5 jit_solution(5654036046080965059)
XLA Ops:
  0.0 0.0 copy-start.1
  0.0 0.0 copy-start.2
  0.0 0.0 copy-start
  0.0 0.7 %copy-done.1 = s32[32,128]{1,0:T(8,128)S(1)} copy-done((s32[32,128]{1,0:T(8,128)S(1)}, s32[32,128]{1,0:T(8,128)}, u32[]{:S(2)}) %copy-start.1) | copy-done | bytes 16408
  0.7 0.0 copy-done.2
  0.7 0.9 %copy-done = f32[4,32,32,128]{3,2,1,0:T(8,128)S(1)} copy-done((f32[4,32,32,128]{3,2,1,0:T(8,128)S(1)}, f32[4,32,32,128]{3,2,1,0:T(8,128)}, u32[]{:S(2)}) %copy-start) | copy-done | bytes 2097176
  1.6 0.9 %columns.1 = (f32[5,32,128]{2,1,0:T(8,128)S(1)}, f32[5,32,128]{2,1,0:T(8,128)S(1)}, f32[8,128]{1,0:T(8,128)S(1)}) custom-call(f32[4,32,32,128]{3,2,1,0:T(8,128)S(1)} %copy-done, f32[40,128]{1,0:T(8,128)S(1)} %pad.4.depth), custom_call_target="tpu_custom_call" | custom-call | tf_op jit(solution)/shard_map/columns/pallas_call | solution.py:442
  2.5 0.5 %collective-permute-start = (f32[5,32,128]{2,1,0:T(8,128)S(1)}, f32[5,32,128]{2,1,0:T(8,128)S(1)}, u32[]{:S(2)}, u32[]{:S(2)}) collective-permute-start(f32[5,32,128]{2,1,0:T(8,128)S(1)} %get-tuple-element.14), channel_id=1, source_target_pairs={{0,2},{1,3},{2,0},{3,1},{4,6},{5,7},{6,4},{7,5},{8,10},{9,11},{10,... | collective-permute-start | bytes 245768 | tf_op jit(solution)/shard_map/ppermute | solution.py:417
  3.0 5.7 %collective-permute-start.1 = (f32[5,32,128]{2,1,0:T(8,128)S(1)}, f32[5,32,128]{2,1,0:T(8,128)S(1)}, u32[]{:S(2)}, u32[]{:S(2)}) collective-permute-start(f32[5,32,128]{2,1,0:T(8,128)S(1)} %get-tuple-element.15), channel_id=1, source_target_pairs={{0,30},{1,31},{2,4},{3,5},{4,2},{5,3},{6,8},{7,9},{8,6},{9,7},{10,... | collective-permute-start | bytes 245768 | tf_op jit(solution)/shard_map/ppermute | solution.py:417
  8.7 0.0 collective-permute-done.ra
  8.7 0.1 far.1
  8.8 0.7 %collective-permute-start.3 = (f32[68,8,128]{2,1,0:T(8,128)S(1)}, f32[68,8,128]{2,1,0:T(8,128)S(1)}, u32[]{:S(2)}, u32[]{:S(2)}) collective-permute-start(f32[68,8,128]{2,1,0:T(8,128)S(1)} %far.1), channel_id=1, source_target_pairs={{0,0},{1,31},{2,2},{3,29},{4,4},{5,27},{6,6},{7,25},{8,8},{9,23},{... | collective-permute-start | bytes 835592 | tf_op jit(solution)/shard_map/ppermute | solution.py:417
  9.5 1.3 %collective-permute-done.1.rb = f32[5,32,128]{2,1,0:T(8,128)S(1)} collective-permute-done((f32[5,32,128]{2,1,0:T(8,128)S(1)}, f32[5,32,128]{2,1,0:T(8,128)S(1)}, u32[]{:S(2)}, u32[]{:S(2)}) %collective-permute-start.1) | collective-permute-done | bytes 81952 | tf_op jit(solution)/shard_map/ppermute | solution.py:417
  10.8 0.1 near.1
  10.9 2.4 %collective-permute-start.2 = (f32[66,8,128]{2,1,0:T(8,128)S(1)}, f32[66,8,128]{2,1,0:T(8,128)S(1)}, u32[]{:S(2)}, u32[]{:S(2)}) collective-permute-start(f32[66,8,128]{2,1,0:T(8,128)S(1)} %near.1), channel_id=1, source_target_pairs={{0,1},{1,0},{2,3},{3,2},{4,5},{5,4},{6,7},{7,6},{8,9},{9,8},{10,11... | collective-permute-start | bytes 811016 | tf_op jit(solution)/shard_map/ppermute | solution.py:417
  13.3 0.6 %collective-permute-start.4 = (f32[8,128]{1,0:T(8,128)S(1)}, f32[8,128]{1,0:T(8,128)S(1)}, u32[]{:S(2)}, u32[]{:S(2)}) collective-permute-start(f32[8,128]{1,0:T(8,128)S(1)} %get-tuple-element.16), channel_id=1, source_target_pairs={{0,0},{1,1},{2,2},{3,27},{4,4},{5,29},{6,6},{7,23},{8,8},{9,25},{1... | collective-permute-start | bytes 12296 | tf_op jit(solution)/shard_map/ppermute | solution.py:417
  14.0 6.0 %inner.1 = (f32[4,32,40,128]{3,2,1,0:T(8,128)S(1)}, f32[4,32,40,128]{3,2,1,0:T(8,128)S(1)}, f32[4,32,36,128]{3,2,1,0:T(8,128)S(1)}, f32[4,32,36,128]{3,2,1,0:T(8...) custom-call(f32[4,32,32,128]{3,2,1,0:T(8,128)S(1)} %copy-done, f32[40,128]{1,0:T(8,128)S(1)} %pad.4.depth, ...), custom_call_target="tpu_custom_call" | custom-call | tf_op jit(solution)/shard_map/inner/pallas_call | solution.py:463
  20.0 0.4 %collective-permute-done.2.p.p1 = f32[66,8,128]{2,1,0:T(8,128)S(1)} collective-permute-done((f32[66,8,128]{2,1,0:T(8,128)S(1)}, f32[66,8,128]{2,1,0:T(8,128)S(1)}, u32[]{:S(2)}, u32[]{:S(2)}) %collective-permute-start.2) | collective-permute-done | bytes 270368 | tf_op jit(solution)/shard_map/ppermute | solution.py:417
  20.3 2.8 %south.1 = f32[4,32,8,128]{3,2,1,0:T(8,128)S(1)} custom-call(f32[66,8,128]{2,1,0:T(8,128)S(1)} %collective-permute-done.2.p.p1, f32[40,128]{1,0:T(8,128)S(1)} %pad.4.depth, f32[40,128]{1,0:T(8,128)S(1)} %get-tuple-element.17.side_depth, f32[4,32,40,128]{3,2,1,0:T(8,128)S(1)} %get-tuple-element.18.main0, f32[4,32,40,128]{3,2,1,0:T(8,128)S(1)} %get-tuple-element.19.side0, ...), custom_call_target="tpu_custom_call" | custom-call | tf_op jit(solution)/shard_map/south/pallas_call | solution.py:473
  23.1 0.0 collective-permute-done.4.cb
  23.1 0.0 collective-permute-done.3.p2
  23.1 3.4 %north.1 = f32[4,32,32,128]{3,2,1,0:T(8,128)} custom-call(f32[66,8,128]{2,1,0:T(8,128)S(1)} %collective-permute-done.2.p.p1, f32[68,8,128]{2,1,0:T(8,128)S(1)} %collective-permute-done.3.p2, f32[8,128]{1,0:T(8,128)S(1)} %collective-permute-done.4.cb, f32[40,128]{1,0:T(8,128)S(1)} %pad.4.depth, f32[40,128]{1,0:T(8,128)S(1)} %get-tuple-element.17.side_depth, ...), custom_call_target="tpu_custom_call" | custom-call | tf_op jit(solution)/shard_map/north/pallas_call | solution.py:482
  (4 shorter events, 0.0 us)
Async XLA Ops:
  0.0 0.7 %copy-start.1 = (s32[32,128]{1,0:T(8,128)S(1)}, s32[32,128]{1,0:T(8,128)}, u32[]{:S(2)}) copy-start(s32[32,128]{1,0:T(8,128)} %param.5) | copy-start | bytes 49156
  0.0 0.7 %copy-start.2 = (s32[32,128]{1,0:T(8,128)S(1)}, s32[32,128]{1,0:T(8,128)}, u32[]{:S(2)}) copy-start(s32[32,128]{1,0:T(8,128)} %param.4) | copy-start | bytes 49156
  0.0 1.6 %copy-start = (f32[4,32,32,128]{3,2,1,0:T(8,128)S(1)}, f32[4,32,32,128]{3,2,1,0:T(8,128)}, u32[]{:S(2)}) copy-start(f32[4,32,32,128]{3,2,1,0:T(8,128)} %state.7) | copy-start | bytes 6291460
  2.5 6.2 %collective-permute-start = (f32[5,32,128]{2,1,0:T(8,128)S(1)}, f32[5,32,128]{2,1,0:T(8,128)S(1)}, u32[]{:S(2)}, u32[]{:S(2)}) collective-permute-start(f32[5,32,128]{2,1,0:T(8,128)S(1)} %get-tuple-element.14), channel_id=1, source_target_pairs={{0,2},{1,3},{2,0},{3,1},{4,6},{5,7},{6,4},{7,5},{8,10},{9,11},{10,... | collective-permute-start | bytes 245768 | tf_op jit(solution)/shard_map/ppermute | solution.py:417
  3.0 7.8 %collective-permute-start.1 = (f32[5,32,128]{2,1,0:T(8,128)S(1)}, f32[5,32,128]{2,1,0:T(8,128)S(1)}, u32[]{:S(2)}, u32[]{:S(2)}) collective-permute-start(f32[5,32,128]{2,1,0:T(8,128)S(1)} %get-tuple-element.15), channel_id=1, source_target_pairs={{0,30},{1,31},{2,4},{3,5},{4,2},{5,3},{6,8},{7,9},{8,6},{9,7},{10,... | collective-permute-start | bytes 245768 | tf_op jit(solution)/shard_map/ppermute | solution.py:417
  8.8 14.4 %collective-permute-start.3 = (f32[68,8,128]{2,1,0:T(8,128)S(1)}, f32[68,8,128]{2,1,0:T(8,128)S(1)}, u32[]{:S(2)}, u32[]{:S(2)}) collective-permute-start(f32[68,8,128]{2,1,0:T(8,128)S(1)} %far.1), channel_id=1, source_target_pairs={{0,0},{1,31},{2,2},{3,29},{4,4},{5,27},{6,6},{7,25},{8,8},{9,23},{... | collective-permute-start | bytes 835592 | tf_op jit(solution)/shard_map/ppermute | solution.py:417
  10.9 9.4 %collective-permute-start.2 = (f32[66,8,128]{2,1,0:T(8,128)S(1)}, f32[66,8,128]{2,1,0:T(8,128)S(1)}, u32[]{:S(2)}, u32[]{:S(2)}) collective-permute-start(f32[66,8,128]{2,1,0:T(8,128)S(1)} %near.1), channel_id=1, source_target_pairs={{0,1},{1,0},{2,3},{3,2},{4,5},{5,4},{6,7},{7,6},{8,9},{9,8},{10,11... | collective-permute-start | bytes 811016 | tf_op jit(solution)/shard_map/ppermute | solution.py:417
  13.3 9.8 %collective-permute-start.4 = (f32[8,128]{1,0:T(8,128)S(1)}, f32[8,128]{1,0:T(8,128)S(1)}, u32[]{:S(2)}, u32[]{:S(2)}) collective-permute-start(f32[8,128]{1,0:T(8,128)S(1)} %get-tuple-element.16), channel_id=1, source_target_pairs={{0,0},{1,1},{2,2},{3,27},{4,4},{5,29},{6,6},{7,23},{8,8},{9,25},{1... | collective-permute-start | bytes 12296 | tf_op jit(solution)/shard_map/ppermute | solution.py:417

commit v5 on v4

--- a/solution.py
+++ b/solution.py
@@ -142,7 +142,7 @@
                     new.append(jnp.where(spot_w, turned, accs[len(new)]))
             return tuple(new)
 
-        accs = lax.fori_loop(0, levels, body, (zero,) * (4 * groups), unroll=16)
+        accs = lax.fori_loop(0, levels, body, (zero,) * (4 * groups), unroll=32)
         for j in range(2):
             for g in range(groups):
                 at = slice(8 * g, 8 * g + 8)
@@ -269,7 +269,7 @@
                 side0[f, k, to, :] = side_tile(easts[f, at, :], wests[f, at, :], group, k)
         return unused
 
-    lax.fori_loop(0, levels, fill, 0, unroll=16)
+    lax.fori_loop(0, levels, fill, 0, unroll=32)
 
     jobs = []
     for w in range(1, groups):
@@ -282,7 +282,7 @@
     for w in range(1, groups - 1):
         cor = coriolis_rows(first_row + 8 * w, total)
         jobs.append((main1, side1, 8 * w + 2, depth[8 * w + 4:8 * w + 12, :], cor, last, 8 * w - 8))
-    sweep(table, levels, jobs, GAIN, 1.0 / GAIN**2, 16, 8)
+    sweep(table, levels, jobs, GAIN, 1.0 / GAIN**2, 32, 16)
 
 
 def south_kernel(p, depth, side_depth, main0, side0, main1, side1, last, rim0, edge0, rim1, edge1, table):
@@ -311,17 +311,17 @@
                 edge1[f, k, 8:12, :] = side1[f, k, 8:12, :]
         return unused
 
-    lax.fori_loop(0, levels, fill, 0, unroll=8)
+    lax.fori_loop(0, levels, fill, 0, unroll=32)
     cor = coriolis_rows(first_row - 2, total)
     sweep(table, levels, [
         (rim0, edge0, 2, depths, cor, rim1, 0),
         (edge0, rim0, 2, side_depth[2:10, :], cor, edge1, 0),
-    ], 1.0, 1.0, 16, 8)
+    ], 1.0, 1.0, 32, 16)
     cor = coriolis_rows(first_row, total)
-    sweep(table, levels, [(rim1, edge1, 2, depth[4:12, :], cor, last, 0)], GAIN, 1.0 / GAIN**2, 16, 8)
-
-
-def north_kernel(p1, p2, cb, depth, side_depth, main0, side0, main1, side1, middle, south, out,
+    sweep(table, levels, [(rim1, edge1, 2, depth[4:12, :], cor, last, 0)], GAIN, 1.0 / GAIN**2, 32, 16)
+
+
+def north_kernel(p1, p2, cb, own_cb, depth, side_depth, main0, side0, main1, side1, middle, south, out,
                  pair0, facing0, pair1, rim1, edge1, last, depths, table, sems):
     levels, rows = main0.shape[1], out.shape[2]
     done = [
@@ -347,8 +347,11 @@
         turned = jnp.take_along_axis(folded(far), flip, axis=0, mode="promise_in_bounds") * sign
         return jnp.where(band_even, p1[index], jnp.where(is_top, turned, far))
 
-    sender_even = (lax.axis_index("lon") % 2 == 0) != is_top
-    far = jnp.where(((lanes() & 3) < 2) == sender_even, p2[2 * levels + 1], cb[...])
+    lon, count = lax.axis_index("lon"), lax.axis_size("lon")
+    lon_even = lon % 2 == 0
+    beyond = jnp.where(lon_even, lon + count - 1, lon + 1) % count
+    beside = jnp.where(is_top & (lon + beyond == count - 1), own_cb[...], cb[...])
+    far = jnp.where(((lanes() & 3) < 2) == (lon_even != is_top), p2[2 * levels + 1], beside)
     turned = jnp.where(sublanes() < 4, folded(far), -folded(far))
     corner = jnp.where(band_even, p1[2 * levels + 1], jnp.where(is_top, turned, far))
     rim_depth = ghost(2 * levels, 1.0)
@@ -375,9 +378,9 @@
                 facing0[f, k, turns(5, 2), :] = corners[2 * f:2 * f + 2, :]
         return unused
 
-    lax.fori_loop(0, levels, fill, 0, unroll=8)
+    lax.fori_loop(0, levels, fill, 0, unroll=32)
     cor = coriolis_rows(first_row + (rows - 4), total, (sublanes() >> 1) + 2 * (sublanes() & 1))
-    sweep(table, levels, [(pair0, facing0, 4, depths[...], cor, pair1, 0, 2, 0)], 1.0, 1.0, 16, 8)
+    sweep(table, levels, [(pair0, facing0, 4, depths[...], cor, pair1, 0, 2, 0)], 1.0, 1.0, 32, 32)
 
     def split(k, unused):
         for f in range(4):
@@ -387,9 +390,9 @@
             edge1[f, k, 4:8, :] = pair1[f, k, turns(0, 4), :]
         return unused
 
-    lax.fori_loop(0, levels, split, 0, unroll=8)
+    lax.fori_loop(0, levels, split, 0, unroll=16)
     cor = coriolis_rows(first_row + (rows - 8), total)
-    sweep(table, levels, [(rim1, edge1, 2, depth[rows - 4:rows + 4, :], cor, last, 0, 1, 0)], GAIN, 1.0 / GAIN**2, 16, 8)
+    sweep(table, levels, [(rim1, edge1, 2, depth[rows - 4:rows + 4, :], cor, last, 0, 1, 0)], GAIN, 1.0 / GAIN**2, 32, 32)
     copy = pltpu.make_async_copy(last, out.at[:, :, rows - 8:rows, :], sems.at[2])
     copy.start()
     for other in done:
@@ -423,8 +426,14 @@
         if b == bands - 1:
             return count - 1 - i, b
         if b == 0:
-            return i, b
+            return mate(i), b
         return i, (b + 1 if b % 2 else b - 1)
+
+    def far_beyond(i, b):
+        middle = count - 1 - beyond(i) == i
+        if b in (0, bands - 1) and middle:
+            return i, bands - 1 - b
+        return far(beyond(i), b) if b else (beyond(i), b)
 
     def call(kernel, vmem, **given):
         return pl.pallas_call(kernel, compiler_params=pltpu.CompilerParams(vmem_limit_bytes=vmem * 2**20), **given)
@@ -445,7 +454,7 @@
     )(state, depth)
     ra = swap(la, lambda i, b: (mate(i), b))
     rb = swap(lb, lambda i, b: (beyond(i), b))
-    rcb = swap(cb, lambda i, b: far(i if b == 0 else beyond(i), b))
+    rcb = swap(cb, far_beyond)
     p2 = call(
         far_kernel, 4, out_shape=shape(2 * levels + 4, 8, 128), in_specs=[VM] * 3, out_specs=VM, name="far",
     )(state, depth, ra)
@@ -483,12 +492,12 @@
         north_kernel,
         12,
         out_shape=shape(*state.shape),
-        in_specs=[VM] * 11,
+        in_specs=[VM] * 12,
         out_specs=HB,
         scratch_shapes=[room(16), room(8), room(8), room(16), room(8), room(8), pltpu.VMEM((8, 128), F32), room_table,
                         pltpu.SemaphoreType.DMA((3,))],
         name="north",
-    )(rp1, rp2, rcb, depth, side_depth, main0, side0, main1, side1, last, first)
+    )(rp1, rp2, rcb, cb, depth, side_depth, main0, side0, main1, side1, last, first)
 
 
 def solution(mesh):

time: 26.8 us -> 24.2 us (0.903)
  starting transfers between devices: 9.9 us -> 8.35 us
  Pallas kernels: 13.2 us -> 12 us
    ppermute x5, starting transfers between devices: 9.9 us -> 8.35 us  [swap(): return lax.ppermute(x, ('lon', 'lat'), pairs)]
    pallas_call x1, Pallas kernels: 3.37 us -> 2.9 us  [per_device(): call(north_kernel, 12, out_shape=shape(*state.shape), in_specs=[VM] * 12,...]
    pallas_call x1, Pallas kernels: 2.79 us -> 2.34 us  [per_device(): call(south_kernel, 10, out_shape=block(8), in_specs=[VM] * 7, out_specs=V...]
  transfers between devices with their start and end apart: 5 -> 5, of which waited for: 2 -> 1; matrix products, arithmetic and copies ran while one was open for 0% -> 0% of each run, Pallas kernels for 34% -> 35%
where the time goes in v5:
time: 24.2 us; the launch traced here: 24 us
  Pallas kernels  12 us (50%)
  starting transfers between devices  8.35 us (35%)
  waiting for transfers between devices  1.93 us (8%)
  local copies, waits for them, and re-layouts  1.61 us (7%)
    ppermute x5, starting transfers between devices, swap(): return lax.ppermute(x, ('lon', 'lat'), pairs)  8.35 us
    pallas_call x1, Pallas kernels, per_device(): call(inner_kernel, 6, out_shape=(block(rows + 8), block(rows + 8), block(...  5.83 us
    pallas_call x1, Pallas kernels, per_device(): call(north_kernel, 12, out_shape=shape(*state.shape), in_specs=[VM] * 12,...  2.9 us
    pallas_call x1, Pallas kernels, per_device(): call(south_kernel, 10, out_shape=block(8), in_specs=[VM] * 7, out_specs=V...  2.34 us
    ppermute x5, waiting for transfers between devices, swap(): return lax.ppermute(x, ('lon', 'lat'), pairs)  1.93 us
    unnamed x6, local copies, waits for them, and re-layouts  1.6 us
    pallas_call x1, Pallas kernels, per_device(): call(columns_kernel, 4, out_shape=(strip, strip, shape(8, 128)), in_specs...  0.69 us
  transfers between devices with their start and end apart: 5, of which 1 were waited for; matrix products, arithmetic and copies ran while one was open for 0% of the time, Pallas kernels for 35%

profile of v5, /device:TPU:0, one launch (start us, length us, event | category | flops | bytes accessed | tf_op | source)
XLA Modules:
  0.0 24.0 jit_solution(16742041034621289109)
XLA Ops:
  0.0 0.0 copy-start.1
  0.0 0.0 copy-start.2
  0.0 0.0 copy-start
  0.0 0.7 %copy-done.1 = s32[32,128]{1,0:T(8,128)S(1)} copy-done((s32[32,128]{1,0:T(8,128)S(1)}, s32[32,128]{1,0:T(8,128)}, u32[]{:S(2)}) %copy-start.1) | copy-done | bytes 16408
  0.7 0.0 copy-done.2
  0.7 0.9 %copy-done = f32[4,32,32,128]{3,2,1,0:T(8,128)S(1)} copy-done((f32[4,32,32,128]{3,2,1,0:T(8,128)S(1)}, f32[4,32,32,128]{3,2,1,0:T(8,128)}, u32[]{:S(2)}) %copy-start) | copy-done | bytes 2097176
  1.6 0.7 %columns.1 = (f32[5,32,128]{2,1,0:T(8,128)S(1)}, f32[5,32,128]{2,1,0:T(8,128)S(1)}, f32[8,128]{1,0:T(8,128)S(1)}) custom-call(f32[4,32,32,128]{3,2,1,0:T(8,128)S(1)} %copy-done, f32[40,128]{1,0:T(8,128)S(1)} %pad.4.depth), custom_call_target="tpu_custom_call" | custom-call | tf_op jit(solution)/shard_map/columns/pallas_call | solution.py:451
  2.3 0.5 %collective-permute-start = (f32[5,32,128]{2,1,0:T(8,128)S(1)}, f32[5,32,128]{2,1,0:T(8,128)S(1)}, u32[]{:S(2)}, u32[]{:S(2)}) collective-permute-start(f32[5,32,128]{2,1,0:T(8,128)S(1)} %get-tuple-element.14), channel_id=1, source_target_pairs={{0,2},{1,3},{2,0},{3,1},{4,6},{5,7},{6,4},{7,5},{8,10},{9,11},{10,... | collective-permute-start | bytes 245768 | tf_op jit(solution)/shard_map/ppermute | solution.py:420
  2.8 5.7 %collective-permute-start.1 = (f32[5,32,128]{2,1,0:T(8,128)S(1)}, f32[5,32,128]{2,1,0:T(8,128)S(1)}, u32[]{:S(2)}, u32[]{:S(2)}) collective-permute-start(f32[5,32,128]{2,1,0:T(8,128)S(1)} %get-tuple-element.15), channel_id=1, source_target_pairs={{0,30},{1,31},{2,4},{3,5},{4,2},{5,3},{6,8},{7,9},{8,6},{9,7},{10,... | collective-permute-start | bytes 245768 | tf_op jit(solution)/shard_map/ppermute | solution.py:420
  8.5 0.0 collective-permute-done.ra
  8.5 0.1 far.1
  8.6 0.1 collective-permute-start.3
  8.7 1.9 %collective-permute-done.1.rb = f32[5,32,128]{2,1,0:T(8,128)S(1)} collective-permute-done((f32[5,32,128]{2,1,0:T(8,128)S(1)}, f32[5,32,128]{2,1,0:T(8,128)S(1)}, u32[]{:S(2)}, u32[]{:S(2)}) %collective-permute-start.1) | collective-permute-done | bytes 81952 | tf_op jit(solution)/shard_map/ppermute | solution.py:420
  10.6 0.1 near.1
  10.8 1.6 %collective-permute-start.2 = (f32[66,8,128]{2,1,0:T(8,128)S(1)}, f32[66,8,128]{2,1,0:T(8,128)S(1)}, u32[]{:S(2)}, u32[]{:S(2)}) collective-permute-start(f32[66,8,128]{2,1,0:T(8,128)S(1)} %near.1), channel_id=1, source_target_pairs={{0,1},{1,0},{2,3},{3,2},{4,5},{5,4},{6,7},{7,6},{8,9},{9,8},{10,11... | collective-permute-start | bytes 811016 | tf_op jit(solution)/shard_map/ppermute | solution.py:420
  12.3 0.5 %collective-permute-start.4 = (f32[8,128]{1,0:T(8,128)S(1)}, f32[8,128]{1,0:T(8,128)S(1)}, u32[]{:S(2)}, u32[]{:S(2)}) collective-permute-start(f32[8,128]{1,0:T(8,128)S(1)} %get-tuple-element.16.own_cb), channel_id=1, source_target_pairs={{0,1},{1,0},{2,4},{3,27},{4,2},{5,29},{6,8},{7,23},{8,6},{9,25},{1... | collective-permute-start | bytes 12296 | tf_op jit(solution)/shard_map/ppermute | solution.py:420
  12.8 5.8 %inner.1 = (f32[4,32,40,128]{3,2,1,0:T(8,128)S(1)}, f32[4,32,40,128]{3,2,1,0:T(8,128)S(1)}, f32[4,32,36,128]{3,2,1,0:T(8,128)S(1)}, f32[4,32,36,128]{3,2,1,0:T(8...) custom-call(f32[4,32,32,128]{3,2,1,0:T(8,128)S(1)} %copy-done, f32[40,128]{1,0:T(8,128)S(1)} %pad.4.depth, ...), custom_call_target="tpu_custom_call" | custom-call | tf_op jit(solution)/shard_map/inner/pallas_call | solution.py:472
  18.7 0.0 collective-permute-done.2.p.p1
  18.7 2.3 %south.1 = f32[4,32,8,128]{3,2,1,0:T(8,128)S(1)} custom-call(f32[66,8,128]{2,1,0:T(8,128)S(1)} %collective-permute-done.2.p.p1, f32[40,128]{1,0:T(8,128)S(1)} %pad.4.depth, f32[40,128]{1,0:T(8,128)S(1)} %get-tuple-element.17.side_depth, f32[4,32,40,128]{3,2,1,0:T(8,128)S(1)} %get-tuple-element.18.main0, f32[4,32,40,128]{3,2,1,0:T(8,128)S(1)} %get-tuple-element.19.side0, ...), custom_call_target="tpu_custom_call" | custom-call | tf_op jit(solution)/shard_map/south/pallas_call | solution.py:482
  21.0 0.0 collective-permute-done.4.cb
  21.1 0.0 collective-permute-done.3.p2
  21.1 2.9 %north.1 = f32[4,32,32,128]{3,2,1,0:T(8,128)} custom-call(f32[66,8,128]{2,1,0:T(8,128)S(1)} %collective-permute-done.2.p.p1, f32[68,8,128]{2,1,0:T(8,128)S(1)} %collective-permute-done.3.p2, f32[8,128]{1,0:T(8,128)S(1)} %collective-permute-done.4.cb, f32[8,128]{1,0:T(8,128)S(1)} %get-tuple-element.16.own_cb, f32[40,128]{1,0:T(8,128)S(1)} %pad.4.depth, ...), custom_call_target="tpu_custom_call" | custom-call | tf_op jit(solution)/shard_map/north/pallas_call | solution.py:491
  (4 shorter events, 0.0 us)
Async XLA Ops:
  0.0 0.7 %copy-start.1 = (s32[32,128]{1,0:T(8,128)S(1)}, s32[32,128]{1,0:T(8,128)}, u32[]{:S(2)}) copy-start(s32[32,128]{1,0:T(8,128)} %param.5) | copy-start | bytes 49156
  0.0 0.7 %copy-start.2 = (s32[32,128]{1,0:T(8,128)S(1)}, s32[32,128]{1,0:T(8,128)}, u32[]{:S(2)}) copy-start(s32[32,128]{1,0:T(8,128)} %param.4) | copy-start | bytes 49156
  0.0 1.6 %copy-start = (f32[4,32,32,128]{3,2,1,0:T(8,128)S(1)}, f32[4,32,32,128]{3,2,1,0:T(8,128)}, u32[]{:S(2)}) copy-start(f32[4,32,32,128]{3,2,1,0:T(8,128)} %state.7) | copy-start | bytes 6291460
  2.3 6.2 %collective-permute-start = (f32[5,32,128]{2,1,0:T(8,128)S(1)}, f32[5,32,128]{2,1,0:T(8,128)S(1)}, u32[]{:S(2)}, u32[]{:S(2)}) collective-permute-start(f32[5,32,128]{2,1,0:T(8,128)S(1)} %get-tuple-element.14), channel_id=1, source_target_pairs={{0,2},{1,3},{2,0},{3,1},{4,6},{5,7},{6,4},{7,5},{8,10},{9,11},{10,... | collective-permute-start | bytes 245768 | tf_op jit(solution)/shard_map/ppermute | solution.py:420
  2.8 7.8 %collective-permute-start.1 = (f32[5,32,128]{2,1,0:T(8,128)S(1)}, f32[5,32,128]{2,1,0:T(8,128)S(1)}, u32[]{:S(2)}, u32[]{:S(2)}) collective-permute-start(f32[5,32,128]{2,1,0:T(8,128)S(1)} %get-tuple-element.15), channel_id=1, source_target_pairs={{0,30},{1,31},{2,4},{3,5},{4,2},{5,3},{6,8},{7,9},{8,6},{9,7},{10,... | collective-permute-start | bytes 245768 | tf_op jit(solution)/shard_map/ppermute | solution.py:420
  8.6 12.4 %collective-permute-start.3 = (f32[68,8,128]{2,1,0:T(8,128)S(1)}, f32[68,8,128]{2,1,0:T(8,128)S(1)}, u32[]{:S(2)}, u32[]{:S(2)}) collective-permute-start(f32[68,8,128]{2,1,0:T(8,128)S(1)} %far.1), channel_id=1, source_target_pairs={{0,2},{1,31},{2,0},{3,29},{4,6},{5,27},{6,4},{7,25},{8,10},{9,23},... | collective-permute-start | bytes 835592 | tf_op jit(solution)/shard_map/ppermute | solution.py:420
  10.8 7.9 %collective-permute-start.2 = (f32[66,8,128]{2,1,0:T(8,128)S(1)}, f32[66,8,128]{2,1,0:T(8,128)S(1)}, u32[]{:S(2)}, u32[]{:S(2)}) collective-permute-start(f32[66,8,128]{2,1,0:T(8,128)S(1)} %near.1), channel_id=1, source_target_pairs={{0,1},{1,0},{2,3},{3,2},{4,5},{5,4},{6,7},{7,6},{8,9},{9,8},{10,11... | collective-permute-start | bytes 811016 | tf_op jit(solution)/shard_map/ppermute | solution.py:420
  12.3 8.7 %collective-permute-start.4 = (f32[8,128]{1,0:T(8,128)S(1)}, f32[8,128]{1,0:T(8,128)S(1)}, u32[]{:S(2)}, u32[]{:S(2)}) collective-permute-start(f32[8,128]{1,0:T(8,128)S(1)} %get-tuple-element.16.own_cb), channel_id=1, source_target_pairs={{0,1},{1,0},{2,4},{3,27},{4,2},{5,29},{6,8},{7,23},{8,6},{9,25},{1... | collective-permute-start | bytes 12296 | tf_op jit(solution)/shard_map/ppermute | solution.py:420

commit v6 on v5

--- a/solution.py
+++ b/solution.py
@@ -17,6 +17,7 @@
 haline = 0.8
 
 F32 = jnp.float32
+PARTS = 4
 VM = pl.BlockSpec(memory_space=pltpu.VMEM)
 HB = pl.BlockSpec(memory_space=pltpu.HBM)
 
@@ -58,12 +59,13 @@
 
 
 def edge_rows(strip, f, r):
-    rows = strip.shape[1]
+    rows = (strip.shape[0] - 8) // 4
+    base = f * rows
     band = lax.axis_index("lat")
     band_even = band % 2 == 0
     is_top = band == lax.axis_size("lat") - 1
-    south, north = strip[f, r:r + 1, :], strip[f, rows - 2 + r:rows - 1 + r, :]
-    folded = strip[f, rows - 1 - r:rows - r, :]
+    south, north = strip[base + r:base + r + 1, :], strip[base + rows - 2 + r:base + rows - 1 + r, :]
+    folded = strip[base + rows - 1 - r:base + rows - r, :]
     return jnp.where(band_even, north, south), jnp.where(band_even, south, jnp.where(is_top, folded, north))
 
 
@@ -145,14 +147,17 @@
         accs = lax.fori_loop(0, levels, body, (zero,) * (4 * groups), unroll=32)
         for j in range(2):
             for g in range(groups):
-                at = slice(8 * g, 8 * g + 8)
+                at = slice((2 * pair + j) * rows + 8 * g, (2 * pair + j) * rows + 8 * g + 8)
                 east, west = accs[2 * (j * groups + g)], accs[2 * (j * groups + g) + 1]
-                la[2 * pair + j, at, :] = jnp.where(lon_even, east, west)
-                lb[2 * pair + j, at, :] = jnp.where(lon_even, west, east)
+                la[at, :] = jnp.where(lon_even, east, west)
+                lb[at, :] = jnp.where(lon_even, west, east)
+    east = west = zero
     for g in range(groups):
-        turned = pltpu.roll(deeps[g], 4, 1)
-        la[4, 8 * g:8 * g + 8, :] = turned
-        lb[4, 8 * g:8 * g + 8, :] = turned
+        turned = pltpu.roll(deeps[g], 4 * g + 4, 1)
+        east = jnp.where(group == g, turned, east)
+        west = jnp.where(group == g + 1, turned, west)
+    la[4 * rows:4 * rows + 8, :] = jnp.where(lon_even, east, west)
+    lb[4 * rows:4 * rows + 8, :] = jnp.where(lon_even, west, east)
     for f in range(4):
         for r in range(2):
             cb[2 * f + r:2 * f + r + 1, :] = edge_rows(lb, f, r)[1]
@@ -164,7 +169,7 @@
     return 0.2 + 0.8 * ((row.astype(F32) + 0.5) / total)
 
 
-def sweep(table, levels, jobs, scale, leave=1.0, unroll=8, unroll_back=8):
+def sweep(table, levels, jobs, scale, leave=1.0, unroll=8, unroll_back=8, parts=1, ready=None):
     lane = lanes()
     zero = jnp.zeros((8, 128), F32)
     jobs = [job if len(job) == 9 else (*job, 1, job[2]) for job in jobs]
@@ -185,7 +190,7 @@
             prov = []
             near = []
             for f in range(4):
-                x = other[f, k, at:at + 8, :]
+                x = other(f, k) if callable(other) else other[f, k, at:at + 8, :]
                 e1 = pltpu.roll(jnp.where(lane == 0, x, q[f]), 127, 1)
                 e2 = pltpu.roll(jnp.where(lane < 2, x, q[f]), 126, 1)
                 w1 = pltpu.roll(jnp.where(lane == 127, x, q[f]), 1, 1)
@@ -229,7 +234,12 @@
                 out.append(value)
         return tuple(out)
 
-    lax.fori_loop(0, levels, backward, (zero,) * (4 * len(jobs)), unroll=unroll_back)
+    carry = (zero,) * (4 * len(jobs))
+    size = levels // parts
+    for n in range(parts):
+        carry = lax.fori_loop(n * size, (n + 1) * size, backward, carry, unroll=min(unroll_back, size))
+        if ready is not None:
+            ready(n, levels - (n + 1) * size, size)
 
 
 def side_tile(east, west, group, k):
@@ -246,17 +256,16 @@
     group = lanes() >> 2
     zero = jnp.zeros((8, 128), F32)
 
-    for f in range(5):
-        for g in range(groups):
-            at = slice(8 * g, 8 * g + 8)
-            a, b = ra[f, at, :], rb[f, at, :]
-            easts[f, at, :] = jnp.where(lon_even, a, b)
-            wests[f, at, :] = jnp.where(lon_even, b, a)
+    for n in range(ra.shape[0] // 8):
+        at = slice(8 * n, 8 * n + 8)
+        a, b = ra[at, :], rb[at, :]
+        easts[at, :] = jnp.where(lon_even, a, b)
+        wests[at, :] = jnp.where(lon_even, b, a)
     side_depth[0:8, :] = zero
     side_depth[rows:rows + 8, :] = zero
     for g in range(groups):
-        at = slice(8 * g, 8 * g + 8)
-        side_depth[8 * g + 4:8 * g + 12, :] = side_tile(easts[4, at, :], wests[4, at, :], group, 0)
+        at = slice(4 * rows, 4 * rows + 8)
+        side_depth[8 * g + 4:8 * g + 12, :] = side_tile(easts[at, :], wests[at, :], group, g)
 
     def fill(k, unused):
         level = k.astype(F32)
@@ -266,7 +275,8 @@
             is_wet = level < depth[to, :]
             for f in range(4):
                 main0[f, k, to, :] = jnp.where(is_wet, state[f, k, at, :], 0.0)
-                side0[f, k, to, :] = side_tile(easts[f, at, :], wests[f, at, :], group, k)
+                of = slice(f * rows + 8 * g, f * rows + 8 * g + 8)
+                side0[f, k, to, :] = side_tile(easts[of, :], wests[of, :], group, k)
         return unused
 
     lax.fori_loop(0, levels, fill, 0, unroll=32)
@@ -322,7 +332,7 @@
 
 
 def north_kernel(p1, p2, cb, own_cb, depth, side_depth, main0, side0, main1, side1, middle, south, out,
-                 pair0, facing0, pair1, rim1, edge1, last, depths, table, sems):
+                 pair0, pair1, rim1, edge1, last, depths, table, sems):
     levels, rows = main0.shape[1], out.shape[2]
     done = [
         pltpu.make_async_copy(middle, out.at[:, :, 8:rows - 8, :], sems.at[0]),
@@ -373,14 +383,16 @@
                 pair0[f, k, turns(1, 4), :] = main0[f, k, rows:rows + 4, :]
                 pair0[f, k, turns(9, 4), :] = rim[4 * j:4 * j + 4, :]
                 pair0[f, k, turns(12, 2), :] = corners[2 * f:2 * f + 2, :]
-                facing0[f, k, turns(0, 4), :] = main0[f, k, rows:rows + 4, :]
-                facing0[f, k, turns(1, 2), :] = side0[f, k, rows + 2:rows + 4, :]
-                facing0[f, k, turns(5, 2), :] = corners[2 * f:2 * f + 2, :]
         return unused
 
     lax.fori_loop(0, levels, fill, 0, unroll=32)
     cor = coriolis_rows(first_row + (rows - 4), total, (sublanes() >> 1) + 2 * (sublanes() & 1))
-    sweep(table, levels, [(pair0, facing0, 4, depths[...], cor, pair1, 0, 2, 0)], 1.0, 1.0, 32, 32)
+    first_turn = sublanes() & 1 == 0
+
+    def facing(f, k):
+        return jnp.where(first_turn, pair0[f, k, 1:9, :], pair0[f, k, 7:15, :])
+
+    sweep(table, levels, [(pair0, facing, 4, depths[...], cor, pair1, 0, 2, 0)], 1.0, 1.0, 32, 32)
 
     def split(k, unused):
         for f in range(4):
@@ -392,12 +404,16 @@
 
     lax.fori_loop(0, levels, split, 0, unroll=16)
     cor = coriolis_rows(first_row + (rows - 8), total)
-    sweep(table, levels, [(rim1, edge1, 2, depth[rows - 4:rows + 4, :], cor, last, 0, 1, 0)], GAIN, 1.0 / GAIN**2, 32, 32)
-    copy = pltpu.make_async_copy(last, out.at[:, :, rows - 8:rows, :], sems.at[2])
-    copy.start()
-    for other in done:
-        other.wait()
-    copy.wait()
+
+    def send(n, k, size):
+        done.append(pltpu.make_async_copy(
+            last.at[:, k:k + size], out.at[:, k:k + size, rows - 8:rows, :], sems.at[2 + n]))
+        done[-1].start()
+
+    sweep(table, levels, [(rim1, edge1, 2, depth[rows - 4:rows + 4, :], cor, last, 0, 1, 0)],
+          GAIN, 1.0 / GAIN**2, 32, 32, PARTS, send)
+    for copy in done:
+        copy.wait()
 
 
 def per_device(state, land_mask, wet_levels):
@@ -441,7 +457,7 @@
     shape = lambda *dims: jax.ShapeDtypeStruct(dims, F32)
     block = lambda n: shape(fields, levels, n, 128)
     room = lambda n: pltpu.VMEM((fields, levels, n, 128), F32)
-    strip = shape(5, rows, 128)
+    strip = shape(4 * rows + 8, 128)
     top = call(
         functools.partial(limit_kernel, levels), 4, out_shape=shape(8, 128), out_specs=VM, name="limit",
         cost_estimate=pl.CostEstimate(flops=10**10, bytes_accessed=4096, transcendentals=0),
@@ -456,7 +472,7 @@
     rb = swap(lb, lambda i, b: (beyond(i), b))
     rcb = swap(cb, far_beyond)
     p2 = call(
-        far_kernel, 4, out_shape=shape(2 * levels + 4, 8, 128), in_specs=[VM] * 3, out_specs=VM, name="far",
+        far_kernel, 4, out_shape=shape(2 * levels + 3, 8, 128), in_specs=[VM] * 3, out_specs=VM, name="far",
     )(state, depth, ra)
     rp2 = swap(p2, far)
     p1 = call(
@@ -476,7 +492,7 @@
                    block(rows - 16)),
         in_specs=[VM] * 4,
         out_specs=(VM,) * 6,
-        scratch_shapes=[pltpu.VMEM((5, rows, 128), F32), pltpu.VMEM((5, rows, 128), F32), room_table],
+        scratch_shapes=[pltpu.VMEM((4 * rows + 8, 128), F32), pltpu.VMEM((4 * rows + 8, 128), F32), room_table],
         name="inner",
     )(state, depth, ra, rb)
     first = call(
@@ -494,8 +510,8 @@
         out_shape=shape(*state.shape),
         in_specs=[VM] * 12,
         out_specs=HB,
-        scratch_shapes=[room(16), room(8), room(8), room(16), room(8), room(8), pltpu.VMEM((8, 128), F32), room_table,
-                        pltpu.SemaphoreType.DMA((3,))],
+        scratch_shapes=[room(16), room(8), room(16), room(8), room(8), pltpu.VMEM((8, 128), F32), room_table,
+                        pltpu.SemaphoreType.DMA((2 + PARTS,))],
         name="north",
     )(rp1, rp2, rcb, cb, depth, side_depth, main0, side0, main1, side1, last, first)
 

time: 24.2 us -> 24 us (level)
  transfers between devices with their start and end apart: 5 -> 5, of which waited for: 1 -> 1; matrix products, arithmetic and copies ran while one was open for 0% -> 0% of each run, Pallas kernels for 35% -> 36%
where the time goes in v6:
time: 24 us; the launch traced here: 23.8 us
  Pallas kernels  11.9 us (50%)
  starting transfers between devices  8.35 us (35%)
  waiting for transfers between devices  1.8 us (8%)
  local copies, waits for them, and re-layouts  1.61 us (7%)
    ppermute x5, starting transfers between devices, swap(): return lax.ppermute(x, ('lon', 'lat'), pairs)  8.35 us
    pallas_call x1, Pallas kernels, per_device(): call(inner_kernel, 6, out_shape=(block(rows + 8), block(rows + 8), block(...  5.94 us
    pallas_call x1, Pallas kernels, per_device(): call(north_kernel, 12, out_shape=shape(*state.shape), in_specs=[VM] * 12,...  2.75 us
    pallas_call x1, Pallas kernels, per_device(): call(south_kernel, 10, out_shape=block(8), in_specs=[VM] * 7, out_specs=V...  2.33 us
    ppermute x5, waiting for transfers between devices, swap(): return lax.ppermute(x, ('lon', 'lat'), pairs)  1.8 us
    unnamed x6, local copies, waits for them, and re-layouts  1.6 us
    pallas_call x1, Pallas kernels, per_device(): call(columns_kernel, 4, out_shape=(strip, strip, shape(8, 128)), in_specs...  0.68 us
  transfers between devices with their start and end apart: 5, of which 1 were waited for; matrix products, arithmetic and copies ran while one was open for 0% of the time, Pallas kernels for 36%

profile of v6, /device:TPU:0, one launch (start us, length us, event | category | flops | bytes accessed | tf_op | source)
XLA Modules:
  0.0 23.8 jit_solution(8808537898460025719)
XLA Ops:
  0.0 0.0 copy-start.1
  0.0 0.0 copy-start.2
  0.0 0.0 copy-start
  0.0 0.7 %copy-done.1 = s32[32,128]{1,0:T(8,128)S(1)} copy-done((s32[32,128]{1,0:T(8,128)S(1)}, s32[32,128]{1,0:T(8,128)}, u32[]{:S(2)}) %copy-start.1) | copy-done | bytes 16408
  0.7 0.0 copy-done.2
  0.7 0.9 %copy-done = f32[4,32,32,128]{3,2,1,0:T(8,128)S(1)} copy-done((f32[4,32,32,128]{3,2,1,0:T(8,128)S(1)}, f32[4,32,32,128]{3,2,1,0:T(8,128)}, u32[]{:S(2)}) %copy-start) | copy-done | bytes 2097176
  1.6 0.7 %columns.1 = (f32[136,128]{1,0:T(8,128)S(1)}, f32[136,128]{1,0:T(8,128)S(1)}, f32[8,128]{1,0:T(8,128)S(1)}) custom-call(f32[4,32,32,128]{3,2,1,0:T(8,128)S(1)} %copy-done, f32[40,128]{1,0:T(8,128)S(1)} %pad.4.depth), custom_call_target="tpu_custom_call" | custom-call | tf_op jit(solution)/shard_map/columns/pallas_call | solution.py:467
  2.3 0.5 %collective-permute-start = (f32[136,128]{1,0:T(8,128)S(1)}, f32[136,128]{1,0:T(8,128)S(1)}, u32[]{:S(2)}, u32[]{:S(2)}) collective-permute-start(f32[136,128]{1,0:T(8,128)S(1)} %get-tuple-element.14), channel_id=1, source_target_pairs={{0,2},{1,3},{2,0},{3,1},{4,6},{5,7},{6,4},{7,5},{8,10},{9,11},{10,... | collective-permute-start | bytes 208904 | tf_op jit(solution)/shard_map/ppermute | solution.py:436
  2.8 5.7 %collective-permute-start.1 = (f32[136,128]{1,0:T(8,128)S(1)}, f32[136,128]{1,0:T(8,128)S(1)}, u32[]{:S(2)}, u32[]{:S(2)}) collective-permute-start(f32[136,128]{1,0:T(8,128)S(1)} %get-tuple-element.15), channel_id=1, source_target_pairs={{0,30},{1,31},{2,4},{3,5},{4,2},{5,3},{6,8},{7,9},{8,6},{9,7},{10,... | collective-permute-start | bytes 208904 | tf_op jit(solution)/shard_map/ppermute | solution.py:436
  8.5 0.0 collective-permute-done.ra
  8.5 0.1 far.1
  8.6 0.1 collective-permute-start.3
  8.7 1.8 %collective-permute-done.1.rb = f32[136,128]{1,0:T(8,128)S(1)} collective-permute-done((f32[136,128]{1,0:T(8,128)S(1)}, f32[136,128]{1,0:T(8,128)S(1)}, u32[]{:S(2)}, u32[]{:S(2)}) %collective-permute-start.1) | collective-permute-done | bytes 69664 | tf_op jit(solution)/shard_map/ppermute | solution.py:436
  10.5 0.1 near.1
  10.6 1.6 %collective-permute-start.2 = (f32[66,8,128]{2,1,0:T(8,128)S(1)}, f32[66,8,128]{2,1,0:T(8,128)S(1)}, u32[]{:S(2)}, u32[]{:S(2)}) collective-permute-start(f32[66,8,128]{2,1,0:T(8,128)S(1)} %near.1), channel_id=1, source_target_pairs={{0,1},{1,0},{2,3},{3,2},{4,5},{5,4},{6,7},{7,6},{8,9},{9,8},{10,11... | collective-permute-start | bytes 811016 | tf_op jit(solution)/shard_map/ppermute | solution.py:436
  12.2 0.5 %collective-permute-start.4 = (f32[8,128]{1,0:T(8,128)S(1)}, f32[8,128]{1,0:T(8,128)S(1)}, u32[]{:S(2)}, u32[]{:S(2)}) collective-permute-start(f32[8,128]{1,0:T(8,128)S(1)} %get-tuple-element.16.own_cb), channel_id=1, source_target_pairs={{0,1},{1,0},{2,4},{3,27},{4,2},{5,29},{6,8},{7,23},{8,6},{9,25},{1... | collective-permute-start | bytes 12296 | tf_op jit(solution)/shard_map/ppermute | solution.py:436
  12.7 5.9 %inner.1 = (f32[4,32,40,128]{3,2,1,0:T(8,128)S(1)}, f32[4,32,40,128]{3,2,1,0:T(8,128)S(1)}, f32[4,32,36,128]{3,2,1,0:T(8,128)S(1)}, f32[4,32,36,128]{3,2,1,0:T(8...) custom-call(f32[4,32,32,128]{3,2,1,0:T(8,128)S(1)} %copy-done, f32[40,128]{1,0:T(8,128)S(1)} %pad.4.depth, ...), custom_call_target="tpu_custom_call" | custom-call | tf_op jit(solution)/shard_map/inner/pallas_call | solution.py:488
  18.7 0.0 collective-permute-done.2.p.p1
  18.7 2.3 %south.1 = f32[4,32,8,128]{3,2,1,0:T(8,128)S(1)} custom-call(f32[66,8,128]{2,1,0:T(8,128)S(1)} %collective-permute-done.2.p.p1, f32[40,128]{1,0:T(8,128)S(1)} %pad.4.depth, f32[40,128]{1,0:T(8,128)S(1)} %get-tuple-element.17.side_depth, f32[4,32,40,128]{3,2,1,0:T(8,128)S(1)} %get-tuple-element.18.main0, f32[4,32,40,128]{3,2,1,0:T(8,128)S(1)} %get-tuple-element.19.side0, ...), custom_call_target="tpu_custom_call" | custom-call | tf_op jit(solution)/shard_map/south/pallas_call | solution.py:498
  21.0 0.0 collective-permute-done.4.cb
  21.0 0.0 collective-permute-done.3.p2
  21.0 2.7 %north.1 = f32[4,32,32,128]{3,2,1,0:T(8,128)} custom-call(f32[66,8,128]{2,1,0:T(8,128)S(1)} %collective-permute-done.2.p.p1, f32[67,8,128]{2,1,0:T(8,128)S(1)} %collective-permute-done.3.p2, f32[8,128]{1,0:T(8,128)S(1)} %collective-permute-done.4.cb, f32[8,128]{1,0:T(8,128)S(1)} %get-tuple-element.16.own_cb, f32[40,128]{1,0:T(8,128)S(1)} %pad.4.depth, ...), custom_call_target="tpu_custom_call" | custom-call | tf_op jit(solution)/shard_map/north/pallas_call | solution.py:507
  (4 shorter events, 0.0 us)
Async XLA Ops:
  0.0 0.7 %copy-start.1 = (s32[32,128]{1,0:T(8,128)S(1)}, s32[32,128]{1,0:T(8,128)}, u32[]{:S(2)}) copy-start(s32[32,128]{1,0:T(8,128)} %param.5) | copy-start | bytes 49156
  0.0 0.7 %copy-start.2 = (s32[32,128]{1,0:T(8,128)S(1)}, s32[32,128]{1,0:T(8,128)}, u32[]{:S(2)}) copy-start(s32[32,128]{1,0:T(8,128)} %param.4) | copy-start | bytes 49156
  0.0 1.6 %copy-start = (f32[4,32,32,128]{3,2,1,0:T(8,128)S(1)}, f32[4,32,32,128]{3,2,1,0:T(8,128)}, u32[]{:S(2)}) copy-start(f32[4,32,32,128]{3,2,1,0:T(8,128)} %state.7) | copy-start | bytes 6291460
  2.3 6.2 %collective-permute-start = (f32[136,128]{1,0:T(8,128)S(1)}, f32[136,128]{1,0:T(8,128)S(1)}, u32[]{:S(2)}, u32[]{:S(2)}) collective-permute-start(f32[136,128]{1,0:T(8,128)S(1)} %get-tuple-element.14), channel_id=1, source_target_pairs={{0,2},{1,3},{2,0},{3,1},{4,6},{5,7},{6,4},{7,5},{8,10},{9,11},{10,... | collective-permute-start | bytes 208904 | tf_op jit(solution)/shard_map/ppermute | solution.py:436
  2.8 7.7 %collective-permute-start.1 = (f32[136,128]{1,0:T(8,128)S(1)}, f32[136,128]{1,0:T(8,128)S(1)}, u32[]{:S(2)}, u32[]{:S(2)}) collective-permute-start(f32[136,128]{1,0:T(8,128)S(1)} %get-tuple-element.15), channel_id=1, source_target_pairs={{0,30},{1,31},{2,4},{3,5},{4,2},{5,3},{6,8},{7,9},{8,6},{9,7},{10,... | collective-permute-start | bytes 208904 | tf_op jit(solution)/shard_map/ppermute | solution.py:436
  8.6 12.4 %collective-permute-start.3 = (f32[67,8,128]{2,1,0:T(8,128)S(1)}, f32[67,8,128]{2,1,0:T(8,128)S(1)}, u32[]{:S(2)}, u32[]{:S(2)}) collective-permute-start(f32[67,8,128]{2,1,0:T(8,128)S(1)} %far.1), channel_id=1, source_target_pairs={{0,2},{1,31},{2,0},{3,29},{4,6},{5,27},{6,4},{7,25},{8,10},{9,23},... | collective-permute-start | bytes 823304 | tf_op jit(solution)/shard_map/ppermute | solution.py:436
  10.6 8.0 %collective-permute-start.2 = (f32[66,8,128]{2,1,0:T(8,128)S(1)}, f32[66,8,128]{2,1,0:T(8,128)S(1)}, u32[]{:S(2)}, u32[]{:S(2)}) collective-permute-start(f32[66,8,128]{2,1,0:T(8,128)S(1)} %near.1), channel_id=1, source_target_pairs={{0,1},{1,0},{2,3},{3,2},{4,5},{5,4},{6,7},{7,6},{8,9},{9,8},{10,11... | collective-permute-start | bytes 811016 | tf_op jit(solution)/shard_map/ppermute | solution.py:436
  12.2 8.8 %collective-permute-start.4 = (f32[8,128]{1,0:T(8,128)S(1)}, f32[8,128]{1,0:T(8,128)S(1)}, u32[]{:S(2)}, u32[]{:S(2)}) collective-permute-start(f32[8,128]{1,0:T(8,128)S(1)} %get-tuple-element.16.own_cb), channel_id=1, source_target_pairs={{0,1},{1,0},{2,4},{3,27},{4,2},{5,29},{6,8},{7,23},{8,6},{9,25},{1... | collective-permute-start | bytes 12296 | tf_op jit(solution)/shard_map/ppermute | solution.py:436

commit v7 on v6

--- a/solution.py
+++ b/solution.py
@@ -169,7 +169,7 @@
     return 0.2 + 0.8 * ((row.astype(F32) + 0.5) / total)
 
 
-def sweep(table, levels, jobs, scale, leave=1.0, unroll=8, unroll_back=8, parts=1, ready=None):
+def sweep(table, parted, levels, jobs, scale, leave=1.0, unroll=8, unroll_back=8, parts=1, ready=None):
     lane = lanes()
     zero = jnp.zeros((8, 128), F32)
     jobs = [job if len(job) == 9 else (*job, 1, job[2]) for job in jobs]
@@ -180,7 +180,7 @@
         inner, lowest = table[0, k], table[1, k]
         level = k.astype(F32)
         out = []
-        for n, (own, other, o, depth, _, dst, d, apart, at) in enumerate(jobs):
+        for n, (own, other, o, depth, _, _, _, apart, at) in enumerate(jobs):
             halves = carry[6 * n:6 * n + 4]
             sums = carry[6 * n + 4:6 * n + 6]
             weight = jnp.where(level < uppers[n], inner, jnp.where(level < depth, lowest, 0.0))
@@ -216,7 +216,7 @@
                 near.append(press + half)
             for f in range(4):
                 part = (prov[f] + halves[f]) * weight
-                dst[f, k, d:d + 8, :] = part
+                parted[n, f, k] = part
                 out.append(part)
             out += near[4:6]
         return tuple(out)
@@ -229,7 +229,7 @@
         out = []
         for n, (_, _, _, _, _, dst, d, _, _) in enumerate(jobs):
             for f in range(4):
-                value = dst[f, k, d:d + 8, :] + ratio * carry[4 * n + f]
+                value = parted[n, f, k] + ratio * carry[4 * n + f]
                 dst[f, k, d:d + 8, :] = value * leave if leave != 1.0 else value
                 out.append(value)
         return tuple(out)
@@ -246,7 +246,7 @@
     return pltpu.roll(jnp.where(group == k, west, east), (124 - 4 * k) & 127, 1)
 
 
-def inner_kernel(state, depth, ra, rb, main0, side0, side1, main1, side_depth, last, easts, wests, table):
+def inner_kernel(state, depth, ra, rb, main0, side0, side1, main1, side_depth, last, easts, wests, parted, table):
     levels, rows = state.shape[1], state.shape[2]
     groups = rows // 8
     lon_even = lax.axis_index("lon") % 2 == 0
@@ -287,15 +287,15 @@
         cor = coriolis_rows(first_row + (8 * w - 2), total)
         jobs.append((main0, side0, o, depth[o:o + 8, :], cor, main1, 8 * w))
         jobs.append((side0, main0, o, side_depth[o:o + 8, :], cor, side1, 8 * w))
-    sweep(table, levels, jobs, 1.0, 1.0, 16, 8)
+    sweep(table, parted, levels, jobs, 1.0, 1.0, 16, 32)
     jobs = []
     for w in range(1, groups - 1):
         cor = coriolis_rows(first_row + 8 * w, total)
         jobs.append((main1, side1, 8 * w + 2, depth[8 * w + 4:8 * w + 12, :], cor, last, 8 * w - 8))
-    sweep(table, levels, jobs, GAIN, 1.0 / GAIN**2, 32, 16)
-
-
-def south_kernel(p, depth, side_depth, main0, side0, main1, side1, last, rim0, edge0, rim1, edge1, table):
+    sweep(table, parted, levels, jobs, GAIN, 1.0 / GAIN**2, 32, 32)
+
+
+def south_kernel(p, depth, side_depth, main0, side0, main1, side1, last, rim0, edge0, rim1, edge1, parted, table):
     levels = main0.shape[1]
     rows = depth.shape[0] - 8
     first_row = lax.axis_index("lat") * rows
@@ -323,16 +323,16 @@
 
     lax.fori_loop(0, levels, fill, 0, unroll=32)
     cor = coriolis_rows(first_row - 2, total)
-    sweep(table, levels, [
+    sweep(table, parted, levels, [
         (rim0, edge0, 2, depths, cor, rim1, 0),
         (edge0, rim0, 2, side_depth[2:10, :], cor, edge1, 0),
     ], 1.0, 1.0, 32, 16)
     cor = coriolis_rows(first_row, total)
-    sweep(table, levels, [(rim1, edge1, 2, depth[4:12, :], cor, last, 0)], GAIN, 1.0 / GAIN**2, 32, 16)
+    sweep(table, parted, levels, [(rim1, edge1, 2, depth[4:12, :], cor, last, 0)], GAIN, 1.0 / GAIN**2, 32, 32)
 
 
 def north_kernel(p1, p2, cb, own_cb, depth, side_depth, main0, side0, main1, side1, middle, south, out,
-                 pair0, pair1, rim1, edge1, last, depths, table, sems):
+                 pair0, pair1, rim1, edge1, last, depths, parted, table, sems):
     levels, rows = main0.shape[1], out.shape[2]
     done = [
         pltpu.make_async_copy(middle, out.at[:, :, 8:rows - 8, :], sems.at[0]),
@@ -392,7 +392,7 @@
     def facing(f, k):
         return jnp.where(first_turn, pair0[f, k, 1:9, :], pair0[f, k, 7:15, :])
 
-    sweep(table, levels, [(pair0, facing, 4, depths[...], cor, pair1, 0, 2, 0)], 1.0, 1.0, 32, 32)
+    sweep(table, parted, levels, [(pair0, facing, 4, depths[...], cor, pair1, 0, 2, 0)], 1.0, 1.0, 32, 32)
 
     def split(k, unused):
         for f in range(4):
@@ -410,7 +410,7 @@
             last.at[:, k:k + size], out.at[:, k:k + size, rows - 8:rows, :], sems.at[2 + n]))
         done[-1].start()
 
-    sweep(table, levels, [(rim1, edge1, 2, depth[rows - 4:rows + 4, :], cor, last, 0, 1, 0)],
+    sweep(table, parted, levels, [(rim1, edge1, 2, depth[rows - 4:rows + 4, :], cor, last, 0, 1, 0)],
           GAIN, 1.0 / GAIN**2, 32, 32, PARTS, send)
     for copy in done:
         copy.wait()
@@ -484,15 +484,17 @@
         same = jnp.where((jnp.arange(128) % 4 < 2) == (lon % 2 == 0), rp2[2 * levels + 1], rcb)
         south = jnp.where(lat % 2 == 0, rp2[:2 * levels + 2].at[2 * levels + 1].set(same), rp1)
 
+    window = lambda n: pltpu.VMEM((n, fields, levels, 8, 128), F32)
     room_table = pltpu.SMEM((2, levels), F32)
     main0, side0, side1, main1, side_depth, last = call(
         inner_kernel,
-        6,
+        10,
         out_shape=(block(rows + 8), block(rows + 8), block(rows + 4), block(rows + 4), shape(rows + 8, 128),
                    block(rows - 16)),
         in_specs=[VM] * 4,
         out_specs=(VM,) * 6,
-        scratch_shapes=[pltpu.VMEM((4 * rows + 8, 128), F32), pltpu.VMEM((4 * rows + 8, 128), F32), room_table],
+        scratch_shapes=[pltpu.VMEM((4 * rows + 8, 128), F32), pltpu.VMEM((4 * rows + 8, 128), F32),
+                        window(rows // 4 - 2), room_table],
         name="inner",
     )(state, depth, ra, rb)
     first = call(
@@ -501,7 +503,7 @@
         out_shape=block(8),
         in_specs=[VM] * 7,
         out_specs=VM,
-        scratch_shapes=[room(16)] * 4 + [room_table],
+        scratch_shapes=[room(16)] * 4 + [window(2), room_table],
         name="south",
     )(south, depth, side_depth, main0, side0, main1, side1)
     return call(
@@ -510,7 +512,7 @@
         out_shape=shape(*state.shape),
         in_specs=[VM] * 12,
         out_specs=HB,
-        scratch_shapes=[room(16), room(8), room(16), room(8), room(8), pltpu.VMEM((8, 128), F32), room_table,
+        scratch_shapes=[room(16), room(8), room(16), room(8), room(8), pltpu.VMEM((8, 128), F32), window(1), room_table,
                         pltpu.SemaphoreType.DMA((2 + PARTS,))],
         name="north",
     )(rp1, rp2, rcb, cb, depth, side_depth, main0, side0, main1, side1, last, first)

time: 24 us -> 23.4 us (0.975)
  Pallas kernels: 11.9 us -> 11.3 us
    pallas_call x1, Pallas kernels: 5.94 us -> 5.63 us  [per_device(): call(inner_kernel, 10, out_shape=(block(rows + 8), block(rows + 8), block...]
  transfers between devices with their start and end apart: 5 -> 5, of which waited for: 1 -> 1; matrix products, arithmetic and copies ran while one was open for 0% -> 0% of each run, Pallas kernels for 36% -> 35%
where the time goes in v7:
time: 23.4 us; the launch traced here: 23.2 us
  Pallas kernels  11.3 us (48%)
  starting transfers between devices  8.35 us (36%)
  waiting for transfers between devices  1.8 us (8%)
  local copies, waits for them, and re-layouts  1.61 us (7%)
    ppermute x5, starting transfers between devices, swap(): return lax.ppermute(x, ('lon', 'lat'), pairs)  8.35 us
    pallas_call x1, Pallas kernels, per_device(): call(inner_kernel, 10, out_shape=(block(rows + 8), block(rows + 8), block...  5.63 us
    pallas_call x1, Pallas kernels, per_device(): call(north_kernel, 12, out_shape=shape(*state.shape), in_specs=[VM] * 12,...  2.59 us
    pallas_call x1, Pallas kernels, per_device(): call(south_kernel, 10, out_shape=block(8), in_specs=[VM] * 7, out_specs=V...  2.21 us
    ppermute x5, waiting for transfers between devices, swap(): return lax.ppermute(x, ('lon', 'lat'), pairs)  1.8 us
    unnamed x6, local copies, waits for them, and re-layouts  1.6 us
    pallas_call x1, Pallas kernels, per_device(): call(columns_kernel, 4, out_shape=(strip, strip, shape(8, 128)), in_specs...  0.68 us
  transfers between devices with their start and end apart: 5, of which 1 were waited for; matrix products, arithmetic and copies ran while one was open for 0% of the time, Pallas kernels for 35%

profile of v7, /device:TPU:0, one launch (start us, length us, event | category | flops | bytes accessed | tf_op | source)
XLA Modules:
  0.0 23.2 jit_solution(14255167077133846502)
XLA Ops:
  0.0 0.0 copy-start.1
  0.0 0.0 copy-start.2
  0.0 0.0 copy-start
  0.0 0.7 %copy-done.1 = s32[32,128]{1,0:T(8,128)S(1)} copy-done((s32[32,128]{1,0:T(8,128)S(1)}, s32[32,128]{1,0:T(8,128)}, u32[]{:S(2)}) %copy-start.1) | copy-done | bytes 16408
  0.7 0.0 copy-done.2
  0.7 0.9 %copy-done = f32[4,32,32,128]{3,2,1,0:T(8,128)S(1)} copy-done((f32[4,32,32,128]{3,2,1,0:T(8,128)S(1)}, f32[4,32,32,128]{3,2,1,0:T(8,128)}, u32[]{:S(2)}) %copy-start) | copy-done | bytes 2097176
  1.6 0.7 %columns.1 = (f32[136,128]{1,0:T(8,128)S(1)}, f32[136,128]{1,0:T(8,128)S(1)}, f32[8,128]{1,0:T(8,128)S(1)}) custom-call(f32[4,32,32,128]{3,2,1,0:T(8,128)S(1)} %copy-done, f32[40,128]{1,0:T(8,128)S(1)} %pad.4.depth), custom_call_target="tpu_custom_call" | custom-call | tf_op jit(solution)/shard_map/columns/pallas_call | solution.py:467
  2.3 0.5 %collective-permute-start = (f32[136,128]{1,0:T(8,128)S(1)}, f32[136,128]{1,0:T(8,128)S(1)}, u32[]{:S(2)}, u32[]{:S(2)}) collective-permute-start(f32[136,128]{1,0:T(8,128)S(1)} %get-tuple-element.14), channel_id=1, source_target_pairs={{0,2},{1,3},{2,0},{3,1},{4,6},{5,7},{6,4},{7,5},{8,10},{9,11},{10,... | collective-permute-start | bytes 208904 | tf_op jit(solution)/shard_map/ppermute | solution.py:436
  2.8 5.7 %collective-permute-start.1 = (f32[136,128]{1,0:T(8,128)S(1)}, f32[136,128]{1,0:T(8,128)S(1)}, u32[]{:S(2)}, u32[]{:S(2)}) collective-permute-start(f32[136,128]{1,0:T(8,128)S(1)} %get-tuple-element.15), channel_id=1, source_target_pairs={{0,30},{1,31},{2,4},{3,5},{4,2},{5,3},{6,8},{7,9},{8,6},{9,7},{10,... | collective-permute-start | bytes 208904 | tf_op jit(solution)/shard_map/ppermute | solution.py:436
  8.5 0.0 collective-permute-done.ra
  8.5 0.1 far.1
  8.6 0.1 collective-permute-start.3
  8.7 1.8 %collective-permute-done.1.rb = f32[136,128]{1,0:T(8,128)S(1)} collective-permute-done((f32[136,128]{1,0:T(8,128)S(1)}, f32[136,128]{1,0:T(8,128)S(1)}, u32[]{:S(2)}, u32[]{:S(2)}) %collective-permute-start.1) | collective-permute-done | bytes 69664 | tf_op jit(solution)/shard_map/ppermute | solution.py:436
  10.5 0.1 near.1
  10.6 1.6 %collective-permute-start.2 = (f32[66,8,128]{2,1,0:T(8,128)S(1)}, f32[66,8,128]{2,1,0:T(8,128)S(1)}, u32[]{:S(2)}, u32[]{:S(2)}) collective-permute-start(f32[66,8,128]{2,1,0:T(8,128)S(1)} %near.1), channel_id=1, source_target_pairs={{0,1},{1,0},{2,3},{3,2},{4,5},{5,4},{6,7},{7,6},{8,9},{9,8},{10,11... | collective-permute-start | bytes 811016 | tf_op jit(solution)/shard_map/ppermute | solution.py:436
  12.2 0.5 %collective-permute-start.4 = (f32[8,128]{1,0:T(8,128)S(1)}, f32[8,128]{1,0:T(8,128)S(1)}, u32[]{:S(2)}, u32[]{:S(2)}) collective-permute-start(f32[8,128]{1,0:T(8,128)S(1)} %get-tuple-element.16.own_cb), channel_id=1, source_target_pairs={{0,1},{1,0},{2,4},{3,27},{4,2},{5,29},{6,8},{7,23},{8,6},{9,25},{1... | collective-permute-start | bytes 12296 | tf_op jit(solution)/shard_map/ppermute | solution.py:436
  12.7 5.6 %inner.1 = (f32[4,32,40,128]{3,2,1,0:T(8,128)S(1)}, f32[4,32,40,128]{3,2,1,0:T(8,128)S(1)}, f32[4,32,36,128]{3,2,1,0:T(8,128)S(1)}, f32[4,32,36,128]{3,2,1,0:T(8...) custom-call(f32[4,32,32,128]{3,2,1,0:T(8,128)S(1)} %copy-done, f32[40,128]{1,0:T(8,128)S(1)} %pad.4.depth, ...), custom_call_target="tpu_custom_call" | custom-call | tf_op jit(solution)/shard_map/inner/pallas_call | solution.py:489
  18.3 0.0 collective-permute-done.2.p.p1
  18.4 2.2 %south.1 = f32[4,32,8,128]{3,2,1,0:T(8,128)S(1)} custom-call(f32[66,8,128]{2,1,0:T(8,128)S(1)} %collective-permute-done.2.p.p1, f32[40,128]{1,0:T(8,128)S(1)} %pad.4.depth, f32[40,128]{1,0:T(8,128)S(1)} %get-tuple-element.17.side_depth, f32[4,32,40,128]{3,2,1,0:T(8,128)S(1)} %get-tuple-element.18.main0, f32[4,32,40,128]{3,2,1,0:T(8,128)S(1)} %get-tuple-element.19.side0, ...), custom_call_target="tpu_custom_call" | custom-call | tf_op jit(solution)/shard_map/south/pallas_call | solution.py:500
  20.6 0.0 collective-permute-done.4.cb
  20.6 0.0 collective-permute-done.3.p2
  20.6 2.6 %north.1 = f32[4,32,32,128]{3,2,1,0:T(8,128)} custom-call(f32[66,8,128]{2,1,0:T(8,128)S(1)} %collective-permute-done.2.p.p1, f32[67,8,128]{2,1,0:T(8,128)S(1)} %collective-permute-done.3.p2, f32[8,128]{1,0:T(8,128)S(1)} %collective-permute-done.4.cb, f32[8,128]{1,0:T(8,128)S(1)} %get-tuple-element.16.own_cb, f32[40,128]{1,0:T(8,128)S(1)} %pad.4.depth, ...), custom_call_target="tpu_custom_call" | custom-call | tf_op jit(solution)/shard_map/north/pallas_call | solution.py:509
  (4 shorter events, 0.0 us)
Async XLA Ops:
  0.0 0.7 %copy-start.1 = (s32[32,128]{1,0:T(8,128)S(1)}, s32[32,128]{1,0:T(8,128)}, u32[]{:S(2)}) copy-start(s32[32,128]{1,0:T(8,128)} %param.5) | copy-start | bytes 49156
  0.0 0.7 %copy-start.2 = (s32[32,128]{1,0:T(8,128)S(1)}, s32[32,128]{1,0:T(8,128)}, u32[]{:S(2)}) copy-start(s32[32,128]{1,0:T(8,128)} %param.4) | copy-start | bytes 49156
  0.0 1.6 %copy-start = (f32[4,32,32,128]{3,2,1,0:T(8,128)S(1)}, f32[4,32,32,128]{3,2,1,0:T(8,128)}, u32[]{:S(2)}) copy-start(f32[4,32,32,128]{3,2,1,0:T(8,128)} %state.7) | copy-start | bytes 6291460
  2.3 6.2 %collective-permute-start = (f32[136,128]{1,0:T(8,128)S(1)}, f32[136,128]{1,0:T(8,128)S(1)}, u32[]{:S(2)}, u32[]{:S(2)}) collective-permute-start(f32[136,128]{1,0:T(8,128)S(1)} %get-tuple-element.14), channel_id=1, source_target_pairs={{0,2},{1,3},{2,0},{3,1},{4,6},{5,7},{6,4},{7,5},{8,10},{9,11},{10,... | collective-permute-start | bytes 208904 | tf_op jit(solution)/shard_map/ppermute | solution.py:436
  2.8 7.7 %collective-permute-start.1 = (f32[136,128]{1,0:T(8,128)S(1)}, f32[136,128]{1,0:T(8,128)S(1)}, u32[]{:S(2)}, u32[]{:S(2)}) collective-permute-start(f32[136,128]{1,0:T(8,128)S(1)} %get-tuple-element.15), channel_id=1, source_target_pairs={{0,30},{1,31},{2,4},{3,5},{4,2},{5,3},{6,8},{7,9},{8,6},{9,7},{10,... | collective-permute-start | bytes 208904 | tf_op jit(solution)/shard_map/ppermute | solution.py:436
  8.6 11.9 %collective-permute-start.3 = (f32[67,8,128]{2,1,0:T(8,128)S(1)}, f32[67,8,128]{2,1,0:T(8,128)S(1)}, u32[]{:S(2)}, u32[]{:S(2)}) collective-permute-start(f32[67,8,128]{2,1,0:T(8,128)S(1)} %far.1), channel_id=1, source_target_pairs={{0,2},{1,31},{2,0},{3,29},{4,6},{5,27},{6,4},{7,25},{8,10},{9,23},... | collective-permute-start | bytes 823304 | tf_op jit(solution)/shard_map/ppermute | solution.py:436
  10.6 7.7 %collective-permute-start.2 = (f32[66,8,128]{2,1,0:T(8,128)S(1)}, f32[66,8,128]{2,1,0:T(8,128)S(1)}, u32[]{:S(2)}, u32[]{:S(2)}) collective-permute-start(f32[66,8,128]{2,1,0:T(8,128)S(1)} %near.1), channel_id=1, source_target_pairs={{0,1},{1,0},{2,3},{3,2},{4,5},{5,4},{6,7},{7,6},{8,9},{9,8},{10,11... | collective-permute-start | bytes 811016 | tf_op jit(solution)/shard_map/ppermute | solution.py:436
  12.2 8.4 %collective-permute-start.4 = (f32[8,128]{1,0:T(8,128)S(1)}, f32[8,128]{1,0:T(8,128)S(1)}, u32[]{:S(2)}, u32[]{:S(2)}) collective-permute-start(f32[8,128]{1,0:T(8,128)S(1)} %get-tuple-element.16.own_cb), channel_id=1, source_target_pairs={{0,1},{1,0},{2,4},{3,27},{4,2},{5,29},{6,8},{7,23},{8,6},{9,25},{1... | collective-permute-start | bytes 12296 | tf_op jit(solution)/shard_map/ppermute | solution.py:436

commit v8 on v7

--- a/solution.py
+++ b/solution.py
@@ -44,6 +44,14 @@
     for n, row in enumerate(factors(table.shape[1])):
         for k, value in enumerate(row):
             table[n, k] = float(value)
+
+
+def over(start, stop, body, carry, unroll):
+    if unroll < stop - start:
+        return lax.fori_loop(start, stop, body, carry, unroll=unroll)
+    for k in range(start, stop):
+        carry = body(k, carry)
+    return carry
 
 
 def lanes():
@@ -173,12 +181,15 @@
     lane = lanes()
     zero = jnp.zeros((8, 128), F32)
     jobs = [job if len(job) == 9 else (*job, 1, job[2]) for job in jobs]
+    fixed = factors(levels)
     turns = [cor * (UNIT * time_step * scale / DRIFT) for _, _, _, _, cor, *_ in jobs]
     uppers = [depth - 1.0 for _, _, _, depth, *_ in jobs]
 
     def forward(k, carry):
-        inner, lowest = table[0, k], table[1, k]
-        level = k.astype(F32)
+        if isinstance(k, int):
+            inner, lowest, level = float(fixed[0, k]), float(fixed[1, k]), float(k)
+        else:
+            inner, lowest, level = table[0, k], table[1, k], k.astype(F32)
         out = []
         for n, (own, other, o, depth, _, _, _, apart, at) in enumerate(jobs):
             halves = carry[6 * n:6 * n + 4]
@@ -221,11 +232,11 @@
             out += near[4:6]
         return tuple(out)
 
-    lax.fori_loop(0, levels, forward, (zero,) * (6 * len(jobs)), unroll=unroll)
+    over(0, levels, forward, (zero,) * (6 * len(jobs)), unroll)
 
     def backward(step, carry):
         k = levels - 1 - step
-        ratio = table[0, k]
+        ratio = float(fixed[0, k]) if isinstance(k, int) else table[0, k]
         out = []
         for n, (_, _, _, _, _, dst, d, _, _) in enumerate(jobs):
             for f in range(4):
@@ -237,7 +248,7 @@
     carry = (zero,) * (4 * len(jobs))
     size = levels // parts
     for n in range(parts):
-        carry = lax.fori_loop(n * size, (n + 1) * size, backward, carry, unroll=min(unroll_back, size))
+        carry = over(n * size, (n + 1) * size, backward, carry, min(unroll_back, size))
         if ready is not None:
             ready(n, levels - (n + 1) * size, size)
 
@@ -301,7 +312,6 @@
     first_row = lax.axis_index("lat") * rows
     total = rows * lax.axis_size("lat")
     has_south = lax.axis_index("lat") > 0
-    fill_table(table)
     corner = jnp.where(has_south, p[2 * levels + 1], 0.0)
     rim_depth = jnp.where(has_south, p[2 * levels], 0.0)
     depths = jnp.where(sublanes() < 2, pltpu.roll(rim_depth, 6, 0), depth[2:10, :])
@@ -345,7 +355,6 @@
     first_row = band * rows
     total = rows * lax.axis_size("lat")
     is_top = band == lax.axis_size("lat") - 1
-    fill_table(table)
     mirror = 127 - lanes()
     flip = sublanes() ^ 3
 

time: 23.4 us -> 23.4 us (level)
  no operation moved by 1% of the time
where the time goes in v8:
time: 23.4 us; the launch traced here: 23.2 us
  Pallas kernels  11.4 us (49%)
  starting transfers between devices  8.35 us (36%)
  waiting for transfers between devices  1.8 us (8%)
  local copies, waits for them, and re-layouts  1.61 us (7%)
    ppermute x5, starting transfers between devices, swap(): return lax.ppermute(x, ('lon', 'lat'), pairs)  8.35 us
    pallas_call x1, Pallas kernels, per_device(): call(inner_kernel, 10, out_shape=(block(rows + 8), block(rows + 8), block...  5.68 us
    pallas_call x1, Pallas kernels, per_device(): call(north_kernel, 12, out_shape=shape(*state.shape), in_specs=[VM] * 12,...  2.57 us
    pallas_call x1, Pallas kernels, per_device(): call(south_kernel, 10, out_shape=block(8), in_specs=[VM] * 7, out_specs=V...  2.21 us
    ppermute x5, waiting for transfers between devices, swap(): return lax.ppermute(x, ('lon', 'lat'), pairs)  1.8 us
    unnamed x6, local copies, waits for them, and re-layouts  1.6 us
    pallas_call x1, Pallas kernels, per_device(): call(columns_kernel, 4, out_shape=(strip, strip, shape(8, 128)), in_specs...  0.68 us
  transfers between devices with their start and end apart: 5, of which 1 were waited for; matrix products, arithmetic and copies ran while one was open for 0% of the time, Pallas kernels for 35%

profile of v8, /device:TPU:0, one launch (start us, length us, event | category | flops | bytes accessed | tf_op | source)
XLA Modules:
  0.0 23.2 jit_solution(216329720310351165)
XLA Ops:
  0.0 0.0 copy-start.1
  0.0 0.0 copy-start.2
  0.0 0.0 copy-start
  0.0 0.7 %copy-done.1 = s32[32,128]{1,0:T(8,128)S(1)} copy-done((s32[32,128]{1,0:T(8,128)S(1)}, s32[32,128]{1,0:T(8,128)}, u32[]{:S(2)}) %copy-start.1) | copy-done | bytes 16408
  0.7 0.0 copy-done.2
  0.7 0.9 %copy-done = f32[4,32,32,128]{3,2,1,0:T(8,128)S(1)} copy-done((f32[4,32,32,128]{3,2,1,0:T(8,128)S(1)}, f32[4,32,32,128]{3,2,1,0:T(8,128)}, u32[]{:S(2)}) %copy-start) | copy-done | bytes 2097176
  1.6 0.7 %columns.1 = (f32[136,128]{1,0:T(8,128)S(1)}, f32[136,128]{1,0:T(8,128)S(1)}, f32[8,128]{1,0:T(8,128)S(1)}) custom-call(f32[4,32,32,128]{3,2,1,0:T(8,128)S(1)} %copy-done, f32[40,128]{1,0:T(8,128)S(1)} %pad.4.depth), custom_call_target="tpu_custom_call" | custom-call | tf_op jit(solution)/shard_map/columns/pallas_call | solution.py:476
  2.3 0.5 %collective-permute-start = (f32[136,128]{1,0:T(8,128)S(1)}, f32[136,128]{1,0:T(8,128)S(1)}, u32[]{:S(2)}, u32[]{:S(2)}) collective-permute-start(f32[136,128]{1,0:T(8,128)S(1)} %get-tuple-element.14), channel_id=1, source_target_pairs={{0,2},{1,3},{2,0},{3,1},{4,6},{5,7},{6,4},{7,5},{8,10},{9,11},{10,... | collective-permute-start | bytes 208904 | tf_op jit(solution)/shard_map/ppermute | solution.py:445
  2.8 5.7 %collective-permute-start.1 = (f32[136,128]{1,0:T(8,128)S(1)}, f32[136,128]{1,0:T(8,128)S(1)}, u32[]{:S(2)}, u32[]{:S(2)}) collective-permute-start(f32[136,128]{1,0:T(8,128)S(1)} %get-tuple-element.15), channel_id=1, source_target_pairs={{0,30},{1,31},{2,4},{3,5},{4,2},{5,3},{6,8},{7,9},{8,6},{9,7},{10,... | collective-permute-start | bytes 208904 | tf_op jit(solution)/shard_map/ppermute | solution.py:445
  8.5 0.0 collective-permute-done.ra
  8.5 0.1 far.1
  8.6 0.1 collective-permute-start.3
  8.7 1.8 %collective-permute-done.1.rb = f32[136,128]{1,0:T(8,128)S(1)} collective-permute-done((f32[136,128]{1,0:T(8,128)S(1)}, f32[136,128]{1,0:T(8,128)S(1)}, u32[]{:S(2)}, u32[]{:S(2)}) %collective-permute-start.1) | collective-permute-done | bytes 69664 | tf_op jit(solution)/shard_map/ppermute | solution.py:445
  10.5 0.1 near.1
  10.6 1.6 %collective-permute-start.2 = (f32[66,8,128]{2,1,0:T(8,128)S(1)}, f32[66,8,128]{2,1,0:T(8,128)S(1)}, u32[]{:S(2)}, u32[]{:S(2)}) collective-permute-start(f32[66,8,128]{2,1,0:T(8,128)S(1)} %near.1), channel_id=1, source_target_pairs={{0,1},{1,0},{2,3},{3,2},{4,5},{5,4},{6,7},{7,6},{8,9},{9,8},{10,11... | collective-permute-start | bytes 811016 | tf_op jit(solution)/shard_map/ppermute | solution.py:445
  12.2 0.5 %collective-permute-start.4 = (f32[8,128]{1,0:T(8,128)S(1)}, f32[8,128]{1,0:T(8,128)S(1)}, u32[]{:S(2)}, u32[]{:S(2)}) collective-permute-start(f32[8,128]{1,0:T(8,128)S(1)} %get-tuple-element.16.own_cb), channel_id=1, source_target_pairs={{0,1},{1,0},{2,4},{3,27},{4,2},{5,29},{6,8},{7,23},{8,6},{9,25},{1... | collective-permute-start | bytes 12296 | tf_op jit(solution)/shard_map/ppermute | solution.py:445
  12.7 5.7 %inner.1 = (f32[4,32,40,128]{3,2,1,0:T(8,128)S(1)}, f32[4,32,40,128]{3,2,1,0:T(8,128)S(1)}, f32[4,32,36,128]{3,2,1,0:T(8,128)S(1)}, f32[4,32,36,128]{3,2,1,0:T(8...) custom-call(f32[4,32,32,128]{3,2,1,0:T(8,128)S(1)} %copy-done, f32[40,128]{1,0:T(8,128)S(1)} %pad.4.depth, ...), custom_call_target="tpu_custom_call" | custom-call | tf_op jit(solution)/shard_map/inner/pallas_call | solution.py:498
  18.4 0.0 collective-permute-done.2.p.p1
  18.4 2.2 %south.1 = f32[4,32,8,128]{3,2,1,0:T(8,128)S(1)} custom-call(f32[66,8,128]{2,1,0:T(8,128)S(1)} %collective-permute-done.2.p.p1, f32[40,128]{1,0:T(8,128)S(1)} %pad.4.depth, f32[40,128]{1,0:T(8,128)S(1)} %get-tuple-element.17.side_depth, f32[4,32,40,128]{3,2,1,0:T(8,128)S(1)} %get-tuple-element.18.main0, f32[4,32,40,128]{3,2,1,0:T(8,128)S(1)} %get-tuple-element.19.side0, ...), custom_call_target="tpu_custom_call" | custom-call | tf_op jit(solution)/shard_map/south/pallas_call | solution.py:509
  20.6 0.0 collective-permute-done.4.cb
  20.6 0.0 collective-permute-done.3.p2
  20.6 2.6 %north.1 = f32[4,32,32,128]{3,2,1,0:T(8,128)} custom-call(f32[66,8,128]{2,1,0:T(8,128)S(1)} %collective-permute-done.2.p.p1, f32[67,8,128]{2,1,0:T(8,128)S(1)} %collective-permute-done.3.p2, f32[8,128]{1,0:T(8,128)S(1)} %collective-permute-done.4.cb, f32[8,128]{1,0:T(8,128)S(1)} %get-tuple-element.16.own_cb, f32[40,128]{1,0:T(8,128)S(1)} %pad.4.depth, ...), custom_call_target="tpu_custom_call" | custom-call | tf_op jit(solution)/shard_map/north/pallas_call | solution.py:518
  (4 shorter events, 0.0 us)
Async XLA Ops:
  0.0 0.7 %copy-start.1 = (s32[32,128]{1,0:T(8,128)S(1)}, s32[32,128]{1,0:T(8,128)}, u32[]{:S(2)}) copy-start(s32[32,128]{1,0:T(8,128)} %param.5) | copy-start | bytes 49156
  0.0 0.7 %copy-start.2 = (s32[32,128]{1,0:T(8,128)S(1)}, s32[32,128]{1,0:T(8,128)}, u32[]{:S(2)}) copy-start(s32[32,128]{1,0:T(8,128)} %param.4) | copy-start | bytes 49156
  0.0 1.6 %copy-start = (f32[4,32,32,128]{3,2,1,0:T(8,128)S(1)}, f32[4,32,32,128]{3,2,1,0:T(8,128)}, u32[]{:S(2)}) copy-start(f32[4,32,32,128]{3,2,1,0:T(8,128)} %state.7) | copy-start | bytes 6291460
  2.3 6.2 %collective-permute-start = (f32[136,128]{1,0:T(8,128)S(1)}, f32[136,128]{1,0:T(8,128)S(1)}, u32[]{:S(2)}, u32[]{:S(2)}) collective-permute-start(f32[136,128]{1,0:T(8,128)S(1)} %get-tuple-element.14), channel_id=1, source_target_pairs={{0,2},{1,3},{2,0},{3,1},{4,6},{5,7},{6,4},{7,5},{8,10},{9,11},{10,... | collective-permute-start | bytes 208904 | tf_op jit(solution)/shard_map/ppermute | solution.py:445
  2.8 7.7 %collective-permute-start.1 = (f32[136,128]{1,0:T(8,128)S(1)}, f32[136,128]{1,0:T(8,128)S(1)}, u32[]{:S(2)}, u32[]{:S(2)}) collective-permute-start(f32[136,128]{1,0:T(8,128)S(1)} %get-tuple-element.15), channel_id=1, source_target_pairs={{0,30},{1,31},{2,4},{3,5},{4,2},{5,3},{6,8},{7,9},{8,6},{9,7},{10,... | collective-permute-start | bytes 208904 | tf_op jit(solution)/shard_map/ppermute | solution.py:445
  8.6 12.0 %collective-permute-start.3 = (f32[67,8,128]{2,1,0:T(8,128)S(1)}, f32[67,8,128]{2,1,0:T(8,128)S(1)}, u32[]{:S(2)}, u32[]{:S(2)}) collective-permute-start(f32[67,8,128]{2,1,0:T(8,128)S(1)} %far.1), channel_id=1, source_target_pairs={{0,2},{1,31},{2,0},{3,29},{4,6},{5,27},{6,4},{7,25},{8,10},{9,23},... | collective-permute-start | bytes 823304 | tf_op jit(solution)/shard_map/ppermute | solution.py:445
  10.6 7.8 %collective-permute-start.2 = (f32[66,8,128]{2,1,0:T(8,128)S(1)}, f32[66,8,128]{2,1,0:T(8,128)S(1)}, u32[]{:S(2)}, u32[]{:S(2)}) collective-permute-start(f32[66,8,128]{2,1,0:T(8,128)S(1)} %near.1), channel_id=1, source_target_pairs={{0,1},{1,0},{2,3},{3,2},{4,5},{5,4},{6,7},{7,6},{8,9},{9,8},{10,11... | collective-permute-start | bytes 811016 | tf_op jit(solution)/shard_map/ppermute | solution.py:445
  12.2 8.4 %collective-permute-start.4 = (f32[8,128]{1,0:T(8,128)S(1)}, f32[8,128]{1,0:T(8,128)S(1)}, u32[]{:S(2)}, u32[]{:S(2)}) collective-permute-start(f32[8,128]{1,0:T(8,128)S(1)} %get-tuple-element.16.own_cb), channel_id=1, source_target_pairs={{0,1},{1,0},{2,4},{3,27},{4,2},{5,29},{6,8},{7,23},{8,6},{9,25},{1... | collective-permute-start | bytes 12296 | tf_op jit(solution)/shard_map/ppermute | solution.py:445
